TPU v7x, 32 devices: a whole 2x2x4 slice. The times are simulated.
32 devices in a mesh: groups: 2 (over x), seq: 16 (over z, y, core).
Axes of the slice: x: 2, y: 2, z: 4, core: 2. Of those that a mesh axis runs over, the one named last changes fastest.
Arguments:
- tokens: bfloat16 [4096, 768], P(('groups', 'seq')), parts along dimension 0, may hold values from -6 to 6
- gain: float32 [768], replicated, may hold values from 0.1 to 1.9
- w_qkv: bfloat16 [768, 2304], replicated, may hold values from -3 to 3
- w_out: bfloat16 [768, 768], replicated, may hold values from -0.21875 to 0.21875
- nbr_list: int32 [64, 8], P('groups'), parts along dimension 0, may hold values from 0 to 31, as said below
- nbr_count: int32 [64], P('groups'), parts along dimension 0, may hold values from 1 to 8, as said below
- cotangent: bfloat16 [4096, 768], P(('groups', 'seq')), parts along dimension 0, may hold values from -6 to 6
Outputs:
- layer_out: bfloat16 [4096, 768], P(('groups', 'seq')), parts along dimension 0
- token_grad: bfloat16 [4096, 768], P(('groups', 'seq')), parts along dimension 0
There are 2 independent parts, one for each index of `groups`. A program takes and returns all parts, laid end to end along the dimension named above; an argument that names none is the same for every part. Nothing has to cross between parts.
Inputs may be any that keep to these rules, and one draw needn't show every extreme that they name: `nbr_list`: block c belongs to device c // 2. Entry 0 of row b is b; entries 1 to nbr_count[b] - 1 are distinct blocks, none equal to b, of devices at offsets -8 to 7 from the owner of b; the remaining entries repeat b. Over the 2 rows of one device, at most one block of each other device is named. `nbr_count`: some block has 8.
All inputs are finite; a program needn't handle non-finite values.
Results may differ from a plain program's by a relative error of at most 0.0049.
Values may be sent and summed in bfloat16 or wider, within the bound.
No kernel may reach another device: no remote copies, remote signals or barrier semaphores. Data moves between devices by JAX's collectives and lax.ppermute only.
A program may use at most 128 MiB of HBM per device.

v0:
```python
import jax
import jax.numpy as jnp
from jax import lax
from jax.sharding import PartitionSpec as P

HD = 64
BLK = 64
MAXNB = 8
HALF = 8


def passed_along(block, axis, distance):
    devices = range(lax.axis_size(axis))
    route = [(i - distance, i) for i in devices if i - distance in devices]
    return lax.ppermute(block, axis, route)


def normalize(tokens, gain):
    inputs = tokens.astype(jnp.float32)
    center = jnp.mean(inputs, axis=-1, keepdims=True)
    spread = jnp.mean((inputs - center) ** 2, axis=-1, keepdims=True)
    inv_std = lax.rsqrt(spread + 1e-05)
    unit = (inputs - center) * inv_std
    return (inputs, unit, inv_std, (unit * gain).astype(jnp.bfloat16))


def backnorm(norm_grad, unit, inv_std, gain, cotangent):
    scaled = norm_grad * gain
    centered = (
        scaled
        - jnp.mean(scaled, axis=-1, keepdims=True)
        - unit * jnp.mean(scaled * unit, axis=-1, keepdims=True)
    )
    return (cotangent.astype(jnp.float32) + inv_std * centered).astype(jnp.bfloat16)


def attend(queries, grads, keys, counts):
    block_count, block_len, model_width = queries.shape
    slot_count = keys.shape[1]
    head_count = model_width // HD
    query_heads = queries.reshape(block_count, block_len, head_count, HD)
    key_heads = keys[..., :model_width].reshape(block_count, slot_count * block_len, head_count, HD)
    value_heads = keys[..., model_width:].reshape(
        block_count, slot_count * block_len, head_count, HD
    )
    live_mask = jnp.arange(slot_count)[None, :] < counts[:, None]
    live_mask = jnp.repeat(live_mask, block_len, axis=1)[:, None, None, :]
    scores = (
        jnp.einsum("qthd,qkhd->qhtk", query_heads, key_heads, preferred_element_type=jnp.float32)
        * 0.125
    )
    scores = jnp.where(live_mask, scores, -1e30)
    row_max = jnp.max(scores, axis=-1, keepdims=True)
    weights = jnp.exp(scores - row_max)
    attn_prob = weights / jnp.sum(weights, axis=-1, keepdims=True)
    prob_low = attn_prob.astype(jnp.bfloat16)
    attended = jnp.einsum(
        "qhtk,qkhd->qthd", prob_low, value_heads, preferred_element_type=jnp.float32
    )
    attended = attended.astype(jnp.bfloat16).reshape(block_count, block_len, model_width)
    grad_heads = grads.reshape(block_count, block_len, head_count, HD)
    prob_grad = jnp.einsum(
        "qthd,qkhd->qhtk", grad_heads, value_heads, preferred_element_type=jnp.float32
    )
    row_dot = jnp.sum(attn_prob * prob_grad, axis=-1, keepdims=True)
    score_grad = (attn_prob * (prob_grad - row_dot) * 0.125).astype(jnp.bfloat16)
    query_grad = jnp.einsum(
        "qhtk,qkhd->qthd", score_grad, key_heads, preferred_element_type=jnp.float32
    )
    query_grad = query_grad.astype(jnp.bfloat16).reshape(block_count, block_len, model_width)
    key_grad = jnp.einsum(
        "qhtk,qthd->qkhd", score_grad, query_heads, preferred_element_type=jnp.float32
    )
    value_grad = jnp.einsum(
        "qhtk,qthd->qkhd", prob_low, grad_heads, preferred_element_type=jnp.float32
    )
    key_grad = key_grad.reshape(block_count, slot_count, block_len, model_width)
    value_grad = value_grad.reshape(block_count, slot_count, block_len, model_width)
    return (attended, query_grad, jnp.concatenate([key_grad, value_grad], axis=-1))


def per_device(tokens, gain, w_qkv, w_out, nbr_list, nbr_count, cotangent):
    position = lax.axis_index("seq")
    token_count, model_width = tokens.shape
    blocks = token_count // BLK
    inputs, unit, inv_std, normed = normalize(tokens, gain)
    projected = jnp.dot(normed, w_qkv, preferred_element_type=jnp.float32)
    queries = projected[:, :model_width].astype(jnp.bfloat16).reshape(blocks, BLK, model_width)
    own_kv = projected[:, model_width:].astype(jnp.bfloat16).reshape(blocks, BLK, 2 * model_width)
    out_grad = lax.dot_general(
        cotangent, w_out, (((1,), (1,)), ((), ())), preferred_element_type=jnp.float32
    ).astype(jnp.bfloat16)
    my_lists = lax.dynamic_slice_in_dim(nbr_list, position * blocks, blocks, 0)
    my_counts = lax.dynamic_slice_in_dim(nbr_count, position * blocks, blocks, 0)
    live_mask = jnp.arange(MAXNB)[None, :] < my_counts[:, None]
    offsets = my_lists // blocks - position
    peer_slot = jnp.where(offsets < 0, offsets + HALF, offsets + HALF - 1)
    peer_offsets = [offset for offset in range(-HALF, HALF) if offset != 0]
    arrived = [passed_along(own_kv, "seq", -offset) for offset in peer_offsets]
    window = jnp.concatenate(arrived + [own_kv], axis=0)
    slots = jnp.where(offsets == 0, 2 * HALF - 1, peer_slot) * blocks + my_lists % blocks
    keys = jnp.take(window, slots, axis=0)
    attended, query_grad, kv_term = attend(
        queries, out_grad.reshape(blocks, BLK, model_width), keys, my_counts
    )
    layer_out = (
        inputs
        + jnp.dot(
            attended.reshape(token_count, model_width), w_out, preferred_element_type=jnp.float32
        )
    ).astype(jnp.bfloat16)
    slot_count = window.shape[0]
    segment_ids = jnp.where(live_mask, slots, slot_count).reshape(blocks * MAXNB)
    partial_value = jax.ops.segment_sum(
        kv_term.reshape(blocks * MAXNB, BLK, 2 * model_width), segment_ids, num_segments=slot_count
    )
    partial_value = partial_value.astype(jnp.bfloat16)
    total = partial_value[slot_count - blocks :].astype(jnp.float32)
    for index, offset in enumerate(peer_offsets):
        returned = passed_along(partial_value[index * blocks : (index + 1) * blocks], "seq", offset)
        total = total + returned.astype(jnp.float32)
    kv_total = total.astype(jnp.bfloat16).reshape(token_count, 2 * model_width)
    qkv_grad = jnp.concatenate([query_grad.reshape(token_count, model_width), kv_total], axis=1)
    norm_grad = lax.dot_general(
        qkv_grad, w_qkv, (((1,), (1,)), ((), ())), preferred_element_type=jnp.float32
    )
    token_grad = backnorm(norm_grad, unit, inv_std, gain, cotangent)
    return (layer_out, token_grad)


def solution(mesh):
    in_specs = (
        P(("groups", "seq"), None),
        P(),
        P(),
        P(),
        P("groups", None),
        P("groups"),
        P(("groups", "seq"), None),
    )
    out_specs = (P(("groups", "seq"), None), P(("groups", "seq"), None))
    return jax.shard_map(
        per_device, mesh=mesh, in_specs=in_specs, out_specs=out_specs, check_vma=False
    )
```

profile of v0, /device:TPU:1, one launch (start us, length us, event | category | flops | bytes accessed | tf_op | source)
XLA Modules:
  0.0 431.4 jit_solution(17643566821822088842)
XLA Ops:
  10.1 8.9 %collective-permute-start.1 = (bf16[2,64,1536]{2,1,0:T(8,128)(2,1)}, bf16[2,64,1536]{2,1,0:T(8,128)(2,1)}, u32[]{:S(2)}, u32[]{:S(2)}) collective-permute-start(bf16[2,64,1536]{2,1,0:T(8,128)(2,1)} %bitcast), channel_id=1, source_target_pairs={{0,7},{1,8},{2,9},{3,10},{4,11},{5,12},{6,13},{7,14},{8,15},{16,23... | collective-permute-start | bytes 1179656 | tf_op jit(solution)/shard_map/ppermute | solution.py:15
  38.4 26.9 %collective-permute-start.2 = (bf16[2,64,1536]{2,1,0:T(8,128)(2,1)}, bf16[2,64,1536]{2,1,0:T(8,128)(2,1)S(1)}, u32[]{:S(2)}, u32[]{:S(2)}) collective-permute-start(bf16[2,64,1536]{2,1,0:T(8,128)(2,1)} %bitcast), channel_id=1, source_target_pairs={{0,6},{1,7},{2,8},{3,9},{4,10},{5,11},{6,12},{7,13},{8,14},{9,15},... | collective-permute-start | bytes 1179656 | tf_op jit(solution)/shard_map/ppermute | solution.py:15
  75.8 6.3 %collective-permute-done.3 = bf16[2,64,1536]{2,1,0:T(8,128)(2,1)S(1)} collective-permute-done((bf16[2,64,1536]{2,1,0:T(8,128)(2,1)}, bf16[2,64,1536]{2,1,0:T(8,128)(2,1)S(1)}, u32[]{:S(2)}, u32[]{:S(2)}) %collective-permute-start.3) | collective-permute-done | bytes 393248 | tf_op jit(solution)/shard_map/ppermute | solution.py:15
  84.6 6.0 %collective-permute-done.4 = bf16[2,64,1536]{2,1,0:T(8,128)(2,1)S(1)} collective-permute-done((bf16[2,64,1536]{2,1,0:T(8,128)(2,1)}, bf16[2,64,1536]{2,1,0:T(8,128)(2,1)S(1)}, u32[]{:S(2)}, u32[]{:S(2)}) %collective-permute-start.4) | collective-permute-done | bytes 393248 | tf_op jit(solution)/shard_map/ppermute | solution.py:15
  108.3 8.1 %collective-permute-done.8 = bf16[2,64,1536]{2,1,0:T(8,128)(2,1)S(1)} collective-permute-done((bf16[2,64,1536]{2,1,0:T(8,128)(2,1)}, bf16[2,64,1536]{2,1,0:T(8,128)(2,1)S(1)}, u32[]{:S(2)}, u32[]{:S(2)}) %collective-permute-start.8) | collective-permute-done | bytes 393248 | tf_op jit(solution)/shard_map/ppermute | solution.py:15
  124.9 9.4 %collective-permute-done.10 = bf16[2,64,1536]{2,1,0:T(8,128)(2,1)S(1)} collective-permute-done((bf16[2,64,1536]{2,1,0:T(8,128)(2,1)}, bf16[2,64,1536]{2,1,0:T(8,128)(2,1)S(1)}, u32[]{:S(2)}, u32[]{:S(2)}) %collective-permute-start.10) | collective-permute-done | bytes 393248 | tf_op jit(solution)/shard_map/ppermute | solution.py:15
  135.1 7.1 %collective-permute-done.11 = bf16[2,64,1536]{2,1,0:T(8,128)(2,1)S(1)} collective-permute-done((bf16[2,64,1536]{2,1,0:T(8,128)(2,1)}, bf16[2,64,1536]{2,1,0:T(8,128)(2,1)S(1)}, u32[]{:S(2)}, u32[]{:S(2)}) %collective-permute-start.11) | collective-permute-done | bytes 393248 | tf_op jit(solution)/shard_map/ppermute | solution.py:15
  164.1 5.4 %reshape.56 = bf16[2,512,12,64]{1,3,2,0:T(8,128)(2,1)} reshape(bf16[2,8,64,768]{2,1,3,0:T(8,128)(2,1)} %copy.38) | data formatting | bytes 3145728 | tf_op jit(solution)/shard_map/reshape | solution.py:42
  173.9 5.4 %reshape.55 = bf16[2,512,12,64]{1,3,2,0:T(8,128)(2,1)} reshape(bf16[2,8,64,768]{2,1,3,0:T(8,128)(2,1)} %copy.35) | data formatting | bytes 3145728 | tf_op jit(solution)/shard_map/reshape | solution.py:43
  192.3 15.3 %fusion.12 = f32[2,512,12,64]{1,3,2,0:T(8,128)} fusion(bf16[2,64,12,64]{1,3,2,0:T(8,128)(2,1)} %copy.45, f32[2,12,64,512]{3,2,1,0:T(8,128)} %fusion.66, f32[2,12,64,512]{3,2,1,0:T(8,128)} %get-tuple-element.24, f32[2,12,64]{2,1,0:T(8,128)} %get-tuple-element.23), kind=kOutput, calls=%fused_computation.15 | convolution fusion | flops 106170368 | bytes 9639936 | tf_op jit(solution)/shard_map/qhtk,qthd->qkhd/dot_general | solution.py:71
  207.5 6.1 %copy.48 = f32[2,512,12,64]{1,0,3,2:T(2,128)} copy(f32[2,512,12,64]{1,3,2,0:T(8,128)} %convolution_bitcast_fusion) | data formatting | bytes 6291456 | tf_op jit(solution)/shard_map/qhtk,qthd->qkhd/transpose | solution.py:74
  217.8 6.7 %concatenate.15 = f32[16,64,768]{1,0,2:T(8,128)} reshape(f32[2,512,12,64]{1,0,3,2:T(2,128)} %copy.46) | data formatting | bytes 6291456 | tf_op jit(solution)/shard_map/concatenate | solution.py:79
  224.4 6.7 %concatenate.16 = f32[16,64,768]{1,0,2:T(8,128)} reshape(f32[2,512,12,64]{1,0,3,2:T(2,128)} %copy.48) | data formatting | bytes 6291456 | tf_op jit(solution)/shard_map/concatenate | solution.py:79
  231.2 12.4 %pad_maximum_fusion = f32[16,64,1536]{1,0,2:T(8,128)} fusion(f32[16,64,768]{1,0,2:T(8,128)} %concatenate.16, f32[16,64,768]{1,0,2:T(8,128)} %concatenate.15), kind=kLoop, calls=%fused_computation.4 | loop fusion | flops 1572864 | bytes 12582912 | tf_op jit(solution)/shard_map/concatenate | solution.py:79
  243.6 9.8 %copy.49 = f32[16,64,1536]{2,1,0:T(8,128)} copy(f32[16,64,1536]{1,0,2:T(8,128)} %pad_maximum_fusion) | data formatting | bytes 12582912 | tf_op jit(solution)/shard_map/concatenate | solution.py:79
  253.3 6.1 %broadcast_in_dim.59 = f32[32,64,1536]{2,1,0:T(8,128)} broadcast(f32[]{:T(128)} %constant.67.clone.1), dimensions={} | broadcast | bytes 12582916 | tf_op jit(solution)/shard_map/broadcast_in_dim | solution.py:114
  259.5 12.9 %scatter_fusion = f32[32,64,1536]{2,1,0:T(8,128)} fusion(f32[32,64,1536]{2,1,0:T(8,128)} %broadcast_in_dim.59, s32[16]{0:T(128)S(1)} %copy-done.22, f32[16,64,1536]{2,1,0:T(8,128)} %copy.49), kind=kCustom, calls=%fused_computation.1 | custom fusion | flops 1572864 | bytes 18874432 | tf_op jit(solution)/shard_map/scatter-add | solution.py:114
  272.3 8.1 %convert_element_type.103 = bf16[32,64,1536]{2,1,0:T(8,128)(2,1)} convert(f32[32,64,1536]{2,1,0:T(8,128)} %scatter_fusion) | non-fusion elementwise | flops 3145728 | bytes 18874368 | tf_op jit(solution)/shard_map/convert_element_type | solution.py:117
  286.2 9.5 %collective-permute-start.29 = (bf16[2,64,1536]{2,1,0:T(8,128)(2,1)S(1)}, bf16[2,64,1536]{2,1,0:T(8,128)(2,1)S(1)}, u32[]{:S(2)}, u32[]{:S(2)}) collective-permute-start(bf16[2,64,1536]{2,1,0:T(8,128)(2,1)S(1)} %get-tuple-element.7), channel_id=1, source_target_pairs={{0,7},{1,8},{2,9},{3,10},{4,11},{5,12},{6,13},{7,14},{8,15},{16,23... | collective-permute-start | bytes 1179656 | tf_op jit(solution)/shard_map/ppermute | solution.py:15
  297.0 5.3 %collective-permute-start.27 = (bf16[2,64,1536]{2,1,0:T(8,128)(2,1)S(1)}, bf16[2,64,1536]{2,1,0:T(8,128)(2,1)S(1)}, u32[]{:S(2)}, u32[]{:S(2)}) collective-permute-start(bf16[2,64,1536]{2,1,0:T(8,128)(2,1)S(1)} %get-tuple-element.9), channel_id=1, source_target_pairs={{0,5},{1,6},{2,7},{3,8},{4,9},{5,10},{6,11},{7,12},{8,13},{9,14},{... | collective-permute-start | bytes 1179656 | tf_op jit(solution)/shard_map/ppermute | solution.py:15
  335.2 5.9 %collective-permute-done.21 = bf16[2,64,1536]{2,1,0:T(8,128)(2,1)S(1)} collective-permute-done((bf16[2,64,1536]{2,1,0:T(8,128)(2,1)S(1)}, bf16[2,64,1536]{2,1,0:T(8,128)(2,1)S(1)}, u32[]{:S(2)}, u32[]{:S(2)}) %collective-permute-start.21) | collective-permute-done | bytes 393248 | tf_op jit(solution)/shard_map/ppermute | solution.py:15
  343.5 14.4 %fusion.23 = bf16[2,64,12,64]{1,3,2,0:T(8,128)(2,1)} fusion(bf16[2,512,12,64]{1,3,2,0:T(8,128)(2,1)} %reshape.56, f32[2,12,64,512]{3,2,1,0:T(8,128)} %fusion.66, f32[2,12,64,512]{3,2,1,0:T(8,128)} %get-tuple-element.24, f32[2,12,64]{2,1,0:T(8,128)} %get-tuple-element.23), kind=kOutput, calls=%fused_computation.25 | convolution fusion | flops 106268672 | bytes 8067072 | tf_op jit(solution)/shard_map/qhtk,qkhd->qthd/dot_general | solution.py:67
  368.6 19.7 %collective-permute-done.18 = bf16[2,64,1536]{2,1,0:T(8,128)(2,1)} collective-permute-done((bf16[2,64,1536]{2,1,0:T(8,128)(2,1)}, bf16[2,64,1536]{2,1,0:T(8,128)(2,1)}, u32[]{:S(2)}, u32[]{:S(2)}) %collective-permute-start.18) | collective-permute-done | bytes 393248 | tf_op jit(solution)/shard_map/ppermute | solution.py:15
  391.6 33.8 %collective-permute-done.16 = bf16[2,64,1536]{2,1,0:T(8,128)(2,1)} collective-permute-done((bf16[2,64,1536]{2,1,0:T(8,128)(2,1)}, bf16[2,64,1536]{2,1,0:T(8,128)(2,1)}, u32[]{:S(2)}, u32[]{:S(2)}) %collective-permute-start.16) | collective-permute-done | bytes 393248 | tf_op jit(solution)/shard_map/ppermute | solution.py:15
  (162 shorter events, 173.8 us)
Async XLA Ops:
  6.2 140.3 %collective-permute-start.14 = (bf16[2,64,1536]{2,1,0:T(8,128)(2,1)}, bf16[2,64,1536]{2,1,0:T(8,128)(2,1)}, u32[]{:S(2)}, u32[]{:S(2)}) collective-permute-start(bf16[2,64,1536]{2,1,0:T(8,128)(2,1)} %bitcast), channel_id=1, source_target_pairs={{7,0},{8,1},{9,2},{10,3},{11,4},{12,5},{13,6},{14,7},{15,8},{23,16... | collective-permute-start | bytes 1179656 | tf_op jit(solution)/shard_map/ppermute | solution.py:15
  7.5 137.3 %collective-permute-start.13 = (bf16[2,64,1536]{2,1,0:T(8,128)(2,1)}, bf16[2,64,1536]{2,1,0:T(8,128)(2,1)}, u32[]{:S(2)}, u32[]{:S(2)}) collective-permute-start(bf16[2,64,1536]{2,1,0:T(8,128)(2,1)} %bitcast), channel_id=1, source_target_pairs={{6,0},{7,1},{8,2},{9,3},{10,4},{11,5},{12,6},{13,7},{14,8},{15,9},... | collective-permute-start | bytes 1179656 | tf_op jit(solution)/shard_map/ppermute | solution.py:15
  8.8 134.2 %collective-permute-start.12 = (bf16[2,64,1536]{2,1,0:T(8,128)(2,1)}, bf16[2,64,1536]{2,1,0:T(8,128)(2,1)}, u32[]{:S(2)}, u32[]{:S(2)}) collective-permute-start(bf16[2,64,1536]{2,1,0:T(8,128)(2,1)} %bitcast), channel_id=1, source_target_pairs={{5,0},{6,1},{7,2},{8,3},{9,4},{10,5},{11,6},{12,7},{13,8},{14,9},{... | collective-permute-start | bytes 1179656 | tf_op jit(solution)/shard_map/ppermute | solution.py:15
  10.1 56.9 %collective-permute-start.1 = (bf16[2,64,1536]{2,1,0:T(8,128)(2,1)}, bf16[2,64,1536]{2,1,0:T(8,128)(2,1)}, u32[]{:S(2)}, u32[]{:S(2)}) collective-permute-start(bf16[2,64,1536]{2,1,0:T(8,128)(2,1)} %bitcast), channel_id=1, source_target_pairs={{0,7},{1,8},{2,9},{3,10},{4,11},{5,12},{6,13},{7,14},{8,15},{16,23... | collective-permute-start | bytes 1179656 | tf_op jit(solution)/shard_map/ppermute | solution.py:15
  19.1 19.3 %collective-permute-start = (bf16[2,64,1536]{2,1,0:T(8,128)(2,1)}, bf16[2,64,1536]{2,1,0:T(8,128)(2,1)}, u32[]{:S(2)}, u32[]{:S(2)}) collective-permute-start(bf16[2,64,1536]{2,1,0:T(8,128)(2,1)} %bitcast), channel_id=1, source_target_pairs={{0,8},{1,9},{2,10},{3,11},{4,12},{5,13},{6,14},{7,15},{16,24},{17,... | collective-permute-start | bytes 1179656 | tf_op jit(solution)/shard_map/ppermute | solution.py:15
  38.4 35.3 %collective-permute-start.2 = (bf16[2,64,1536]{2,1,0:T(8,128)(2,1)}, bf16[2,64,1536]{2,1,0:T(8,128)(2,1)S(1)}, u32[]{:S(2)}, u32[]{:S(2)}) collective-permute-start(bf16[2,64,1536]{2,1,0:T(8,128)(2,1)} %bitcast), channel_id=1, source_target_pairs={{0,6},{1,7},{2,8},{3,9},{4,10},{5,11},{6,12},{7,13},{8,14},{9,15},... | collective-permute-start | bytes 1179656 | tf_op jit(solution)/shard_map/ppermute | solution.py:15
  73.7 16.9 %collective-permute-start.4 = (bf16[2,64,1536]{2,1,0:T(8,128)(2,1)}, bf16[2,64,1536]{2,1,0:T(8,128)(2,1)S(1)}, u32[]{:S(2)}, u32[]{:S(2)}) collective-permute-start(bf16[2,64,1536]{2,1,0:T(8,128)(2,1)} %bitcast), channel_id=1, source_target_pairs={{0,4},{1,5},{2,6},{3,7},{4,8},{5,9},{6,10},{7,11},{8,12},{9,13},{1... | collective-permute-start | bytes 1179656 | tf_op jit(solution)/shard_map/ppermute | solution.py:15
  106.2 16.6 %collective-permute-start.9 = (bf16[2,64,1536]{2,1,0:T(8,128)(2,1)}, bf16[2,64,1536]{2,1,0:T(8,128)(2,1)S(1)}, u32[]{:S(2)}, u32[]{:S(2)}) collective-permute-start(bf16[2,64,1536]{2,1,0:T(8,128)(2,1)} %bitcast), channel_id=1, source_target_pairs={{2,0},{3,1},{4,2},{5,3},{6,4},{7,5},{8,6},{9,7},{10,8},{11,9},{12,... | collective-permute-start | bytes 1179656 | tf_op jit(solution)/shard_map/ppermute | solution.py:15
  116.4 17.9 %collective-permute-start.10 = (bf16[2,64,1536]{2,1,0:T(8,128)(2,1)}, bf16[2,64,1536]{2,1,0:T(8,128)(2,1)S(1)}, u32[]{:S(2)}, u32[]{:S(2)}) collective-permute-start(bf16[2,64,1536]{2,1,0:T(8,128)(2,1)} %bitcast), channel_id=1, source_target_pairs={{3,0},{4,1},{5,2},{6,3},{7,4},{8,5},{9,6},{10,7},{11,8},{12,9},{13... | collective-permute-start | bytes 1179656 | tf_op jit(solution)/shard_map/ppermute | solution.py:15
  122.8 19.4 %collective-permute-start.11 = (bf16[2,64,1536]{2,1,0:T(8,128)(2,1)}, bf16[2,64,1536]{2,1,0:T(8,128)(2,1)S(1)}, u32[]{:S(2)}, u32[]{:S(2)}) collective-permute-start(bf16[2,64,1536]{2,1,0:T(8,128)(2,1)} %bitcast), channel_id=1, source_target_pairs={{4,0},{5,1},{6,2},{7,3},{8,4},{9,5},{10,6},{11,7},{12,8},{13,9},{1... | collective-permute-start | bytes 1179656 | tf_op jit(solution)/shard_map/ppermute | solution.py:15
  284.9 20.5 %collective-permute-start.15 = (bf16[2,64,1536]{2,1,0:T(8,128)(2,1)S(1)}, bf16[2,64,1536]{2,1,0:T(8,128)(2,1)S(1)}, u32[]{:S(2)}, u32[]{:S(2)}) collective-permute-start(bf16[2,64,1536]{2,1,0:T(8,128)(2,1)S(1)} %get-tuple-element.6), channel_id=1, source_target_pairs={{8,0},{9,1},{10,2},{11,3},{12,4},{13,5},{14,6},{15,7},{24,16},{25,... | collective-permute-start | bytes 1179656 | tf_op jit(solution)/shard_map/ppermute | solution.py:15
  286.2 20.6 %collective-permute-start.29 = (bf16[2,64,1536]{2,1,0:T(8,128)(2,1)S(1)}, bf16[2,64,1536]{2,1,0:T(8,128)(2,1)S(1)}, u32[]{:S(2)}, u32[]{:S(2)}) collective-permute-start(bf16[2,64,1536]{2,1,0:T(8,128)(2,1)S(1)} %get-tuple-element.7), channel_id=1, source_target_pairs={{0,7},{1,8},{2,9},{3,10},{4,11},{5,12},{6,13},{7,14},{8,15},{16,23... | collective-permute-start | bytes 1179656 | tf_op jit(solution)/shard_map/ppermute | solution.py:15
  297.0 19.8 %collective-permute-start.27 = (bf16[2,64,1536]{2,1,0:T(8,128)(2,1)S(1)}, bf16[2,64,1536]{2,1,0:T(8,128)(2,1)S(1)}, u32[]{:S(2)}, u32[]{:S(2)}) collective-permute-start(bf16[2,64,1536]{2,1,0:T(8,128)(2,1)S(1)} %get-tuple-element.9), channel_id=1, source_target_pairs={{0,5},{1,6},{2,7},{3,8},{4,9},{5,10},{6,11},{7,12},{8,13},{9,14},{... | collective-permute-start | bytes 1179656 | tf_op jit(solution)/shard_map/ppermute | solution.py:15
  302.4 22.8 %collective-permute-start.26 = (bf16[2,64,1536]{2,1,0:T(8,128)(2,1)S(1)}, bf16[2,64,1536]{2,1,0:T(8,128)(2,1)S(1)}, u32[]{:S(2)}, u32[]{:S(2)}) collective-permute-start(bf16[2,64,1536]{2,1,0:T(8,128)(2,1)S(1)} %get-tuple-element.10), channel_id=1, source_target_pairs={{0,4},{1,5},{2,6},{3,7},{4,8},{5,9},{6,10},{7,11},{8,12},{9,13},{1... | collective-permute-start | bytes 1179656 | tf_op jit(solution)/shard_map/ppermute | solution.py:15
  305.4 24.6 %collective-permute-start.25 = (bf16[2,64,1536]{2,1,0:T(8,128)(2,1)S(1)}, bf16[2,64,1536]{2,1,0:T(8,128)(2,1)S(1)}, u32[]{:S(2)}, u32[]{:S(2)}) collective-permute-start(bf16[2,64,1536]{2,1,0:T(8,128)(2,1)S(1)} %get-tuple-element.11), channel_id=1, source_target_pairs={{0,3},{1,4},{2,5},{3,6},{4,7},{5,8},{6,9},{7,10},{8,11},{9,12},{10... | collective-permute-start | bytes 1179656 | tf_op jit(solution)/shard_map/ppermute | solution.py:15
  306.8 24.5 %collective-permute-start.24 = (bf16[2,64,1536]{2,1,0:T(8,128)(2,1)S(1)}, bf16[2,64,1536]{2,1,0:T(8,128)(2,1)S(1)}, u32[]{:S(2)}, u32[]{:S(2)}) collective-permute-start(bf16[2,64,1536]{2,1,0:T(8,128)(2,1)S(1)} %get-tuple-element.12), channel_id=1, source_target_pairs={{0,2},{1,3},{2,4},{3,5},{4,6},{5,7},{6,8},{7,9},{8,10},{9,11},{10,... | collective-permute-start | bytes 1179656 | tf_op jit(solution)/shard_map/ppermute | solution.py:15
  308.5 24.1 %collective-permute-start.23 = (bf16[2,64,1536]{2,1,0:T(8,128)(2,1)S(1)}, bf16[2,64,1536]{2,1,0:T(8,128)(2,1)S(1)}, u32[]{:S(2)}, u32[]{:S(2)}) collective-permute-start(bf16[2,64,1536]{2,1,0:T(8,128)(2,1)S(1)} %get-tuple-element.13), channel_id=1, source_target_pairs={{0,1},{1,2},{2,3},{3,4},{4,5},{5,6},{6,7},{7,8},{8,9},{9,10},{10,1... | collective-permute-start | bytes 1179656 | tf_op jit(solution)/shard_map/ppermute | solution.py:15
  316.8 17.1 %collective-permute-start.22 = (bf16[2,64,1536]{2,1,0:T(8,128)(2,1)S(1)}, bf16[2,64,1536]{2,1,0:T(8,128)(2,1)S(1)}, u32[]{:S(2)}, u32[]{:S(2)}) collective-permute-start(bf16[2,64,1536]{2,1,0:T(8,128)(2,1)S(1)} %get-tuple-element.14), channel_id=1, source_target_pairs={{1,0},{2,1},{3,2},{4,3},{5,4},{6,5},{7,6},{8,7},{9,8},{10,9},{11,1... | collective-permute-start | bytes 1179656 | tf_op jit(solution)/shard_map/ppermute | solution.py:15
  326.0 15.2 %collective-permute-start.21 = (bf16[2,64,1536]{2,1,0:T(8,128)(2,1)S(1)}, bf16[2,64,1536]{2,1,0:T(8,128)(2,1)S(1)}, u32[]{:S(2)}, u32[]{:S(2)}) collective-permute-start(bf16[2,64,1536]{2,1,0:T(8,128)(2,1)S(1)} %get-tuple-element.15), channel_id=1, source_target_pairs={{2,0},{3,1},{4,2},{5,3},{6,4},{7,5},{8,6},{9,7},{10,8},{11,9},{12,... | collective-permute-start | bytes 1179656 | tf_op jit(solution)/shard_map/ppermute | solution.py:15
  330.0 38.6 %collective-permute-start.20 = (bf16[2,64,1536]{2,1,0:T(8,128)(2,1)}, bf16[2,64,1536]{2,1,0:T(8,128)(2,1)}, u32[]{:S(2)}, u32[]{:S(2)}) collective-permute-start(bf16[2,64,1536]{2,1,0:T(8,128)(2,1)} %get-tuple-element.16), channel_id=1, source_target_pairs={{3,0},{4,1},{5,2},{6,3},{7,4},{8,5},{9,6},{10,7},{11,8},{12,9},{13... | collective-permute-start | bytes 1179656 | tf_op jit(solution)/shard_map/ppermute | solution.py:15
  331.3 37.3 %collective-permute-start.19 = (bf16[2,64,1536]{2,1,0:T(8,128)(2,1)}, bf16[2,64,1536]{2,1,0:T(8,128)(2,1)}, u32[]{:S(2)}, u32[]{:S(2)}) collective-permute-start(bf16[2,64,1536]{2,1,0:T(8,128)(2,1)} %get-tuple-element.17), channel_id=1, source_target_pairs={{4,0},{5,1},{6,2},{7,3},{8,4},{9,5},{10,6},{11,7},{12,8},{13,9},{1... | collective-permute-start | bytes 1179656 | tf_op jit(solution)/shard_map/ppermute | solution.py:15
  332.6 55.7 %collective-permute-start.18 = (bf16[2,64,1536]{2,1,0:T(8,128)(2,1)}, bf16[2,64,1536]{2,1,0:T(8,128)(2,1)}, u32[]{:S(2)}, u32[]{:S(2)}) collective-permute-start(bf16[2,64,1536]{2,1,0:T(8,128)(2,1)} %get-tuple-element.18), channel_id=1, source_target_pairs={{5,0},{6,1},{7,2},{8,3},{9,4},{10,5},{11,6},{12,7},{13,8},{14,9},{... | collective-permute-start | bytes 1179656 | tf_op jit(solution)/shard_map/ppermute | solution.py:15
  333.9 57.7 %collective-permute-start.17 = (bf16[2,64,1536]{2,1,0:T(8,128)(2,1)}, bf16[2,64,1536]{2,1,0:T(8,128)(2,1)}, u32[]{:S(2)}, u32[]{:S(2)}) collective-permute-start(bf16[2,64,1536]{2,1,0:T(8,128)(2,1)} %get-tuple-element.19), channel_id=1, source_target_pairs={{6,0},{7,1},{8,2},{9,3},{10,4},{11,5},{12,6},{13,7},{14,8},{15,9},... | collective-permute-start | bytes 1179656 | tf_op jit(solution)/shard_map/ppermute | solution.py:15
  341.9 83.5 %collective-permute-start.16 = (bf16[2,64,1536]{2,1,0:T(8,128)(2,1)}, bf16[2,64,1536]{2,1,0:T(8,128)(2,1)}, u32[]{:S(2)}, u32[]{:S(2)}) collective-permute-start(bf16[2,64,1536]{2,1,0:T(8,128)(2,1)} %get-tuple-element.20), channel_id=1, source_target_pairs={{7,0},{8,1},{9,2},{10,3},{11,4},{12,5},{13,6},{14,7},{15,8},{23,16... | collective-permute-start | bytes 1179656 | tf_op jit(solution)/shard_map/ppermute | solution.py:15
  (32 other events, 645.5 us)
where the time goes:
time: 434 us; the launch traced here: 431 us
  waiting for transfers between devices  121 us (28%)
  local copies, waits for them, and re-layouts  114 us (26%)
  starting transfers between devices  100 us (23%)
  matrix products  52 us (12%)
  other arithmetic  43 us (10%)
    ppermute x30, waiting for transfers between devices, passed_along(): return lax.ppermute(block, axis, route)  121 us
    ppermute x30, starting transfers between devices, passed_along(): return lax.ppermute(block, axis, route)  100 us
    concatenate x3, local copies, waits for them, and re-layouts, attend(): jnp.concatenate([key_grad, value_grad], axis=-1)  23.2 us
    unnamed x67, local copies, waits for them, and re-layouts  19 us
    dot_general x1, matrix products, attend(): jnp.einsum('qhtk,qthd->qkhd', score_grad, query_heads, preferred_element_...  15.3 us
    dot_general x1, matrix products, attend(): jnp.einsum('qhtk,qkhd->qthd', score_grad, key_heads, preferred_element_ty...  14.4 us
    scatter-add x1, other arithmetic, per_device(): jax.ops.segment_sum(kv_term.reshape(blocks * MAXNB, BLK, 2 * model_width)...  12.9 us
    concatenate x1, other arithmetic, attend(): jnp.concatenate([key_grad, value_grad], axis=-1)  12.4 us
  transfers between devices with their start and end apart: 30, of which 17 were waited for; matrix products, arithmetic and copies ran while one was open for 14% of the time, Pallas kernels for 0%

commit v1 on v0

v1 whole, which is shorter than its diff:
```python
import functools

import jax
import jax.numpy as jnp
from jax import lax
from jax.experimental import pallas as pl
from jax.experimental.pallas import tpu as pltpu
from jax.sharding import PartitionSpec as P

HD = 64
BLK = 64
MAXNB = 8
HALF = 8
REACH = (HALF + 1) // 2
F32 = jnp.float32
BF16 = jnp.bfloat16


def exchange_rounds(chips):
    near = lambda a, b: 0 <= b < chips and abs(a - b) <= REACH
    if chips <= 8 and chips & (chips - 1) == 0:
        masks = list(range(1, chips))
        return [
            (lambda k, m=m: k ^ m, lambda k, m=m: k ^ m, [(k, k ^ m) for k in range(chips) if near(k, k ^ m)])
            for m in masks
        ]
    shifts = [d for d in range(-REACH, REACH + 1) if d != 0]
    return [
        (lambda k, d=d: k + d, lambda k, d=d: k - d, [(k, k + d) for k in range(chips) if near(k, k + d)])
        for d in shifts
    ]


def round_of(chips, mine, peer):
    if chips <= 8 and chips & (chips - 1) == 0:
        return mine ^ peer
    d = peer - mine
    return jnp.where(d < 0, d + REACH + 1, jnp.where(d == 0, 0, d + REACH))


def layer_norm(x):
    center = jnp.mean(x, axis=-1, keepdims=True)
    spread = jnp.mean((x - center) ** 2, axis=-1, keepdims=True)
    inv_std = lax.rsqrt(spread + 1e-05)
    return (x - center) * inv_std, inv_std


def dot(a, b, ca, cb):
    return lax.dot_general(a, b, (((ca,), (cb,)), ((), ())), preferred_element_type=F32)


def main_kernel(rounds, meta, *refs):
    windows = refs[: 2 * (rounds + 1)]
    q_ref, g_ref, gain_ref, w_hbm = refs[2 * (rounds + 1) : 2 * (rounds + 1) + 4]
    outs = refs[2 * (rounds + 1) + 4 :]
    att_ref, dq_ref, own_ref, sib_ref = outs[:4]
    msg_refs = outs[4 : 4 + rounds]
    xs, normed, kv, kvt, acc, w, sems, wsem = outs[4 + rounds :]
    width = q_ref.shape[1]
    slots = 2 * MAXNB
    span = MAXNB * BLK

    wcopy = pltpu.make_async_copy(w_hbm, w, wsem)
    copies = [
        pltpu.make_async_copy(ref, xs.at[pl.ds(2 * i, 2)], sems.at[i]) for i, ref in enumerate(windows)
    ]
    for c in copies:
        c.start()
    wcopy.start()
    acc[...] = jnp.zeros_like(acc)
    for c in copies:
        c.wait()
    gain = gain_ref[...]
    for s in range(slots):
        unit, _ = layer_norm(xs[meta[s]].astype(F32))
        normed[s * BLK : (s + 1) * BLK, :] = (unit * gain).astype(BF16)
    wcopy.wait()
    rows = 256
    for i in range(slots * BLK // rows):
        part = pl.ds(i * rows, rows)
        kv[part, :] = dot(normed[part, :], w[:, width:], 1, 0).astype(BF16)

    lane = lax.broadcasted_iota(jnp.int32, (1, 2 * HD), 1)
    low = (lane < HD).astype(F32)
    high = 1.0 - low
    slot_row = lax.broadcasted_iota(jnp.int32, (span, 1), 0)
    for b in range(2):
        live = slot_row < meta[2 * slots + b] * BLK
        for p in range(width // (2 * HD)):
            lanes = pl.ds(p * 2 * HD, 2 * HD)
            vlanes = pl.ds(width + p * 2 * HD, 2 * HD)
            tok = pl.ds(b * BLK, BLK)
            krows = pl.ds(b * span, span)
            q = q_ref[tok, lanes].astype(F32) * 0.125
            g = g_ref[tok, lanes].astype(F32)
            qd = jnp.concatenate([q * low, q * high], axis=0).astype(BF16)
            gd = jnp.concatenate([g * low, g * high], axis=0).astype(BF16)
            k = kv[krows, lanes]
            v = kv[krows, vlanes]
            scores = jnp.where(live, dot(k, qd, 1, 1), -1e30)
            weights = jnp.exp(scores - jnp.max(scores, axis=0, keepdims=True))
            prob = weights * (1.0 / jnp.sum(weights, axis=0, keepdims=True))
            low_prob = prob.astype(BF16)
            pg = dot(v, gd, 1, 1)
            row_dot = jnp.sum(prob * pg, axis=0, keepdims=True)
            sg = (prob * (pg - row_dot)).astype(BF16)
            kvt[krows, lanes] = dot(sg, qd, 1, 0).astype(BF16)
            kvt[krows, vlanes] = dot(low_prob, gd, 1, 0).astype(BF16)
            att = dot(low_prob, v, 0, 0)
            dq = dot(sg, k, 0, 0) * 0.125
            att_ref[tok, lanes] = jnp.where(lane < HD, att[:BLK], att[BLK:]).astype(BF16)
            dq_ref[tok, lanes] = jnp.where(lane < HD, dq[:BLK], dq[BLK:]).astype(BF16)

    for i in range(slots * BLK // rows):
        part = dot(kvt[pl.ds(i * rows, rows), :], w[:, width:], 1, 1)
        for j in range(rows // BLK):
            at = meta[slots + i * (rows // BLK) + j]
            acc[at] = acc[at] + part[j * BLK : (j + 1) * BLK, :]
    own_ref[0:BLK, :] = acc[0]
    own_ref[BLK : 2 * BLK, :] = acc[1]
    sib_ref[...] = acc[2].astype(BF16)
    for r in range(rounds):
        msg_refs[r][0:BLK, :] = acc[3 + 2 * r].astype(BF16)
        msg_refs[r][BLK : 2 * BLK, :] = acc[4 + 2 * r].astype(BF16)


def main_call(meta, windows, queries, grads, gain, w_qkv):
    rounds = len(windows) // 2 - 1
    tokens, width = queries.shape
    any_spec = pl.BlockSpec(memory_space=pl.ANY)
    vmem = pl.BlockSpec(memory_space=pltpu.VMEM)
    slots = 2 * MAXNB
    outs = [
        jax.ShapeDtypeStruct((tokens, width), BF16),
        jax.ShapeDtypeStruct((tokens, width), BF16),
        jax.ShapeDtypeStruct((tokens, width), F32),
        jax.ShapeDtypeStruct((BLK, width), BF16),
    ] + [jax.ShapeDtypeStruct((2 * BLK, width), BF16)] * rounds
    return pl.pallas_call(
        functools.partial(main_kernel, rounds),
        out_shape=outs,
        in_specs=[pl.BlockSpec(memory_space=pltpu.SMEM)] + [any_spec] * len(windows) + [vmem] * 3 + [any_spec],
        out_specs=[vmem] * len(outs),
        scratch_shapes=[
            pltpu.VMEM((2 * len(windows), BLK, width), BF16),
            pltpu.VMEM((slots * BLK, width), BF16),
            pltpu.VMEM((slots * BLK, 2 * width), BF16),
            pltpu.VMEM((slots * BLK, 2 * width), BF16),
            pltpu.VMEM((4 + 2 * rounds, BLK, width), F32),
            pltpu.VMEM(w_qkv.shape, BF16),
            pltpu.SemaphoreType.DMA((len(windows),)),
            pltpu.SemaphoreType.DMA,
        ],
        compiler_params=pltpu.CompilerParams(vmem_limit_bytes=48 * 2**20),
        cost_estimate=pl.CostEstimate(flops=8 * 10**9, bytes_accessed=12 * 10**6, transcendentals=10**6),
    )(meta, *[x.reshape(2, BLK, width) for x in windows], queries, grads, gain.reshape(1, width), w_qkv)


def final_kernel(rounds, parity, *refs):
    came = refs[:rounds]
    sibs, sib, base, tok_ref, cot_ref, gain_ref, out_ref, total = refs[rounds:]
    total[...] = base[...]
    one = sib[...].astype(F32)
    total[parity[0]] = total[parity[0]] + one
    for r in range(rounds):
        at = parity[1 + r]
        total[at] = total[at] + came[r][0:BLK, :].astype(F32)
        at = parity[1 + rounds + r]
        total[at] = total[at] + sibs[r * BLK : (r + 1) * BLK, :].astype(F32)
    gain = gain_ref[...]
    for b in range(2):
        rows = pl.ds(b * BLK, BLK)
        unit, inv_std = layer_norm(tok_ref[rows, :].astype(F32))
        scaled = total[b] * gain
        centered = (
            scaled
            - jnp.mean(scaled, axis=-1, keepdims=True)
            - unit * jnp.mean(scaled * unit, axis=-1, keepdims=True)
        )
        out_ref[rows, :] = (cot_ref[rows, :].astype(F32) + inv_std * centered).astype(BF16)


def final_call(parity, came, sibs, sib, base, tokens, cotangent, gain):
    rounds = len(came)
    count, width = tokens.shape
    vmem = pl.BlockSpec(memory_space=pltpu.VMEM)
    return pl.pallas_call(
        functools.partial(final_kernel, rounds),
        out_shape=jax.ShapeDtypeStruct((count, width), BF16),
        in_specs=[pl.BlockSpec(memory_space=pltpu.SMEM)] + [vmem] * (rounds + 6),
        out_specs=vmem,
        scratch_shapes=[pltpu.VMEM((2, BLK, width), F32)],
        compiler_params=pltpu.CompilerParams(vmem_limit_bytes=32 * 2**20),
    )(parity, *came, sibs, sib, base.reshape(2, BLK, width), tokens, cotangent, gain.reshape(1, width))


def per_device(tokens, gain, w_qkv, w_out, nbr_list, nbr_count, cotangent):
    devices = lax.axis_size("seq")
    chips = devices // 2
    count, width = tokens.shape
    blocks = count // BLK
    plan = exchange_rounds(chips)
    rounds = len(plan)
    mate = [(i, i ^ 1) for i in range(devices)]

    def fetch(x, pairs):
        return lax.ppermute(x, "seq", [(2 * s + c, 2 * r + c) for r, s in pairs for c in range(2)])

    def give(x, pairs):
        return lax.ppermute(x, "seq", [(2 * r + c, 2 * s + c) for r, s in pairs for c in range(2)])

    arrived = [None] * rounds
    for r in reversed(range(rounds)):
        arrived[r] = fetch(tokens, plan[r][2])
    windows = [tokens, lax.ppermute(tokens, "seq", mate)]
    for r in range(rounds):
        windows += [arrived[r], lax.ppermute(arrived[r], "seq", mate)]

    position = lax.axis_index("seq")
    chip, core = position // 2, position % 2
    my_lists = lax.dynamic_slice_in_dim(nbr_list, position * blocks, blocks, 0)
    my_counts = lax.dynamic_slice_in_dim(nbr_count, position * blocks, blocks, 0)
    owner = my_lists // blocks
    block = my_lists % blocks
    turn = round_of(chips, chip, owner // 2)
    other = (owner % 2) ^ core
    source = (turn * 2 + other) * 2 + block
    target = jnp.where(owner == position, block, 1 + 2 * turn + other)
    live = jnp.arange(MAXNB)[None, :] < my_counts[:, None]
    target = jnp.where(live, target, 3 + 2 * rounds)
    meta = jnp.concatenate([source.reshape(-1), target.reshape(-1), my_counts]).astype(jnp.int32)

    all_live = jnp.arange(MAXNB)[None, :] < nbr_count[:, None]
    names_odd = jnp.any((all_live & (nbr_list == position * blocks + 1)).reshape(devices, -1), axis=1)
    givers = jnp.stack([position ^ 1] + [plan[r][1](chip) * 2 + core for r in range(rounds)]
                       + [plan[r][1](chip) * 2 + (1 - core) for r in range(rounds)])
    parity = jnp.take(names_odd.astype(jnp.int32), jnp.clip(givers, 0, devices - 1))

    unit, _ = layer_norm(tokens.astype(F32))
    normed = (unit * gain).astype(BF16)
    queries = jnp.dot(normed, w_qkv[:, :width], preferred_element_type=F32).astype(BF16)
    out_grad = dot(cotangent, w_out, 1, 1).astype(BF16)

    attended, query_grad, own, sib, *messages = main_call(meta, windows, queries, out_grad, gain, w_qkv)

    sib = lax.ppermute(sib, "seq", mate)
    came = [None] * rounds
    for r in reversed(range(rounds)):
        came[r] = give(messages[r], plan[r][2])
    sibs = lax.ppermute(jnp.concatenate([x[BLK:] for x in came], axis=0), "seq", mate)
    layer_out = (tokens.astype(F32) + jnp.dot(attended, w_out, preferred_element_type=F32)).astype(BF16)
    base = own + dot(query_grad, w_qkv[:, :width], 1, 1)
    token_grad = final_call(parity, came, sibs, sib, base, tokens, cotangent, gain)
    return (layer_out, token_grad)


def solution(mesh):
    in_specs = (
        P(("groups", "seq"), None),
        P(),
        P(),
        P(),
        P("groups", None),
        P("groups"),
        P(("groups", "seq"), None),
    )
    out_specs = (P(("groups", "seq"), None), P(("groups", "seq"), None))
    return jax.shard_map(
        per_device, mesh=mesh, in_specs=in_specs, out_specs=out_specs, check_vma=False
    )
```

time: 434 us -> 97.7 us (0.23)
  the two profiles are of different devices: /device:TPU:1 before, /device:TPU:13 now
where the time goes in v1:
time: 97.7 us; the launch traced here: 97.3 us
  starting transfers between devices  32.9 us (34%)
  waiting for transfers between devices  26.7 us (27%)
  Pallas kernels  20.8 us (21%)
  local copies, waits for them, and re-layouts  7.48 us (8%)
  matrix products  5.12 us (5%)
  other arithmetic  3.33 us (3%)
    pallas_call x1, Pallas kernels, main_call(): pl.pallas_call(functools.partial(main_kernel, rounds), out_shape=outs, in...  19 us
    ppermute x7, waiting for transfers between devices, give(): lax.ppermute(x, 'seq', [(2 * r + c, 2 * s + c) for r, s in pairs for c in...  18.6 us
    ppermute x7, starting transfers between devices, fetch(): lax.ppermute(x, 'seq', [(2 * s + c, 2 * r + c) for r, s in pairs for c in...  12.1 us
    ppermute x7, starting transfers between devices, give(): lax.ppermute(x, 'seq', [(2 * r + c, 2 * s + c) for r, s in pairs for c in...  10.7 us
    ppermute x7, waiting for transfers between devices, fetch(): lax.ppermute(x, 'seq', [(2 * s + c, 2 * r + c) for r, s in pairs for c in...  6.95 us
    ppermute x7, starting transfers between devices, per_device(): windows += [arrived[r], lax.ppermute(arrived[r], 'seq', mate)]  5.53 us
    unnamed x32, local copies, waits for them, and re-layouts  4.75 us
    ppermute x1, starting transfers between devices, per_device(): windows = [tokens, lax.ppermute(tokens, 'seq', mate)]  2.69 us
  transfers between devices with their start and end apart: 24, of which 11 were waited for; matrix products, arithmetic and copies ran while one was open for 12% of the time, Pallas kernels for 0%

profile of v1, /device:TPU:13, one launch (start us, length us, event | category | flops | bytes accessed | tf_op | source)
XLA Modules:
  0.0 97.3 jit_solution(1148116420917608235)
XLA Ops:
  0.6 3.3 %collective-permute-start.11 = (bf16[128,768]{1,0:T(8,128)(2,1)}, bf16[128,768]{1,0:T(8,128)(2,1)S(1)}, u32[]{:S(2)}, u32[]{:S(2)}) collective-permute-start(bf16[128,768]{1,0:T(8,128)(2,1)} %refs_10_.1), channel_id=1, source_target_pairs={{8,4},{9,5},{10,6},{11,7},{4,8},{5,9},{6,10},{7,11},{24,20},{25,21... | collective-permute-start | bytes 589832 | tf_op jit(solution)/shard_map/ppermute | solution.py:207
  4.0 1.9 %collective-permute-start.9 = (bf16[128,768]{1,0:T(8,128)(2,1)}, bf16[128,768]{1,0:T(8,128)(2,1)S(1)}, u32[]{:S(2)}, u32[]{:S(2)}) collective-permute-start(bf16[128,768]{1,0:T(8,128)(2,1)} %refs_10_.1), channel_id=1, source_target_pairs={{8,2},{9,3},{12,6},{13,7},{2,8},{3,9},{6,12},{7,13},{24,18},{25,19... | collective-permute-start | bytes 589832 | tf_op jit(solution)/shard_map/ppermute | solution.py:207
  7.3 3.4 %collective-permute-start.3 = (bf16[128,768]{1,0:T(8,128)(2,1)}, bf16[128,768]{1,0:T(8,128)(2,1)S(1)}, u32[]{:S(2)}, u32[]{:S(2)}) collective-permute-start(bf16[128,768]{1,0:T(8,128)(2,1)} %refs_10_.1), channel_id=1, source_target_pairs={{4,0},{5,1},{6,2},{7,3},{0,4},{1,5},{2,6},{3,7},{12,8},{13,9},{14,... | collective-permute-start | bytes 589832 | tf_op jit(solution)/shard_map/ppermute | solution.py:207
  15.7 1.8 %convolution_convert_fusion.1.refs_16_ = bf16[128,768]{1,0:T(8,128)(2,1)S(1)} fusion(bf16[768,2304]{1,0:T(8,128)(2,1)} %refs_19_.1, bf16[128,768]{1,0:T(8,128)(2,1)} %refs_10_.1, f32[768]{0:T(1024)} %param.8, f32[128]{0:T(128)S(1)} %add_rsqrt_fusion, f32[128]{0:T(128)S(1)} %broadcast_multiply_fusion), kind=kOutput, calls=%fused_computation.4 | convolution fusion | flops 151584768 | bytes 1577984 | tf_op jit(solution)/shard_map/dot_general | solution.py:241
  17.6 2.9 %collective-permute-done.9 = bf16[128,768]{1,0:T(8,128)(2,1)S(1)} collective-permute-done((bf16[128,768]{1,0:T(8,128)(2,1)}, bf16[128,768]{1,0:T(8,128)(2,1)S(1)}, u32[]{:S(2)}, u32[]{:S(2)}) %collective-permute-start.9) | collective-permute-done | bytes 196640 | tf_op jit(solution)/shard_map/ppermute | solution.py:207
  20.5 2.7 %collective-permute-start = (bf16[128,768]{1,0:T(8,128)(2,1)S(1)}, bf16[128,768]{1,0:T(8,128)(2,1)S(1)}, u32[]{:S(2)}, u32[]{:S(2)}) collective-permute-start(bf16[128,768]{1,0:T(8,128)(2,1)S(1)} %copy-done.1), channel_id=1, source_target_pairs={{0,1},{1,0},{2,3},{3,2},{4,5},{5,4},{6,7},{7,6},{8,9},{9,8},{10,11... | collective-permute-start | bytes 589832 | tf_op jit(solution)/shard_map/ppermute | solution.py:215
  23.2 1.5 %collective-permute-done.7 = bf16[128,768]{1,0:T(8,128)(2,1)S(1)} collective-permute-done((bf16[128,768]{1,0:T(8,128)(2,1)}, bf16[128,768]{1,0:T(8,128)(2,1)S(1)}, u32[]{:S(2)}, u32[]{:S(2)}) %collective-permute-start.7) | collective-permute-done | bytes 196640 | tf_op jit(solution)/shard_map/ppermute | solution.py:207
  24.8 2.0 %collective-permute-start.13 = (bf16[128,768]{1,0:T(8,128)(2,1)S(1)}, bf16[128,768]{1,0:T(8,128)(2,1)S(1)}, u32[]{:S(2)}, u32[]{:S(2)}) collective-permute-start(bf16[128,768]{1,0:T(8,128)(2,1)S(1)} %copy-done.1), channel_id=1, source_target_pairs={{10,4},{11,5},{8,6},{9,7},{6,8},{7,9},{4,10},{5,11},{26,20},{27,21... | collective-permute-start | bytes 589832 | tf_op jit(solution)/shard_map/ppermute | solution.py:207
  26.8 1.9 %collective-permute-start.12 = (bf16[128,768]{1,0:T(8,128)(2,1)S(1)}, bf16[128,768]{1,0:T(8,128)(2,1)S(1)}, u32[]{:S(2)}, u32[]{:S(2)}) collective-permute-start(bf16[128,768]{1,0:T(8,128)(2,1)S(1)} %collective-permute-done.11), channel_id=1, source_target_pairs={{0,1},{1,0},{2,3},{3,2},{4,5},{5,4},{6,7},{7,6},{8,9},{9,8},{10,11... | collective-permute-start | bytes 589832 | tf_op jit(solution)/shard_map/ppermute | solution.py:217
  29.9 2.5 %collective-permute-done.13 = bf16[128,768]{1,0:T(8,128)(2,1)S(1)} collective-permute-done((bf16[128,768]{1,0:T(8,128)(2,1)S(1)}, bf16[128,768]{1,0:T(8,128)(2,1)S(1)}, u32[]{:S(2)}, u32[]{:S(2)}) %collective-permute-start.13) | collective-permute-done | bytes 196640 | tf_op jit(solution)/shard_map/ppermute | solution.py:207
  32.4 2.5 %collective-permute-start.4 = (bf16[128,768]{1,0:T(8,128)(2,1)S(1)}, bf16[128,768]{1,0:T(8,128)(2,1)S(1)}, u32[]{:S(2)}, u32[]{:S(2)}) collective-permute-start(bf16[128,768]{1,0:T(8,128)(2,1)S(1)} %collective-permute-done.3), channel_id=1, source_target_pairs={{0,1},{1,0},{2,3},{3,2},{4,5},{5,4},{6,7},{7,6},{8,9},{9,8},{10,11... | collective-permute-start | bytes 589832 | tf_op jit(solution)/shard_map/ppermute | solution.py:217
  36.6 19.0 %shard_map.86 = (bf16[128,768]{1,0:T(8,128)(2,1)S(1)}, bf16[128,768]{1,0:T(8,128)(2,1)S(1)}, f32[128,768]{1,0:T(8,128)S(1)}, bf16[64,768]{1,0:T(8,128)(2,1)S(1)}...) custom-call(s32[34]{0:T(128)S(1)} %pad_add_fusion.meta, ...), custom_call_target="tpu_custom_call" | custom-call | flops 8000000000 | bytes 12000000 | tf_op jit(solution)/shard_map/pallas_call | solution.py:139
  61.4 2.6 %collective-permute-start.17 = (bf16[128,768]{1,0:T(8,128)(2,1)}, bf16[128,768]{1,0:T(8,128)(2,1)S(1)}, u32[]{:S(2)}, u32[]{:S(2)}) collective-permute-start(bf16[128,768]{1,0:T(8,128)(2,1)} %copy-done.7), channel_id=1, source_target_pairs={{0,6},{1,7},{2,4},{3,5},{4,2},{5,3},{6,0},{7,1},{8,14},{9,15},{10,... | collective-permute-start | bytes 589832 | tf_op jit(solution)/shard_map/ppermute | solution.py:210
  64.0 4.0 %collective-permute-start.19 = (bf16[128,768]{1,0:T(8,128)(2,1)}, bf16[128,768]{1,0:T(8,128)(2,1)S(1)}, u32[]{:S(2)}, u32[]{:S(2)}) collective-permute-start(bf16[128,768]{1,0:T(8,128)(2,1)} %copy-done.5), channel_id=1, source_target_pairs={{2,8},{3,9},{6,12},{7,13},{8,2},{9,3},{12,6},{13,7},{18,24},{19,25... | collective-permute-start | bytes 589832 | tf_op jit(solution)/shard_map/ppermute | solution.py:210
  68.0 1.9 %collective-permute-start.20 = (bf16[128,768]{1,0:T(8,128)(2,1)}, bf16[128,768]{1,0:T(8,128)(2,1)S(1)}, u32[]{:S(2)}, u32[]{:S(2)}) collective-permute-start(bf16[128,768]{1,0:T(8,128)(2,1)} %copy-done.4), channel_id=1, source_target_pairs={{4,8},{5,9},{6,10},{7,11},{8,4},{9,5},{10,6},{11,7},{20,24},{21,25... | collective-permute-start | bytes 589832 | tf_op jit(solution)/shard_map/ppermute | solution.py:210
  70.0 2.1 %collective-permute-start.21 = (bf16[128,768]{1,0:T(8,128)(2,1)}, bf16[128,768]{1,0:T(8,128)(2,1)S(1)}, u32[]{:S(2)}, u32[]{:S(2)}) collective-permute-start(bf16[128,768]{1,0:T(8,128)(2,1)} %copy-done.3), channel_id=1, source_target_pairs={{4,10},{5,11},{6,8},{7,9},{8,6},{9,7},{10,4},{11,5},{20,26},{21,27... | collective-permute-start | bytes 589832 | tf_op jit(solution)/shard_map/ppermute | solution.py:210
  72.1 2.4 %collective-permute-done.17.refs_2_ = bf16[128,768]{1,0:T(8,128)(2,1)S(1)} collective-permute-done((bf16[128,768]{1,0:T(8,128)(2,1)}, bf16[128,768]{1,0:T(8,128)(2,1)S(1)}, u32[]{:S(2)}, u32[]{:S(2)}) %collective-permute-start.17) | collective-permute-done | bytes 196640 | tf_op jit(solution)/shard_map/ppermute | solution.py:210
  74.5 1.6 %collective-permute-done.18.refs_3_ = bf16[128,768]{1,0:T(8,128)(2,1)S(1)} collective-permute-done((bf16[128,768]{1,0:T(8,128)(2,1)}, bf16[128,768]{1,0:T(8,128)(2,1)S(1)}, u32[]{:S(2)}, u32[]{:S(2)}) %collective-permute-start.18) | collective-permute-done | bytes 196640 | tf_op jit(solution)/shard_map/ppermute | solution.py:210
  76.1 4.2 %collective-permute-done.19.refs_4_ = bf16[128,768]{1,0:T(8,128)(2,1)S(1)} collective-permute-done((bf16[128,768]{1,0:T(8,128)(2,1)}, bf16[128,768]{1,0:T(8,128)(2,1)S(1)}, u32[]{:S(2)}, u32[]{:S(2)}) %collective-permute-start.19) | collective-permute-done | bytes 196640 | tf_op jit(solution)/shard_map/ppermute | solution.py:210
  80.4 4.3 %collective-permute-done.20.refs_5_ = bf16[128,768]{1,0:T(8,128)(2,1)S(1)} collective-permute-done((bf16[128,768]{1,0:T(8,128)(2,1)}, bf16[128,768]{1,0:T(8,128)(2,1)S(1)}, u32[]{:S(2)}, u32[]{:S(2)}) %collective-permute-start.20) | collective-permute-done | bytes 196640 | tf_op jit(solution)/shard_map/ppermute | solution.py:210
  84.6 6.1 %collective-permute-done.21.refs_6_ = bf16[128,768]{1,0:T(8,128)(2,1)S(1)} collective-permute-done((bf16[128,768]{1,0:T(8,128)(2,1)}, bf16[128,768]{1,0:T(8,128)(2,1)S(1)}, u32[]{:S(2)}, u32[]{:S(2)}) %collective-permute-start.21) | collective-permute-done | bytes 196640 | tf_op jit(solution)/shard_map/ppermute | solution.py:210
  90.7 1.8 %collective-permute-start.22 = (bf16[448,768]{1,0:T(8,128)(2,1)S(1)}, bf16[448,768]{1,0:T(8,128)(2,1)S(1)}, u32[]{:S(2)}, u32[]{:S(2)}) collective-permute-start(bf16[448,768]{1,0:T(8,128)(2,1)S(1)} %slice_dynamic-update-slice_fusion), channel_id=1, source_target_pairs={{0,1},{1,0},{2,3},{3,2},{4,5},{5,4},{6,7},{7,6},{8,9},{9,8},{10,11... | collective-permute-start | bytes 2064392 | tf_op jit(solution)/shard_map/ppermute | solution.py:250
  93.6 1.8 %fusion.1 = f32[128,768]{1,0:T(8,128)S(1)} fusion(bf16[128,768]{1,0:T(8,128)(2,1)S(1)} %get-tuple-element.23, bf16[768,2304]{1,0:T(8,128)(2,1)} %refs_19_.1), kind=kOutput, calls=%fused_computation.5 | convolution fusion | flops 150994944 | bytes 1769472 | tf_op jit(solution)/shard_map/dot_general | solution.py:49
  95.5 1.8 %shard_map.87 = bf16[128,768]{1,0:T(8,128)(2,1)} custom-call(s32[15]{0:T(128)S(1)} %and_select_fusion.parity, bf16[128,768]{1,0:T(8,128)(2,1)S(1)} %collective-permute-done.15.refs_0_, bf16[128,768]{1,0:T(8,128)(2,1)S(1)} %collective-permute-done.16.refs_1_, bf16[128,768]{1,0:T(8,128)(2,1)S(1)} %collective-permute-done.17.refs_2_, ...), custom_call_target="tpu_custom_call" | custom-call | tf_op jit(solution)/shard_map/pallas_call | solution.py:187
  (86 shorter events, 16.3 us)
Async XLA Ops:
  0.6 16.9 %collective-permute-start.11 = (bf16[128,768]{1,0:T(8,128)(2,1)}, bf16[128,768]{1,0:T(8,128)(2,1)S(1)}, u32[]{:S(2)}, u32[]{:S(2)}) collective-permute-start(bf16[128,768]{1,0:T(8,128)(2,1)} %refs_10_.1), channel_id=1, source_target_pairs={{8,4},{9,5},{10,6},{11,7},{4,8},{5,9},{6,10},{7,11},{24,20},{25,21... | collective-permute-start | bytes 589832 | tf_op jit(solution)/shard_map/ppermute | solution.py:207
  4.0 16.5 %collective-permute-start.9 = (bf16[128,768]{1,0:T(8,128)(2,1)}, bf16[128,768]{1,0:T(8,128)(2,1)S(1)}, u32[]{:S(2)}, u32[]{:S(2)}) collective-permute-start(bf16[128,768]{1,0:T(8,128)(2,1)} %refs_10_.1), channel_id=1, source_target_pairs={{8,2},{9,3},{12,6},{13,7},{2,8},{3,9},{6,12},{7,13},{24,18},{25,19... | collective-permute-start | bytes 589832 | tf_op jit(solution)/shard_map/ppermute | solution.py:207
  5.9 18.8 %collective-permute-start.7 = (bf16[128,768]{1,0:T(8,128)(2,1)}, bf16[128,768]{1,0:T(8,128)(2,1)S(1)}, u32[]{:S(2)}, u32[]{:S(2)}) collective-permute-start(bf16[128,768]{1,0:T(8,128)(2,1)} %refs_10_.1), channel_id=1, source_target_pairs={{8,0},{9,1},{10,2},{11,3},{12,4},{13,5},{14,6},{15,7},{0,8},{1,9},... | collective-permute-start | bytes 589832 | tf_op jit(solution)/shard_map/ppermute | solution.py:207
  6.0 20.8 %collective-permute-start.5 = (bf16[128,768]{1,0:T(8,128)(2,1)}, bf16[128,768]{1,0:T(8,128)(2,1)S(1)}, u32[]{:S(2)}, u32[]{:S(2)}) collective-permute-start(bf16[128,768]{1,0:T(8,128)(2,1)} %refs_10_.1), channel_id=1, source_target_pairs={{6,0},{7,1},{4,2},{5,3},{2,4},{3,5},{0,6},{1,7},{14,8},{15,9},{12,... | collective-permute-start | bytes 589832 | tf_op jit(solution)/shard_map/ppermute | solution.py:207
  7.3 21.4 %collective-permute-start.3 = (bf16[128,768]{1,0:T(8,128)(2,1)}, bf16[128,768]{1,0:T(8,128)(2,1)S(1)}, u32[]{:S(2)}, u32[]{:S(2)}) collective-permute-start(bf16[128,768]{1,0:T(8,128)(2,1)} %refs_10_.1), channel_id=1, source_target_pairs={{4,0},{5,1},{6,2},{7,3},{0,4},{1,5},{2,6},{3,7},{12,8},{13,9},{14,... | collective-permute-start | bytes 589832 | tf_op jit(solution)/shard_map/ppermute | solution.py:207
  17.5 11.8 %collective-permute-start.1 = (bf16[128,768]{1,0:T(8,128)(2,1)S(1)}, bf16[128,768]{1,0:T(8,128)(2,1)S(1)}, u32[]{:S(2)}, u32[]{:S(2)}) collective-permute-start(bf16[128,768]{1,0:T(8,128)(2,1)S(1)} %copy-done.1), channel_id=1, source_target_pairs={{2,0},{3,1},{0,2},{1,3},{6,4},{7,5},{4,6},{5,7},{10,8},{11,9},{8,1... | collective-permute-start | bytes 589832 | tf_op jit(solution)/shard_map/ppermute | solution.py:207
  20.5 9.3 %collective-permute-start = (bf16[128,768]{1,0:T(8,128)(2,1)S(1)}, bf16[128,768]{1,0:T(8,128)(2,1)S(1)}, u32[]{:S(2)}, u32[]{:S(2)}) collective-permute-start(bf16[128,768]{1,0:T(8,128)(2,1)S(1)} %copy-done.1), channel_id=1, source_target_pairs={{0,1},{1,0},{2,3},{3,2},{4,5},{5,4},{6,7},{7,6},{8,9},{9,8},{10,11... | collective-permute-start | bytes 589832 | tf_op jit(solution)/shard_map/ppermute | solution.py:215
  24.8 7.6 %collective-permute-start.13 = (bf16[128,768]{1,0:T(8,128)(2,1)S(1)}, bf16[128,768]{1,0:T(8,128)(2,1)S(1)}, u32[]{:S(2)}, u32[]{:S(2)}) collective-permute-start(bf16[128,768]{1,0:T(8,128)(2,1)S(1)} %copy-done.1), channel_id=1, source_target_pairs={{10,4},{11,5},{8,6},{9,7},{6,8},{7,9},{4,10},{5,11},{26,20},{27,21... | collective-permute-start | bytes 589832 | tf_op jit(solution)/shard_map/ppermute | solution.py:207
  26.8 8.1 %collective-permute-start.12 = (bf16[128,768]{1,0:T(8,128)(2,1)S(1)}, bf16[128,768]{1,0:T(8,128)(2,1)S(1)}, u32[]{:S(2)}, u32[]{:S(2)}) collective-permute-start(bf16[128,768]{1,0:T(8,128)(2,1)S(1)} %collective-permute-done.11), channel_id=1, source_target_pairs={{0,1},{1,0},{2,3},{3,2},{4,5},{5,4},{6,7},{7,6},{8,9},{9,8},{10,11... | collective-permute-start | bytes 589832 | tf_op jit(solution)/shard_map/ppermute | solution.py:217
  28.7 6.2 %collective-permute-start.10 = (bf16[128,768]{1,0:T(8,128)(2,1)S(1)}, bf16[128,768]{1,0:T(8,128)(2,1)S(1)}, u32[]{:S(2)}, u32[]{:S(2)}) collective-permute-start(bf16[128,768]{1,0:T(8,128)(2,1)S(1)} %collective-permute-done.9), channel_id=1, source_target_pairs={{0,1},{1,0},{2,3},{3,2},{4,5},{5,4},{6,7},{7,6},{8,9},{9,8},{10,11... | collective-permute-start | bytes 589832 | tf_op jit(solution)/shard_map/ppermute | solution.py:217
  29.3 6.1 %collective-permute-start.8 = (bf16[128,768]{1,0:T(8,128)(2,1)S(1)}, bf16[128,768]{1,0:T(8,128)(2,1)S(1)}, u32[]{:S(2)}, u32[]{:S(2)}) collective-permute-start(bf16[128,768]{1,0:T(8,128)(2,1)S(1)} %collective-permute-done.7), channel_id=1, source_target_pairs={{0,1},{1,0},{2,3},{3,2},{4,5},{5,4},{6,7},{7,6},{8,9},{9,8},{10,11... | collective-permute-start | bytes 589832 | tf_op jit(solution)/shard_map/ppermute | solution.py:217
  29.8 5.6 %collective-permute-start.6 = (bf16[128,768]{1,0:T(8,128)(2,1)S(1)}, bf16[128,768]{1,0:T(8,128)(2,1)S(1)}, u32[]{:S(2)}, u32[]{:S(2)}) collective-permute-start(bf16[128,768]{1,0:T(8,128)(2,1)S(1)} %collective-permute-done.5), channel_id=1, source_target_pairs={{0,1},{1,0},{2,3},{3,2},{4,5},{5,4},{6,7},{7,6},{8,9},{9,8},{10,11... | collective-permute-start | bytes 589832 | tf_op jit(solution)/shard_map/ppermute | solution.py:217
  32.4 3.5 %collective-permute-start.4 = (bf16[128,768]{1,0:T(8,128)(2,1)S(1)}, bf16[128,768]{1,0:T(8,128)(2,1)S(1)}, u32[]{:S(2)}, u32[]{:S(2)}) collective-permute-start(bf16[128,768]{1,0:T(8,128)(2,1)S(1)} %collective-permute-done.3), channel_id=1, source_target_pairs={{0,1},{1,0},{2,3},{3,2},{4,5},{5,4},{6,7},{7,6},{8,9},{9,8},{10,11... | collective-permute-start | bytes 589832 | tf_op jit(solution)/shard_map/ppermute | solution.py:217
  34.9 1.4 %collective-permute-start.2 = (bf16[128,768]{1,0:T(8,128)(2,1)S(1)}, bf16[128,768]{1,0:T(8,128)(2,1)S(1)}, u32[]{:S(2)}, u32[]{:S(2)}) collective-permute-start(bf16[128,768]{1,0:T(8,128)(2,1)S(1)} %collective-permute-done.1), channel_id=1, source_target_pairs={{0,1},{1,0},{2,3},{3,2},{4,5},{5,4},{6,7},{7,6},{8,9},{9,8},{10,11... | collective-permute-start | bytes 589832 | tf_op jit(solution)/shard_map/ppermute | solution.py:217
  34.9 1.7 %collective-permute-start.14 = (bf16[128,768]{1,0:T(8,128)(2,1)S(1)}, bf16[128,768]{1,0:T(8,128)(2,1)S(1)}, u32[]{:S(2)}, u32[]{:S(2)}) collective-permute-start(bf16[128,768]{1,0:T(8,128)(2,1)S(1)} %collective-permute-done.13), channel_id=1, source_target_pairs={{0,1},{1,0},{2,3},{3,2},{4,5},{5,4},{6,7},{7,6},{8,9},{9,8},{10,11... | collective-permute-start | bytes 589832 | tf_op jit(solution)/shard_map/ppermute | solution.py:217
  60.3 7.7 %collective-permute-start.15 = (bf16[128,768]{1,0:T(8,128)(2,1)}, bf16[128,768]{1,0:T(8,128)(2,1)S(1)}, u32[]{:S(2)}, u32[]{:S(2)}) collective-permute-start(bf16[128,768]{1,0:T(8,128)(2,1)} %get-tuple-element.14), channel_id=1, source_target_pairs={{0,2},{1,3},{2,0},{3,1},{4,6},{5,7},{6,4},{7,5},{8,10},{9,11},{10,... | collective-permute-start | bytes 589832 | tf_op jit(solution)/shard_map/ppermute | solution.py:210
  61.3 8.7 %collective-permute-start.16 = (bf16[128,768]{1,0:T(8,128)(2,1)}, bf16[128,768]{1,0:T(8,128)(2,1)S(1)}, u32[]{:S(2)}, u32[]{:S(2)}) collective-permute-start(bf16[128,768]{1,0:T(8,128)(2,1)} %copy-done.8), channel_id=1, source_target_pairs={{0,4},{1,5},{2,6},{3,7},{4,0},{5,1},{6,2},{7,3},{8,12},{9,13},{10,... | collective-permute-start | bytes 589832 | tf_op jit(solution)/shard_map/ppermute | solution.py:210
  61.4 13.1 %collective-permute-start.17 = (bf16[128,768]{1,0:T(8,128)(2,1)}, bf16[128,768]{1,0:T(8,128)(2,1)S(1)}, u32[]{:S(2)}, u32[]{:S(2)}) collective-permute-start(bf16[128,768]{1,0:T(8,128)(2,1)} %copy-done.7), channel_id=1, source_target_pairs={{0,6},{1,7},{2,4},{3,5},{4,2},{5,3},{6,0},{7,1},{8,14},{9,15},{10,... | collective-permute-start | bytes 589832 | tf_op jit(solution)/shard_map/ppermute | solution.py:210
  64.0 12.0 %collective-permute-start.18 = (bf16[128,768]{1,0:T(8,128)(2,1)}, bf16[128,768]{1,0:T(8,128)(2,1)S(1)}, u32[]{:S(2)}, u32[]{:S(2)}) collective-permute-start(bf16[128,768]{1,0:T(8,128)(2,1)} %copy-done.6), channel_id=1, source_target_pairs={{0,8},{1,9},{2,10},{3,11},{4,12},{5,13},{6,14},{7,15},{8,0},{9,1},... | collective-permute-start | bytes 589832 | tf_op jit(solution)/shard_map/ppermute | solution.py:210
  64.0 16.3 %collective-permute-start.19 = (bf16[128,768]{1,0:T(8,128)(2,1)}, bf16[128,768]{1,0:T(8,128)(2,1)S(1)}, u32[]{:S(2)}, u32[]{:S(2)}) collective-permute-start(bf16[128,768]{1,0:T(8,128)(2,1)} %copy-done.5), channel_id=1, source_target_pairs={{2,8},{3,9},{6,12},{7,13},{8,2},{9,3},{12,6},{13,7},{18,24},{19,25... | collective-permute-start | bytes 589832 | tf_op jit(solution)/shard_map/ppermute | solution.py:210
  68.0 16.6 %collective-permute-start.20 = (bf16[128,768]{1,0:T(8,128)(2,1)}, bf16[128,768]{1,0:T(8,128)(2,1)S(1)}, u32[]{:S(2)}, u32[]{:S(2)}) collective-permute-start(bf16[128,768]{1,0:T(8,128)(2,1)} %copy-done.4), channel_id=1, source_target_pairs={{4,8},{5,9},{6,10},{7,11},{8,4},{9,5},{10,6},{11,7},{20,24},{21,25... | collective-permute-start | bytes 589832 | tf_op jit(solution)/shard_map/ppermute | solution.py:210
  70.0 20.7 %collective-permute-start.21 = (bf16[128,768]{1,0:T(8,128)(2,1)}, bf16[128,768]{1,0:T(8,128)(2,1)S(1)}, u32[]{:S(2)}, u32[]{:S(2)}) collective-permute-start(bf16[128,768]{1,0:T(8,128)(2,1)} %copy-done.3), channel_id=1, source_target_pairs={{4,10},{5,11},{6,8},{7,9},{8,6},{9,7},{10,4},{11,5},{20,26},{21,27... | collective-permute-start | bytes 589832 | tf_op jit(solution)/shard_map/ppermute | solution.py:210
  90.7 4.8 %collective-permute-start.22 = (bf16[448,768]{1,0:T(8,128)(2,1)S(1)}, bf16[448,768]{1,0:T(8,128)(2,1)S(1)}, u32[]{:S(2)}, u32[]{:S(2)}) collective-permute-start(bf16[448,768]{1,0:T(8,128)(2,1)S(1)} %slice_dynamic-update-slice_fusion), channel_id=1, source_target_pairs={{0,1},{1,0},{2,3},{3,2},{4,5},{5,4},{6,7},{7,6},{8,9},{9,8},{10,11... | collective-permute-start | bytes 2064392 | tf_op jit(solution)/shard_map/ppermute | solution.py:250
  92.5 3.0 %collective-permute-start.23 = (bf16[64,768]{1,0:T(8,128)(2,1)S(1)}, bf16[64,768]{1,0:T(8,128)(2,1)S(1)}, u32[]{:S(2)}, u32[]{:S(2)}) collective-permute-start(bf16[64,768]{1,0:T(8,128)(2,1)S(1)} %copy-done.10), channel_id=1, source_target_pairs={{0,1},{1,0},{2,3},{3,2},{4,5},{5,4},{6,7},{7,6},{8,9},{9,8},{10,11... | collective-permute-start | bytes 294920 | tf_op jit(solution)/shard_map/ppermute | solution.py:246
  (13 other events, 135.2 us)

commit v2 on v1

v2 whole, which is shorter than its diff:
```python
import functools

import jax
import jax.numpy as jnp
from jax import lax
from jax.experimental import pallas as pl
from jax.experimental.pallas import tpu as pltpu
from jax.sharding import PartitionSpec as P

HD = 64
BLK = 64
MAXNB = 8
HALF = 8
REACH = (HALF + 1) // 2
F32 = jnp.float32
BF16 = jnp.bfloat16


class Round:
    def __init__(self, fetch, source, give, giver):
        self.fetch, self.source, self.give, self.giver = fetch, source, give, giver


def exchange_rounds(chips):
    near = lambda a, b: 0 <= a < chips and 0 <= b < chips and abs(a - b) <= REACH
    if chips == 8:
        rounds = []
        for m in range(1, 8):
            pairs = [(k, k ^ m) for k in range(chips) if near(k, k ^ m)]
            relay = m in (3, 5, 7)
            fetch = [(k, k ^ 1) for k, _ in pairs] if relay else pairs
            rounds.append(Round(fetch, (m ^ 1) - 1 if relay else None, pairs, lambda k, m=m: k ^ m))
        return rounds, [5, 1, 3, 0, 2, 6, 4], [3, 5, 4, 6, 2, 1, 0]
    rounds = []
    for d in range(-REACH, REACH + 1):
        if d != 0:
            pairs = [(k, k + d) for k in range(chips) if near(k, k + d)]
            rounds.append(Round(pairs, None, [(s, r) for r, s in pairs], lambda k, d=d: k - d))
    return rounds, list(range(len(rounds))), list(range(len(rounds)))


def round_of(chips, mine, peer):
    if chips == 8:
        return mine ^ peer
    d = peer - mine
    return jnp.where(d < 0, d + REACH + 1, jnp.where(d == 0, 0, d + REACH))


def layer_norm(x):
    center = jnp.mean(x, axis=-1, keepdims=True)
    spread = jnp.mean((x - center) ** 2, axis=-1, keepdims=True)
    inv_std = lax.rsqrt(spread + 1e-05)
    return (x - center) * inv_std, inv_std


def dot(a, b, ca, cb):
    return lax.dot_general(a, b, (((ca,), (cb,)), ((), ())), preferred_element_type=F32)


def call(kernel, out_shape, in_specs, out_specs, scratch, mib, flops=0):
    return pl.pallas_call(
        kernel,
        out_shape=out_shape,
        in_specs=in_specs,
        out_specs=out_specs,
        scratch_shapes=scratch,
        compiler_params=pltpu.CompilerParams(vmem_limit_bytes=mib * 2**20),
        cost_estimate=pl.CostEstimate(flops=flops, bytes_accessed=5 * 10**6, transcendentals=0),
    )


SMEM = pl.BlockSpec(memory_space=pltpu.SMEM)
VMEM = pl.BlockSpec(memory_space=pltpu.VMEM)
ANY = pl.BlockSpec(memory_space=pl.ANY)
HBM = pl.BlockSpec(memory_space=pltpu.HBM)


def weight_copies(source, target, sems):
    rows, columns = target.shape
    band = rows // sems.shape[0]
    from_column = source.shape[1] - columns
    return [
        pltpu.make_async_copy(
            source.at[pl.ds(i * band, band), pl.ds(from_column, columns)],
            target.at[pl.ds(i * band, band)],
            sems.at[i],
        )
        for i in range(sems.shape[0])
    ]


def main_kernel(rounds, meta, *refs):
    count = 2 * (rounds + 1)
    windows = refs[:count]
    q_ref, g_ref, gain_ref, w_hbm = refs[count : count + 4]
    att_ref, dq_ref, own_ref, sib_ref = refs[count + 4 : count + 8]
    msg_refs = refs[count + 8 : count + 8 + rounds]
    normed, kv, kvt, acc, stage, w, msems, wsems = refs[count + 8 + rounds :]
    width = q_ref.shape[1]
    wcopies = weight_copies(w_hbm, w, wsems)
    for c in wcopies:
        c.start()
    slots = 2 * MAXNB
    span = MAXNB * BLK

    gain = gain_ref[...]
    for i in range(count):
        for j in range(2):

            @pl.when(meta[2 * slots + 2 + 2 * i + j] != 0)
            def _():
                unit, _ = layer_norm(windows[i][j * BLK : (j + 1) * BLK, :].astype(F32))
                normed[2 * i + j] = (unit * gain).astype(BF16)

    for c in wcopies:
        c.wait()
    rows = 256
    for i in range(slots * BLK // rows):
        part = jnp.concatenate([normed[meta[4 * i + j]] for j in range(4)], axis=0)
        kv[pl.ds(i * rows, rows), :] = dot(part, w[...], 1, 0).astype(BF16)
    acc[...] = jnp.zeros_like(acc)

    lane = lax.broadcasted_iota(jnp.int32, (1, 2 * HD), 1)
    low = (lane < HD).astype(F32)
    high = 1.0 - low
    slot_row = lax.broadcasted_iota(jnp.int32, (span, 1), 0)
    for b in range(2):
        live = slot_row < meta[2 * slots + b] * BLK
        for p in range(width // (2 * HD)):
            lanes = pl.ds(p * 2 * HD, 2 * HD)
            vlanes = pl.ds(width + p * 2 * HD, 2 * HD)
            tok = pl.ds(b * BLK, BLK)
            krows = pl.ds(b * span, span)
            q = q_ref[tok, lanes].astype(F32) * 0.125
            g = g_ref[tok, lanes].astype(F32)
            qd = jnp.concatenate([q * low, q * high], axis=0).astype(BF16)
            gd = jnp.concatenate([g * low, g * high], axis=0).astype(BF16)
            k = kv[krows, lanes]
            v = kv[krows, vlanes]
            scores = jnp.where(live, dot(k, qd, 1, 1), -1e30)
            weights = jnp.exp(scores - jnp.max(scores, axis=0, keepdims=True))
            prob = weights * (1.0 / jnp.sum(weights, axis=0, keepdims=True))
            low_prob = prob.astype(BF16)
            pg = dot(v, gd, 1, 1)
            row_dot = jnp.sum(prob * pg, axis=0, keepdims=True)
            sg = (prob * (pg - row_dot)).astype(BF16)
            kvt[krows, lanes] = dot(sg, qd, 1, 0).astype(BF16)
            kvt[krows, vlanes] = dot(low_prob, gd, 1, 0).astype(BF16)
            att = dot(low_prob, v, 0, 0)
            dq = dot(sg, k, 0, 0) * 0.125
            att_ref[tok, lanes] = jnp.where(lane < HD, att[:BLK], att[BLK:]).astype(BF16)
            dq_ref[tok, lanes] = jnp.where(lane < HD, dq[:BLK], dq[BLK:]).astype(BF16)

    for i in range(slots * BLK // rows):
        part = dot(kvt[pl.ds(i * rows, rows), :], w[...], 1, 1)
        for j in range(rows // BLK):
            at = meta[slots + i * (rows // BLK) + j]
            acc[at] = acc[at] + part[j * BLK : (j + 1) * BLK, :]
    for r in range(rounds):
        stage[r, 0:BLK, :] = acc[3 + 2 * r].astype(BF16)
        stage[r, BLK : 2 * BLK, :] = acc[4 + 2 * r].astype(BF16)
        pltpu.make_async_copy(stage.at[r], msg_refs[r], msems.at[r]).start()
    own_ref[0:BLK, :] = acc[0]
    own_ref[BLK : 2 * BLK, :] = acc[1]
    sib_ref[...] = acc[2].astype(BF16)
    for r in range(rounds):
        pltpu.make_async_copy(stage.at[r], msg_refs[r], msems.at[r]).wait()


def main_call(meta, windows, queries, grads, gain, w_qkv):
    rounds = len(windows) // 2 - 1
    tokens, width = queries.shape
    slots = 2 * MAXNB
    shape = jax.ShapeDtypeStruct
    return call(
        functools.partial(main_kernel, rounds),
        [shape((tokens, width), BF16)] * 2
        + [shape((tokens, width), F32), shape((BLK, width), BF16)]
        + [shape((2 * BLK, width), BF16)] * rounds,
        [SMEM] + [VMEM] * (len(windows) + 3) + [ANY],
        [VMEM] * 4 + [HBM] * rounds,
        [
            pltpu.VMEM((2 * len(windows), BLK, width), BF16),
            pltpu.VMEM((slots * BLK, 2 * width), BF16),
            pltpu.VMEM((slots * BLK, 2 * width), BF16),
            pltpu.VMEM((4 + 2 * rounds, BLK, width), F32),
            pltpu.VMEM((rounds, 2 * BLK, width), BF16),
            pltpu.VMEM((width, 2 * width), BF16),
            pltpu.SemaphoreType.DMA((rounds,)),
            pltpu.SemaphoreType.DMA((6,)),
        ],
        48,
        8 * 10**9,
    )(meta, *windows, queries, grads, gain, w_qkv)


def add_came(total, came, at, rows):
    total[at] = total[at] + came[rows, :].astype(F32)


def middle_kernel(rows_of, parity, came, *refs):
    att_ref, dq_ref, own_ref, tok_ref, wqkv_hbm, wout_hbm, out_ref, total, wq, wout, sems = refs
    width = tok_ref.shape[1]
    copies = [
        pltpu.make_async_copy(wout_hbm, wout, sems.at[0]),
        pltpu.make_async_copy(wqkv_hbm.at[:, pl.ds(0, width)], wq, sems.at[1]),
    ]
    for c in copies:
        c.start()
    for c in copies:
        c.wait()
    out = tok_ref[...].astype(F32) + dot(att_ref[...], wout[...], 1, 0)
    out_ref[...] = out.astype(BF16)
    base = own_ref[...] + dot(dq_ref[...], wq[...], 1, 1)
    for b in range(2):
        total[b] = base[b * BLK : (b + 1) * BLK, :]
    add_came(total, came, parity[rows_of], pl.ds(0, BLK))


def middle_call(rows_of, parity, came, attended, query_grad, own, tokens, w_qkv, w_out):
    count, width = tokens.shape
    return call(
        functools.partial(middle_kernel, rows_of),
        [jax.ShapeDtypeStruct((count, width), BF16), jax.ShapeDtypeStruct((2, BLK, width), F32)],
        [SMEM] + [VMEM] * 5 + [ANY] * 2,
        [VMEM] * 2,
        [pltpu.VMEM((width, width), BF16)] * 2 + [pltpu.SemaphoreType.DMA((2,))],
        48,
    )(parity, came, attended, query_grad, own, tokens, w_qkv, w_out)


def final_kernel(rounds, done, parity, *refs):
    came, sibs = refs[:rounds], refs[rounds : 2 * rounds]
    sib, base, tok_ref, cot_ref, gain_ref, out_ref, total = refs[2 * rounds :]
    total[...] = base[...]
    add_came(total, sib, parity[0], pl.ds(0, BLK))
    for r in range(rounds):
        if r != done:
            add_came(total, came[r], parity[1 + r], pl.ds(0, BLK))
        add_came(total, sibs[r], parity[1 + rounds + r], pl.ds(BLK, BLK))
    gain = gain_ref[...]
    for b in range(2):
        rows = pl.ds(b * BLK, BLK)
        unit, inv_std = layer_norm(tok_ref[rows, :].astype(F32))
        scaled = total[b] * gain
        centered = (
            scaled
            - jnp.mean(scaled, axis=-1, keepdims=True)
            - unit * jnp.mean(scaled * unit, axis=-1, keepdims=True)
        )
        out_ref[rows, :] = (cot_ref[rows, :].astype(F32) + inv_std * centered).astype(BF16)


def final_call(done, parity, came, sibs, sib, base, tokens, cotangent, gain):
    rounds = len(came)
    count, width = tokens.shape
    return call(
        functools.partial(final_kernel, rounds, done),
        jax.ShapeDtypeStruct((count, width), BF16),
        [SMEM] + [VMEM] * (2 * rounds + 5),
        VMEM,
        [pltpu.VMEM((2, BLK, width), F32)],
        8,
    )(parity, *came, *sibs, sib, base, tokens, cotangent, gain)


def per_device(tokens, gain, w_qkv, w_out, nbr_list, nbr_count, cotangent):
    devices = lax.axis_size("seq")
    chips = devices // 2
    count, width = tokens.shape
    blocks = count // BLK
    plan, fetch_order, give_order = exchange_rounds(chips)
    rounds = len(plan)
    mate = [(i, i ^ 1) for i in range(devices)]

    def send(x, pairs):
        return lax.ppermute(x, "seq", [(2 * s + c, 2 * r + c) for r, s in pairs for c in range(2)])

    arrived, passed = [None] * rounds, [None] * rounds
    for r in fetch_order:
        source = plan[r].source
        arrived[r] = send(tokens if source is None else arrived[source], plan[r].fetch)
    for r in fetch_order:
        passed[r] = lax.ppermute(arrived[r], "seq", mate)
    windows = [tokens, lax.ppermute(tokens, "seq", mate)]
    for r in range(rounds):
        windows += [arrived[r], passed[r]]

    position = lax.axis_index("seq")
    chip, core = position // 2, position % 2
    my_lists = lax.dynamic_slice_in_dim(nbr_list, position * blocks, blocks, 0)
    my_counts = lax.dynamic_slice_in_dim(nbr_count, position * blocks, blocks, 0)
    owner = my_lists // blocks
    block = my_lists % blocks
    turn = round_of(chips, chip, owner // 2)
    other = (owner % 2) ^ core
    source = (turn * 2 + other) * 2 + block
    target = jnp.where(owner == position, block, 1 + 2 * turn + other)
    live = jnp.arange(MAXNB)[None, :] < my_counts[:, None]
    target = jnp.where(live, target, 3 + 2 * rounds)
    named = jnp.any(source.reshape(-1, 1) == jnp.arange(4 * (rounds + 1))[None, :], axis=0)
    meta = jnp.concatenate([source.reshape(-1), target.reshape(-1), my_counts, named]).astype(jnp.int32)

    all_live = jnp.arange(MAXNB)[None, :] < nbr_count[:, None]
    names_odd = jnp.any((all_live & (nbr_list == position * blocks + 1)).reshape(devices, -1), axis=1)
    givers = jnp.stack([position ^ 1] + [plan[r].giver(chip) * 2 + core for r in range(rounds)]
                       + [plan[r].giver(chip) * 2 + (1 - core) for r in range(rounds)])
    parity = jnp.take(names_odd.astype(jnp.int32), jnp.clip(givers, 0, devices - 1))

    gain = gain.reshape(1, width)
    unit, _ = layer_norm(tokens.astype(F32))
    normed = (unit * gain).astype(BF16)
    queries = jnp.dot(normed, w_qkv[:, :width], preferred_element_type=F32).astype(BF16)
    out_grad = dot(cotangent, w_out, 1, 1).astype(BF16)
    attended, query_grad, own, sib, *messages = main_call(meta, windows, queries, out_grad, gain, w_qkv)

    sib = lax.ppermute(sib, "seq", mate)
    came, sibs = [None] * rounds, [None] * rounds
    first, last = give_order[0], give_order[-1]
    for r in give_order:
        if r == last:
            layer_out, base = middle_call(
                1 + first, parity, came[first], attended, query_grad, own, tokens, w_qkv, w_out
            )
            messages[r], layer_out, base = lax.optimization_barrier((messages[r], layer_out, base))
        came[r] = send(messages[r], plan[r].give)
    for r in give_order:
        sibs[r] = lax.ppermute(came[r], "seq", mate)
    token_grad = final_call(first, parity, came, sibs, sib, base, tokens, cotangent, gain)
    return (layer_out, token_grad)


def solution(mesh):
    in_specs = (
        P(("groups", "seq"), None),
        P(),
        P(),
        P(),
        P("groups", None),
        P("groups"),
        P(("groups", "seq"), None),
    )
    out_specs = (P(("groups", "seq"), None), P(("groups", "seq"), None))
    return jax.shard_map(
        per_device, mesh=mesh, in_specs=in_specs, out_specs=out_specs, check_vma=False
    )
```

time: 97.7 us -> 84.8 us (0.87)
  waiting for transfers between devices: 26.7 us -> 15 us
  starting transfers between devices: 32.9 us -> 38.5 us
  local copies, waits for them, and re-layouts: 7.48 us -> 2.73 us
  matrix products: 5.12 us -> 2.31 us
    ppermute x22 -> x28, waiting for transfers between devices: 26.7 us -> 15 us  [the longest x14 13.3 us: send(): lax.ppermute(x, 'seq', [(2 * s + c, 2 * r + c) for r, s in pairs for c in...]
    ppermute x22 -> x28, starting transfers between devices: 30.1 us -> 36.3 us  [the longest x14 26.2 us: send(): lax.ppermute(x, 'seq', [(2 * s + c, 2 * r + c) for r, s in pairs for c in...]
    unnamed x32 -> x6, local copies, waits for them, and re-layouts: 4.75 us -> 0.02 us
    dot_general x2 -> x1, matrix products: 2.34 us -> 0.55 us  [dot(): lax.dot_general(a, b, (((ca,), (cb,)), ((), ())), preferred_element_type=...]
    dot_general x1 -> x0, matrix products: 1.01 us -> none  [per_device(): jnp.dot(attended, w_out, preferred_element_type=F32)]
    pallas_call x2 -> x3, Pallas kernels: 20.8 us -> 21.1 us  [the longest x1 16.2 us: main_call(): call(functools.partial(main_kernel, rounds), [shape((tokens, width), BF16...]
  transfers between devices with their start and end apart: 24 -> 30, of which waited for: 11 -> 9; matrix products, arithmetic and copies ran while one was open for 12% -> 11% of each run, Pallas kernels for 0% -> 4%
where the time goes in v2:
time: 84.8 us; the launch traced here: 84.6 us
  starting transfers between devices  38.5 us (45%)
  Pallas kernels  21.1 us (25%)
  waiting for transfers between devices  15 us (18%)
  other arithmetic  3.98 us (5%)
  local copies, waits for them, and re-layouts  2.73 us (3%)
  matrix products  2.31 us (3%)
  between operations  0.9 us (1%)
    ppermute x14, starting transfers between devices, send(): lax.ppermute(x, 'seq', [(2 * s + c, 2 * r + c) for r, s in pairs for c in...  26.2 us
    pallas_call x1, Pallas kernels, main_call(): call(functools.partial(main_kernel, rounds), [shape((tokens, width), BF16...  16.2 us
    ppermute x14, waiting for transfers between devices, send(): lax.ppermute(x, 'seq', [(2 * s + c, 2 * r + c) for r, s in pairs for c in...  13.3 us
    ppermute x7, starting transfers between devices, per_device(): sibs[r] = lax.ppermute(came[r], 'seq', mate)  6.7 us
    ppermute x7, starting transfers between devices, per_device(): passed[r] = lax.ppermute(arrived[r], 'seq', mate)  3.39 us
    pallas_call x1, Pallas kernels, middle_call(): call(functools.partial(middle_kernel, rows_of), [jax.ShapeDtypeStruct((co...  3.16 us
    ppermute x1, starting transfers between devices, per_device(): windows = [tokens, lax.ppermute(tokens, 'seq', mate)]  1.8 us
    dot_general x1, matrix products, per_device(): jnp.dot(normed, w_qkv[:, :width], preferred_element_type=F32).astype(BF16)  1.76 us
  transfers between devices with their start and end apart: 30, of which 9 were waited for; matrix products, arithmetic and copies ran while one was open for 11% of the time, Pallas kernels for 4%

profile of v2, /device:TPU:13, one launch (start us, length us, event | category | flops | bytes accessed | tf_op | source)
XLA Modules:
  0.0 84.6 jit_solution(18390088306567272179)
XLA Ops:
  0.6 3.2 %collective-permute-start.11 = (bf16[128,768]{1,0:T(8,128)(2,1)}, bf16[128,768]{1,0:T(8,128)(2,1)S(1)}, u32[]{:S(2)}, u32[]{:S(2)}) collective-permute-start(bf16[128,768]{1,0:T(8,128)(2,1)} %refs_16_.1), channel_id=1, source_target_pairs={{8,4},{9,5},{10,6},{11,7},{4,8},{5,9},{6,10},{7,11},{24,20},{25,21... | collective-permute-start | bytes 589832 | tf_op jit(solution)/shard_map/ppermute | solution.py:277
  3.9 1.3 %collective-permute-start.3 = (bf16[128,768]{1,0:T(8,128)(2,1)}, bf16[128,768]{1,0:T(8,128)(2,1)S(1)}, u32[]{:S(2)}, u32[]{:S(2)}) collective-permute-start(bf16[128,768]{1,0:T(8,128)(2,1)} %refs_16_.1), channel_id=1, source_target_pairs={{4,0},{5,1},{6,2},{7,3},{0,4},{1,5},{2,6},{3,7},{12,8},{13,9},{14,... | collective-permute-start | bytes 589832 | tf_op jit(solution)/shard_map/ppermute | solution.py:277
  5.5 1.8 %collective-permute-start = (bf16[128,768]{1,0:T(8,128)(2,1)}, bf16[128,768]{1,0:T(8,128)(2,1)S(1)}, u32[]{:S(2)}, u32[]{:S(2)}) collective-permute-start(bf16[128,768]{1,0:T(8,128)(2,1)} %refs_16_.1), channel_id=1, source_target_pairs={{0,1},{1,0},{2,3},{3,2},{4,5},{5,4},{6,7},{7,6},{8,9},{9,8},{10,11... | collective-permute-start | bytes 589832 | tf_op jit(solution)/shard_map/ppermute | solution.py:285
  14.0 3.3 %collective-permute-start.13 = (bf16[128,768]{1,0:T(8,128)(2,1)S(1)}, bf16[128,768]{1,0:T(8,128)(2,1)S(1)}, u32[]{:S(2)}, u32[]{:S(2)}) collective-permute-start(bf16[128,768]{1,0:T(8,128)(2,1)S(1)} %collective-permute-done.11.refs_12_), channel_id=1, source_target_pairs={{6,4},{7,5},{4,6},{5,7},{10,8},{11,9},{8,10},{9,11},{22,20},{23,21... | collective-permute-start | bytes 589832 | tf_op jit(solution)/shard_map/ppermute | solution.py:277
  17.9 1.3 %collective-permute-start.9 = (bf16[128,768]{1,0:T(8,128)(2,1)S(1)}, bf16[128,768]{1,0:T(8,128)(2,1)S(1)}, u32[]{:S(2)}, u32[]{:S(2)}) collective-permute-start(bf16[128,768]{1,0:T(8,128)(2,1)S(1)} %collective-permute-done.7.refs_8_), channel_id=1, source_target_pairs={{0,2},{1,3},{4,6},{5,7},{10,8},{11,9},{14,12},{15,13},{16,18},{17,... | collective-permute-start | bytes 589832 | tf_op jit(solution)/shard_map/ppermute | solution.py:277
  19.3 2.4 %collective-permute-start.5 = (bf16[128,768]{1,0:T(8,128)(2,1)S(1)}, bf16[128,768]{1,0:T(8,128)(2,1)S(1)}, u32[]{:S(2)}, u32[]{:S(2)}) collective-permute-start(bf16[128,768]{1,0:T(8,128)(2,1)S(1)} %collective-permute-done.3.refs_4_), channel_id=1, source_target_pairs={{2,0},{3,1},{0,2},{1,3},{6,4},{7,5},{4,6},{5,7},{10,8},{11,9},{8,1... | collective-permute-start | bytes 589832 | tf_op jit(solution)/shard_map/ppermute | solution.py:277
  21.7 1.8 %fusion.2.refs_16_ = bf16[128,768]{1,0:T(8,128)(2,1)S(1)} fusion(bf16[768,2304]{1,0:T(8,128)(2,1)} %refs_4_.1, bf16[128,768]{1,0:T(8,128)(2,1)} %refs_16_.1, f32[768]{0:T(1024)} %param.8, f32[128]{0:T(128)S(1)} %add_rsqrt_fusion, f32[128]{0:T(128)S(1)} %broadcast_multiply_fusion), kind=kOutput, calls=%fused_computation.3 | convolution fusion | flops 151584768 | bytes 1577984 | tf_op jit(solution)/shard_map/dot_general | solution.py:313
  24.1 2.7 %collective-permute-done.9.refs_10_ = bf16[128,768]{1,0:T(8,128)(2,1)S(1)} collective-permute-done((bf16[128,768]{1,0:T(8,128)(2,1)S(1)}, bf16[128,768]{1,0:T(8,128)(2,1)S(1)}, u32[]{:S(2)}, u32[]{:S(2)}) %collective-permute-start.9) | collective-permute-done | bytes 196640 | tf_op jit(solution)/shard_map/ppermute | solution.py:277
  26.8 1.3 %collective-permute-start.14 = (bf16[128,768]{1,0:T(8,128)(2,1)S(1)}, bf16[128,768]{1,0:T(8,128)(2,1)S(1)}, u32[]{:S(2)}, u32[]{:S(2)}) collective-permute-start(bf16[128,768]{1,0:T(8,128)(2,1)S(1)} %collective-permute-done.13.refs_14_), channel_id=1, source_target_pairs={{0,1},{1,0},{2,3},{3,2},{4,5},{5,4},{6,7},{7,6},{8,9},{9,8},{10,11... | collective-permute-start | bytes 589832 | tf_op jit(solution)/shard_map/ppermute | solution.py:284
  28.0 2.9 %collective-permute-done.5.refs_6_ = bf16[128,768]{1,0:T(8,128)(2,1)S(1)} collective-permute-done((bf16[128,768]{1,0:T(8,128)(2,1)S(1)}, bf16[128,768]{1,0:T(8,128)(2,1)S(1)}, u32[]{:S(2)}, u32[]{:S(2)}) %collective-permute-start.5) | collective-permute-done | bytes 196640 | tf_op jit(solution)/shard_map/ppermute | solution.py:277
  32.9 16.2 %shard_map.86 = (bf16[128,768]{1,0:T(8,128)(2,1)S(1)}, bf16[128,768]{1,0:T(8,128)(2,1)S(1)}, f32[128,768]{1,0:T(8,128)S(1)}, bf16[64,768]{1,0:T(8,128)(2,1)S(1)}...) custom-call(s32[66]{0:T(128)S(1)} %pad_add_fusion.meta, ...), custom_call_target="tpu_custom_call" | custom-call | flops 8000000000 | bytes 5000000 | tf_op jit(solution)/shard_map/pallas_call | solution.py:175
  50.0 1.8 %collective-permute-start.17 = (bf16[128,768]{1,0:T(8,128)(2,1)S(1)}, bf16[128,768]{1,0:T(8,128)(2,1)S(1)}, u32[]{:S(2)}, u32[]{:S(2)}) collective-permute-start(bf16[128,768]{1,0:T(8,128)(2,1)S(1)} %get-tuple-element.27), channel_id=1, source_target_pairs={{4,0},{5,1},{6,2},{7,3},{0,4},{1,5},{2,6},{3,7},{12,8},{13,9},{14,... | collective-permute-start | bytes 589832 | tf_op jit(solution)/shard_map/ppermute | solution.py:277
  51.8 2.0 %collective-permute-start.18 = (bf16[128,768]{1,0:T(8,128)(2,1)S(1)}, bf16[128,768]{1,0:T(8,128)(2,1)S(1)}, u32[]{:S(2)}, u32[]{:S(2)}) collective-permute-start(bf16[128,768]{1,0:T(8,128)(2,1)S(1)} %get-tuple-element.28), channel_id=1, source_target_pairs={{6,0},{7,1},{4,2},{5,3},{2,4},{3,5},{0,6},{1,7},{14,8},{15,9},{12,... | collective-permute-start | bytes 589832 | tf_op jit(solution)/shard_map/ppermute | solution.py:277
  53.8 2.4 %collective-permute-start.19 = (bf16[128,768]{1,0:T(8,128)(2,1)S(1)}, bf16[128,768]{1,0:T(8,128)(2,1)S(1)}, u32[]{:S(2)}, u32[]{:S(2)}) collective-permute-start(bf16[128,768]{1,0:T(8,128)(2,1)S(1)} %get-tuple-element.29), channel_id=1, source_target_pairs={{8,2},{9,3},{12,6},{13,7},{2,8},{3,9},{6,12},{7,13},{24,18},{25,19... | collective-permute-start | bytes 589832 | tf_op jit(solution)/shard_map/ppermute | solution.py:277
  56.2 2.4 %collective-permute-done.15.came.refs_3_ = bf16[128,768]{1,0:T(8,128)(2,1)S(1)} collective-permute-done((bf16[128,768]{1,0:T(8,128)(2,1)S(1)}, bf16[128,768]{1,0:T(8,128)(2,1)S(1)}, u32[]{:S(2)}, u32[]{:S(2)}) %collective-permute-start.15) | collective-permute-done | bytes 196640 | tf_op jit(solution)/shard_map/ppermute | solution.py:277
  58.6 3.6 %collective-permute-start.20 = (bf16[128,768]{1,0:T(8,128)(2,1)S(1)}, bf16[128,768]{1,0:T(8,128)(2,1)S(1)}, u32[]{:S(2)}, u32[]{:S(2)}) collective-permute-start(bf16[128,768]{1,0:T(8,128)(2,1)S(1)} %get-tuple-element.30), channel_id=1, source_target_pairs={{8,4},{9,5},{10,6},{11,7},{4,8},{5,9},{6,10},{7,11},{24,20},{25,21... | collective-permute-start | bytes 589832 | tf_op jit(solution)/shard_map/ppermute | solution.py:277
  62.1 3.2 %shard_map.87 = (bf16[128,768]{1,0:T(8,128)(2,1)}, f32[2,64,768]{2,1,0:T(8,128)S(1)}) custom-call(s32[15]{0:T(128)S(1)} %and_select_fusion.parity, bf16[128,768]{1,0:T(8,128)(2,1)S(1)} %collective-permute-done.15.came.refs_3_, bf16[128,768]{1,0:T(8,128)(2,1)S(1)} %get-tuple-element.20.refs_0_, bf16[128,768]{1,0:T(8,128)(2,1)S(1)} %get-tuple-element.21.refs_1_, ...), custom_call_target="tpu_custom_call" | custom-call | bytes 5000000 | tf_op jit(solution)/shard_map/pallas_call | solution.py:222
  65.3 4.2 %collective-permute-start.21 = (bf16[128,768]{1,0:T(8,128)(2,1)S(1)}, bf16[128,768]{1,0:T(8,128)(2,1)S(1)}, u32[]{:S(2)}, u32[]{:S(2)}) collective-permute-start(bf16[128,768]{1,0:T(8,128)(2,1)S(1)} %get-tuple-element.31), channel_id=1, source_target_pairs={{10,4},{11,5},{8,6},{9,7},{6,8},{7,9},{4,10},{5,11},{26,20},{27,21... | collective-permute-start | bytes 589832 | tf_op jit(solution)/shard_map/ppermute | solution.py:277
  69.6 1.3 %collective-permute-start.25 = (bf16[128,768]{1,0:T(8,128)(2,1)S(1)}, bf16[128,768]{1,0:T(8,128)(2,1)S(1)}, u32[]{:S(2)}, u32[]{:S(2)}) collective-permute-start(bf16[128,768]{1,0:T(8,128)(2,1)S(1)} %collective-permute-done.15.came.refs_3_), channel_id=1, source_target_pairs={{0,1},{1,0},{2,3},{3,2},{4,5},{5,4},{6,7},{7,6},{8,9},{9,8},{10,11... | collective-permute-start | bytes 589832 | tf_op jit(solution)/shard_map/ppermute | solution.py:328
  71.4 1.3 %collective-permute-start.24 = (bf16[128,768]{1,0:T(8,128)(2,1)S(1)}, bf16[128,768]{1,0:T(8,128)(2,1)S(1)}, u32[]{:S(2)}, u32[]{:S(2)}) collective-permute-start(bf16[128,768]{1,0:T(8,128)(2,1)S(1)} %collective-permute-done.18.refs_2_), channel_id=1, source_target_pairs={{0,1},{1,0},{2,3},{3,2},{4,5},{5,4},{6,7},{7,6},{8,9},{9,8},{10,11... | collective-permute-start | bytes 589832 | tf_op jit(solution)/shard_map/ppermute | solution.py:328
  72.7 4.8 %collective-permute-done.21.refs_6_ = bf16[128,768]{1,0:T(8,128)(2,1)S(1)} collective-permute-done((bf16[128,768]{1,0:T(8,128)(2,1)S(1)}, bf16[128,768]{1,0:T(8,128)(2,1)S(1)}, u32[]{:S(2)}, u32[]{:S(2)}) %collective-permute-start.21) | collective-permute-done | bytes 196640 | tf_op jit(solution)/shard_map/ppermute | solution.py:277
  77.5 1.2 %collective-permute-start.26 = (bf16[128,768]{1,0:T(8,128)(2,1)S(1)}, bf16[128,768]{1,0:T(8,128)(2,1)S(1)}, u32[]{:S(2)}, u32[]{:S(2)}) collective-permute-start(bf16[128,768]{1,0:T(8,128)(2,1)S(1)} %collective-permute-done.19.refs_4_), channel_id=1, source_target_pairs={{0,1},{1,0},{2,3},{3,2},{4,5},{5,4},{6,7},{7,6},{8,9},{9,8},{10,11... | collective-permute-start | bytes 589832 | tf_op jit(solution)/shard_map/ppermute | solution.py:328
  79.2 1.8 %collective-permute-start.27 = (bf16[128,768]{1,0:T(8,128)(2,1)S(1)}, bf16[128,768]{1,0:T(8,128)(2,1)S(1)}, u32[]{:S(2)}, u32[]{:S(2)}) collective-permute-start(bf16[128,768]{1,0:T(8,128)(2,1)S(1)} %collective-permute-done.20.refs_5_), channel_id=1, source_target_pairs={{0,1},{1,0},{2,3},{3,2},{4,5},{5,4},{6,7},{7,6},{8,9},{9,8},{10,11... | collective-permute-start | bytes 589832 | tf_op jit(solution)/shard_map/ppermute | solution.py:328
  82.8 1.8 %shard_map.88 = bf16[128,768]{1,0:T(8,128)(2,1)} custom-call(s32[15]{0:T(128)S(1)} %and_select_fusion.parity, bf16[128,768]{1,0:T(8,128)(2,1)S(1)} %collective-permute-done.16.refs_0_, bf16[128,768]{1,0:T(8,128)(2,1)S(1)} %collective-permute-done.17.refs_1_, bf16[128,768]{1,0:T(8,128)(2,1)S(1)} %collective-permute-done.18.refs_2_, ...), custom_call_target="tpu_custom_call" | custom-call | bytes 5000000 | tf_op jit(solution)/shard_map/pallas_call | solution.py:257
  (71 shorter events, 13.9 us)
Async XLA Ops:
  0.6 13.4 %collective-permute-start.11 = (bf16[128,768]{1,0:T(8,128)(2,1)}, bf16[128,768]{1,0:T(8,128)(2,1)S(1)}, u32[]{:S(2)}, u32[]{:S(2)}) collective-permute-start(bf16[128,768]{1,0:T(8,128)(2,1)} %refs_16_.1), channel_id=1, source_target_pairs={{8,4},{9,5},{10,6},{11,7},{4,8},{5,9},{6,10},{7,11},{24,20},{25,21... | collective-permute-start | bytes 589832 | tf_op jit(solution)/shard_map/ppermute | solution.py:277
  3.8 13.5 %collective-permute-start.7 = (bf16[128,768]{1,0:T(8,128)(2,1)}, bf16[128,768]{1,0:T(8,128)(2,1)S(1)}, u32[]{:S(2)}, u32[]{:S(2)}) collective-permute-start(bf16[128,768]{1,0:T(8,128)(2,1)} %refs_16_.1), channel_id=1, source_target_pairs={{8,0},{9,1},{10,2},{11,3},{12,4},{13,5},{14,6},{15,7},{0,8},{1,9},... | collective-permute-start | bytes 589832 | tf_op jit(solution)/shard_map/ppermute | solution.py:277
  3.9 14.0 %collective-permute-start.3 = (bf16[128,768]{1,0:T(8,128)(2,1)}, bf16[128,768]{1,0:T(8,128)(2,1)S(1)}, u32[]{:S(2)}, u32[]{:S(2)}) collective-permute-start(bf16[128,768]{1,0:T(8,128)(2,1)} %refs_16_.1), channel_id=1, source_target_pairs={{4,0},{5,1},{6,2},{7,3},{0,4},{1,5},{2,6},{3,7},{12,8},{13,9},{14,... | collective-permute-start | bytes 589832 | tf_op jit(solution)/shard_map/ppermute | solution.py:277
  5.3 13.9 %collective-permute-start.1 = (bf16[128,768]{1,0:T(8,128)(2,1)}, bf16[128,768]{1,0:T(8,128)(2,1)S(1)}, u32[]{:S(2)}, u32[]{:S(2)}) collective-permute-start(bf16[128,768]{1,0:T(8,128)(2,1)} %refs_16_.1), channel_id=1, source_target_pairs={{2,0},{3,1},{0,2},{1,3},{6,4},{7,5},{4,6},{5,7},{10,8},{11,9},{8,1... | collective-permute-start | bytes 589832 | tf_op jit(solution)/shard_map/ppermute | solution.py:277
  5.5 13.8 %collective-permute-start = (bf16[128,768]{1,0:T(8,128)(2,1)}, bf16[128,768]{1,0:T(8,128)(2,1)S(1)}, u32[]{:S(2)}, u32[]{:S(2)}) collective-permute-start(bf16[128,768]{1,0:T(8,128)(2,1)} %refs_16_.1), channel_id=1, source_target_pairs={{0,1},{1,0},{2,3},{3,2},{4,5},{5,4},{6,7},{7,6},{8,9},{9,8},{10,11... | collective-permute-start | bytes 589832 | tf_op jit(solution)/shard_map/ppermute | solution.py:285
  14.0 9.4 %collective-permute-start.13 = (bf16[128,768]{1,0:T(8,128)(2,1)S(1)}, bf16[128,768]{1,0:T(8,128)(2,1)S(1)}, u32[]{:S(2)}, u32[]{:S(2)}) collective-permute-start(bf16[128,768]{1,0:T(8,128)(2,1)S(1)} %collective-permute-done.11.refs_12_), channel_id=1, source_target_pairs={{6,4},{7,5},{4,6},{5,7},{10,8},{11,9},{8,10},{9,11},{22,20},{23,21... | collective-permute-start | bytes 589832 | tf_op jit(solution)/shard_map/ppermute | solution.py:277
  17.3 6.7 %collective-permute-start.12 = (bf16[128,768]{1,0:T(8,128)(2,1)S(1)}, bf16[128,768]{1,0:T(8,128)(2,1)S(1)}, u32[]{:S(2)}, u32[]{:S(2)}) collective-permute-start(bf16[128,768]{1,0:T(8,128)(2,1)S(1)} %collective-permute-done.11.refs_12_), channel_id=1, source_target_pairs={{0,1},{1,0},{2,3},{3,2},{4,5},{5,4},{6,7},{7,6},{8,9},{9,8},{10,11... | collective-permute-start | bytes 589832 | tf_op jit(solution)/shard_map/ppermute | solution.py:284
  17.9 8.9 %collective-permute-start.9 = (bf16[128,768]{1,0:T(8,128)(2,1)S(1)}, bf16[128,768]{1,0:T(8,128)(2,1)S(1)}, u32[]{:S(2)}, u32[]{:S(2)}) collective-permute-start(bf16[128,768]{1,0:T(8,128)(2,1)S(1)} %collective-permute-done.7.refs_8_), channel_id=1, source_target_pairs={{0,2},{1,3},{4,6},{5,7},{10,8},{11,9},{14,12},{15,13},{16,18},{17,... | collective-permute-start | bytes 589832 | tf_op jit(solution)/shard_map/ppermute | solution.py:277
  19.2 8.8 %collective-permute-start.8 = (bf16[128,768]{1,0:T(8,128)(2,1)S(1)}, bf16[128,768]{1,0:T(8,128)(2,1)S(1)}, u32[]{:S(2)}, u32[]{:S(2)}) collective-permute-start(bf16[128,768]{1,0:T(8,128)(2,1)S(1)} %collective-permute-done.7.refs_8_), channel_id=1, source_target_pairs={{0,1},{1,0},{2,3},{3,2},{4,5},{5,4},{6,7},{7,6},{8,9},{9,8},{10,11... | collective-permute-start | bytes 589832 | tf_op jit(solution)/shard_map/ppermute | solution.py:284
  19.3 11.7 %collective-permute-start.5 = (bf16[128,768]{1,0:T(8,128)(2,1)S(1)}, bf16[128,768]{1,0:T(8,128)(2,1)S(1)}, u32[]{:S(2)}, u32[]{:S(2)}) collective-permute-start(bf16[128,768]{1,0:T(8,128)(2,1)S(1)} %collective-permute-done.3.refs_4_), channel_id=1, source_target_pairs={{2,0},{3,1},{0,2},{1,3},{6,4},{7,5},{4,6},{5,7},{10,8},{11,9},{8,1... | collective-permute-start | bytes 589832 | tf_op jit(solution)/shard_map/ppermute | solution.py:277
  23.5 8.9 %collective-permute-start.4 = (bf16[128,768]{1,0:T(8,128)(2,1)S(1)}, bf16[128,768]{1,0:T(8,128)(2,1)S(1)}, u32[]{:S(2)}, u32[]{:S(2)}) collective-permute-start(bf16[128,768]{1,0:T(8,128)(2,1)S(1)} %collective-permute-done.3.refs_4_), channel_id=1, source_target_pairs={{0,1},{1,0},{2,3},{3,2},{4,5},{5,4},{6,7},{7,6},{8,9},{9,8},{10,11... | collective-permute-start | bytes 589832 | tf_op jit(solution)/shard_map/ppermute | solution.py:284
  24.0 8.4 %collective-permute-start.2 = (bf16[128,768]{1,0:T(8,128)(2,1)S(1)}, bf16[128,768]{1,0:T(8,128)(2,1)S(1)}, u32[]{:S(2)}, u32[]{:S(2)}) collective-permute-start(bf16[128,768]{1,0:T(8,128)(2,1)S(1)} %collective-permute-done.1.refs_2_), channel_id=1, source_target_pairs={{0,1},{1,0},{2,3},{3,2},{4,5},{5,4},{6,7},{7,6},{8,9},{9,8},{10,11... | collective-permute-start | bytes 589832 | tf_op jit(solution)/shard_map/ppermute | solution.py:284
  26.8 5.6 %collective-permute-start.14 = (bf16[128,768]{1,0:T(8,128)(2,1)S(1)}, bf16[128,768]{1,0:T(8,128)(2,1)S(1)}, u32[]{:S(2)}, u32[]{:S(2)}) collective-permute-start(bf16[128,768]{1,0:T(8,128)(2,1)S(1)} %collective-permute-done.13.refs_14_), channel_id=1, source_target_pairs={{0,1},{1,0},{2,3},{3,2},{4,5},{5,4},{6,7},{7,6},{8,9},{9,8},{10,11... | collective-permute-start | bytes 589832 | tf_op jit(solution)/shard_map/ppermute | solution.py:284
  49.1 16.2 %collective-permute-start.29 = (bf16[64,768]{1,0:T(8,128)(2,1)S(1)}, bf16[64,768]{1,0:T(8,128)(2,1)S(1)}, u32[]{:S(2)}, u32[]{:S(2)}) collective-permute-start(bf16[64,768]{1,0:T(8,128)(2,1)S(1)} %get-tuple-element.32), channel_id=1, source_target_pairs={{0,1},{1,0},{2,3},{3,2},{4,5},{5,4},{6,7},{7,6},{8,9},{9,8},{10,11... | collective-permute-start | bytes 294920 | tf_op jit(solution)/shard_map/ppermute | solution.py:317
  49.5 9.0 %collective-permute-start.15 = (bf16[128,768]{1,0:T(8,128)(2,1)S(1)}, bf16[128,768]{1,0:T(8,128)(2,1)S(1)}, u32[]{:S(2)}, u32[]{:S(2)}) collective-permute-start(bf16[128,768]{1,0:T(8,128)(2,1)S(1)} %get-tuple-element.19), channel_id=1, source_target_pairs={{8,0},{9,1},{10,2},{11,3},{12,4},{13,5},{14,6},{15,7},{0,8},{1,9},... | collective-permute-start | bytes 589832 | tf_op jit(solution)/shard_map/ppermute | solution.py:277
  50.0 19.4 %collective-permute-start.17 = (bf16[128,768]{1,0:T(8,128)(2,1)S(1)}, bf16[128,768]{1,0:T(8,128)(2,1)S(1)}, u32[]{:S(2)}, u32[]{:S(2)}) collective-permute-start(bf16[128,768]{1,0:T(8,128)(2,1)S(1)} %get-tuple-element.27), channel_id=1, source_target_pairs={{4,0},{5,1},{6,2},{7,3},{0,4},{1,5},{2,6},{3,7},{12,8},{13,9},{14,... | collective-permute-start | bytes 589832 | tf_op jit(solution)/shard_map/ppermute | solution.py:277
  51.8 17.7 %collective-permute-start.18 = (bf16[128,768]{1,0:T(8,128)(2,1)S(1)}, bf16[128,768]{1,0:T(8,128)(2,1)S(1)}, u32[]{:S(2)}, u32[]{:S(2)}) collective-permute-start(bf16[128,768]{1,0:T(8,128)(2,1)S(1)} %get-tuple-element.28), channel_id=1, source_target_pairs={{6,0},{7,1},{4,2},{5,3},{2,4},{3,5},{0,6},{1,7},{14,8},{15,9},{12,... | collective-permute-start | bytes 589832 | tf_op jit(solution)/shard_map/ppermute | solution.py:277
  53.8 17.1 %collective-permute-start.19 = (bf16[128,768]{1,0:T(8,128)(2,1)S(1)}, bf16[128,768]{1,0:T(8,128)(2,1)S(1)}, u32[]{:S(2)}, u32[]{:S(2)}) collective-permute-start(bf16[128,768]{1,0:T(8,128)(2,1)S(1)} %get-tuple-element.29), channel_id=1, source_target_pairs={{8,2},{9,3},{12,6},{13,7},{2,8},{3,9},{6,12},{7,13},{24,18},{25,19... | collective-permute-start | bytes 589832 | tf_op jit(solution)/shard_map/ppermute | solution.py:277
  58.6 12.8 %collective-permute-start.20 = (bf16[128,768]{1,0:T(8,128)(2,1)S(1)}, bf16[128,768]{1,0:T(8,128)(2,1)S(1)}, u32[]{:S(2)}, u32[]{:S(2)}) collective-permute-start(bf16[128,768]{1,0:T(8,128)(2,1)S(1)} %get-tuple-element.30), channel_id=1, source_target_pairs={{8,4},{9,5},{10,6},{11,7},{4,8},{5,9},{6,10},{7,11},{24,20},{25,21... | collective-permute-start | bytes 589832 | tf_op jit(solution)/shard_map/ppermute | solution.py:277
  65.3 12.2 %collective-permute-start.21 = (bf16[128,768]{1,0:T(8,128)(2,1)S(1)}, bf16[128,768]{1,0:T(8,128)(2,1)S(1)}, u32[]{:S(2)}, u32[]{:S(2)}) collective-permute-start(bf16[128,768]{1,0:T(8,128)(2,1)S(1)} %get-tuple-element.31), channel_id=1, source_target_pairs={{10,4},{11,5},{8,6},{9,7},{6,8},{7,9},{4,10},{5,11},{26,20},{27,21... | collective-permute-start | bytes 589832 | tf_op jit(solution)/shard_map/ppermute | solution.py:277
  69.5 9.8 %collective-permute-start.16 = (bf16[128,768]{1,0:T(8,128)(2,1)S(1)}, bf16[128,768]{1,0:T(8,128)(2,1)S(1)}, u32[]{:S(2)}, u32[]{:S(2)}) collective-permute-start(bf16[128,768]{1,0:T(8,128)(2,1)S(1)} %get-tuple-element.26), channel_id=1, source_target_pairs={{2,0},{3,1},{0,2},{1,3},{6,4},{7,5},{4,6},{5,7},{10,8},{11,9},{8,1... | collective-permute-start | bytes 589832 | tf_op jit(solution)/shard_map/ppermute | solution.py:277
  69.6 11.5 %collective-permute-start.25 = (bf16[128,768]{1,0:T(8,128)(2,1)S(1)}, bf16[128,768]{1,0:T(8,128)(2,1)S(1)}, u32[]{:S(2)}, u32[]{:S(2)}) collective-permute-start(bf16[128,768]{1,0:T(8,128)(2,1)S(1)} %collective-permute-done.15.came.refs_3_), channel_id=1, source_target_pairs={{0,1},{1,0},{2,3},{3,2},{4,5},{5,4},{6,7},{7,6},{8,9},{9,8},{10,11... | collective-permute-start | bytes 589832 | tf_op jit(solution)/shard_map/ppermute | solution.py:328
  70.9 10.2 %collective-permute-start.23 = (bf16[128,768]{1,0:T(8,128)(2,1)S(1)}, bf16[128,768]{1,0:T(8,128)(2,1)S(1)}, u32[]{:S(2)}, u32[]{:S(2)}) collective-permute-start(bf16[128,768]{1,0:T(8,128)(2,1)S(1)} %collective-permute-done.17.refs_1_), channel_id=1, source_target_pairs={{0,1},{1,0},{2,3},{3,2},{4,5},{5,4},{6,7},{7,6},{8,9},{9,8},{10,11... | collective-permute-start | bytes 589832 | tf_op jit(solution)/shard_map/ppermute | solution.py:328
  71.4 10.2 %collective-permute-start.24 = (bf16[128,768]{1,0:T(8,128)(2,1)S(1)}, bf16[128,768]{1,0:T(8,128)(2,1)S(1)}, u32[]{:S(2)}, u32[]{:S(2)}) collective-permute-start(bf16[128,768]{1,0:T(8,128)(2,1)S(1)} %collective-permute-done.18.refs_2_), channel_id=1, source_target_pairs={{0,1},{1,0},{2,3},{3,2},{4,5},{5,4},{6,7},{7,6},{8,9},{9,8},{10,11... | collective-permute-start | bytes 589832 | tf_op jit(solution)/shard_map/ppermute | solution.py:328
  (9 other events, 61.8 us)

commit v3 on v2

--- a/solution.py
+++ b/solution.py
@@ -11,6 +11,7 @@
 BLK = 64
 MAXNB = 8
 HALF = 8
+PACK = 4
 REACH = (HALF + 1) // 2
 F32 = jnp.float32
 BF16 = jnp.bfloat16
@@ -30,7 +31,7 @@
             relay = m in (3, 5, 7)
             fetch = [(k, k ^ 1) for k, _ in pairs] if relay else pairs
             rounds.append(Round(fetch, (m ^ 1) - 1 if relay else None, pairs, lambda k, m=m: k ^ m))
-        return rounds, [5, 1, 3, 0, 2, 6, 4], [3, 5, 4, 6, 2, 1, 0]
+        return rounds, [5, 0, 3, 1, 2, 6, 4], [3, 1, 0, 4, 2, 5, 6]
     rounds = []
     for d in range(-REACH, REACH + 1):
         if d != 0:
@@ -72,7 +73,6 @@
 SMEM = pl.BlockSpec(memory_space=pltpu.SMEM)
 VMEM = pl.BlockSpec(memory_space=pltpu.VMEM)
 ANY = pl.BlockSpec(memory_space=pl.ANY)
-HBM = pl.BlockSpec(memory_space=pltpu.HBM)
 
 
 def weight_copies(source, target, sems):
@@ -89,13 +89,13 @@
     ]
 
 
-def main_kernel(rounds, meta, *refs):
-    count = 2 * (rounds + 1)
+def main_kernel(rounds, places, meta, *refs):
+    count = len(places)
     windows = refs[:count]
     q_ref, g_ref, gain_ref, w_hbm = refs[count : count + 4]
     att_ref, dq_ref, own_ref, sib_ref = refs[count + 4 : count + 8]
     msg_refs = refs[count + 8 : count + 8 + rounds]
-    normed, kv, kvt, acc, stage, w, msems, wsems = refs[count + 8 + rounds :]
+    normed, kv, kvt, acc, w, wsems = refs[count + 8 + rounds :]
     width = q_ref.shape[1]
     wcopies = weight_copies(w_hbm, w, wsems)
     for c in wcopies:
@@ -104,13 +104,13 @@
     span = MAXNB * BLK
 
     gain = gain_ref[...]
-    for i in range(count):
+    for ref, place in zip(windows, places):
         for j in range(2):
 
-            @pl.when(meta[2 * slots + 2 + 2 * i + j] != 0)
+            @pl.when(meta[2 * slots + 2 + 2 * place + j] != 0)
             def _():
-                unit, _ = layer_norm(windows[i][j * BLK : (j + 1) * BLK, :].astype(F32))
-                normed[2 * i + j] = (unit * gain).astype(BF16)
+                unit, _ = layer_norm(ref[j * BLK : (j + 1) * BLK, :].astype(F32))
+                normed[2 * place + j] = (unit * gain).astype(BF16)
 
     for c in wcopies:
         c.wait()
@@ -120,21 +120,28 @@
         kv[pl.ds(i * rows, rows), :] = dot(part, w[...], 1, 0).astype(BF16)
     acc[...] = jnp.zeros_like(acc)
 
-    lane = lax.broadcasted_iota(jnp.int32, (1, 2 * HD), 1)
-    low = (lane < HD).astype(F32)
-    high = 1.0 - low
+    group = PACK * HD
+    lane = lax.broadcasted_iota(jnp.int32, (1, group), 1)
+    masks = [(lane // HD == h).astype(BF16) for h in range(PACK)]
     slot_row = lax.broadcasted_iota(jnp.int32, (span, 1), 0)
+
+    def diagonal(x):
+        out = x[:BLK]
+        for h in range(1, PACK):
+            out = jnp.where(lane < h * HD, out, x[h * BLK : (h + 1) * BLK])
+        return out
+
     for b in range(2):
         live = slot_row < meta[2 * slots + b] * BLK
-        for p in range(width // (2 * HD)):
-            lanes = pl.ds(p * 2 * HD, 2 * HD)
-            vlanes = pl.ds(width + p * 2 * HD, 2 * HD)
+        for p in range(width // group):
+            lanes = pl.ds(p * group, group)
+            vlanes = pl.ds(width + p * group, group)
             tok = pl.ds(b * BLK, BLK)
             krows = pl.ds(b * span, span)
-            q = q_ref[tok, lanes].astype(F32) * 0.125
-            g = g_ref[tok, lanes].astype(F32)
-            qd = jnp.concatenate([q * low, q * high], axis=0).astype(BF16)
-            gd = jnp.concatenate([g * low, g * high], axis=0).astype(BF16)
+            q = q_ref[tok, lanes] * 0.125
+            g = g_ref[tok, lanes]
+            qd = jnp.concatenate([q * m for m in masks], axis=0)
+            gd = jnp.concatenate([g * m for m in masks], axis=0)
             k = kv[krows, lanes]
             v = kv[krows, vlanes]
             scores = jnp.where(live, dot(k, qd, 1, 1), -1e30)
@@ -146,10 +153,8 @@
             sg = (prob * (pg - row_dot)).astype(BF16)
             kvt[krows, lanes] = dot(sg, qd, 1, 0).astype(BF16)
             kvt[krows, vlanes] = dot(low_prob, gd, 1, 0).astype(BF16)
-            att = dot(low_prob, v, 0, 0)
-            dq = dot(sg, k, 0, 0) * 0.125
-            att_ref[tok, lanes] = jnp.where(lane < HD, att[:BLK], att[BLK:]).astype(BF16)
-            dq_ref[tok, lanes] = jnp.where(lane < HD, dq[:BLK], dq[BLK:]).astype(BF16)
+            att_ref[tok, lanes] = diagonal(dot(low_prob, v, 0, 0)).astype(BF16)
+            dq_ref[tok, lanes] = (diagonal(dot(sg, k, 0, 0)) * 0.125).astype(BF16)
 
     for i in range(slots * BLK // rows):
         part = dot(kvt[pl.ds(i * rows, rows), :], w[...], 1, 1)
@@ -157,36 +162,31 @@
             at = meta[slots + i * (rows // BLK) + j]
             acc[at] = acc[at] + part[j * BLK : (j + 1) * BLK, :]
     for r in range(rounds):
-        stage[r, 0:BLK, :] = acc[3 + 2 * r].astype(BF16)
-        stage[r, BLK : 2 * BLK, :] = acc[4 + 2 * r].astype(BF16)
-        pltpu.make_async_copy(stage.at[r], msg_refs[r], msems.at[r]).start()
+        msg_refs[r][0:BLK, :] = acc[3 + 2 * r].astype(BF16)
+        msg_refs[r][BLK : 2 * BLK, :] = acc[4 + 2 * r].astype(BF16)
     own_ref[0:BLK, :] = acc[0]
     own_ref[BLK : 2 * BLK, :] = acc[1]
     sib_ref[...] = acc[2].astype(BF16)
-    for r in range(rounds):
-        pltpu.make_async_copy(stage.at[r], msg_refs[r], msems.at[r]).wait()
-
-
-def main_call(meta, windows, queries, grads, gain, w_qkv):
+
+
+def main_call(meta, places, windows, queries, grads, gain, w_qkv):
     rounds = len(windows) // 2 - 1
     tokens, width = queries.shape
     slots = 2 * MAXNB
     shape = jax.ShapeDtypeStruct
     return call(
-        functools.partial(main_kernel, rounds),
+        functools.partial(main_kernel, rounds, places),
         [shape((tokens, width), BF16)] * 2
         + [shape((tokens, width), F32), shape((BLK, width), BF16)]
         + [shape((2 * BLK, width), BF16)] * rounds,
         [SMEM] + [VMEM] * (len(windows) + 3) + [ANY],
-        [VMEM] * 4 + [HBM] * rounds,
+        [VMEM] * (4 + rounds),
         [
             pltpu.VMEM((2 * len(windows), BLK, width), BF16),
             pltpu.VMEM((slots * BLK, 2 * width), BF16),
             pltpu.VMEM((slots * BLK, 2 * width), BF16),
             pltpu.VMEM((4 + 2 * rounds, BLK, width), F32),
-            pltpu.VMEM((rounds, 2 * BLK, width), BF16),
             pltpu.VMEM((width, 2 * width), BF16),
-            pltpu.SemaphoreType.DMA((rounds,)),
             pltpu.SemaphoreType.DMA((6,)),
         ],
         48,
@@ -229,8 +229,9 @@
     )(parity, came, attended, query_grad, own, tokens, w_qkv, w_out)
 
 
-def final_kernel(rounds, done, parity, *refs):
-    came, sibs = refs[:rounds], refs[rounds : 2 * rounds]
+def final_kernel(order, done, parity, *refs):
+    rounds = len(order)
+    came, sibs = dict(zip(order, refs[:rounds])), dict(zip(order, refs[rounds : 2 * rounds]))
     sib, base, tok_ref, cot_ref, gain_ref, out_ref, total = refs[2 * rounds :]
     total[...] = base[...]
     add_came(total, sib, parity[0], pl.ds(0, BLK))
@@ -251,17 +252,17 @@
         out_ref[rows, :] = (cot_ref[rows, :].astype(F32) + inv_std * centered).astype(BF16)
 
 
-def final_call(done, parity, came, sibs, sib, base, tokens, cotangent, gain):
+def final_call(order, done, parity, came, sibs, sib, base, tokens, cotangent, gain):
     rounds = len(came)
     count, width = tokens.shape
     return call(
-        functools.partial(final_kernel, rounds, done),
+        functools.partial(final_kernel, order, done),
         jax.ShapeDtypeStruct((count, width), BF16),
         [SMEM] + [VMEM] * (2 * rounds + 5),
         VMEM,
         [pltpu.VMEM((2, BLK, width), F32)],
         8,
-    )(parity, *came, *sibs, sib, base, tokens, cotangent, gain)
+    )(parity, *[came[r] for r in order], *[sibs[r] for r in order], sib, base, tokens, cotangent, gain)
 
 
 def per_device(tokens, gain, w_qkv, w_out, nbr_list, nbr_count, cotangent):
@@ -282,9 +283,17 @@
         arrived[r] = send(tokens if source is None else arrived[source], plan[r].fetch)
     for r in fetch_order:
         passed[r] = lax.ppermute(arrived[r], "seq", mate)
-    windows = [tokens, lax.ppermute(tokens, "seq", mate)]
-    for r in range(rounds):
-        windows += [arrived[r], passed[r]]
+    direct = [r for r in fetch_order if plan[r].source is None]
+    relayed = [r for r in fetch_order if plan[r].source is not None]
+    windows, places = [tokens], [0]
+    for some in (direct, relayed):
+        windows += [arrived[r] for r in some]
+        places += [2 * (r + 1) for r in some]
+        if some is direct:
+            windows.append(lax.ppermute(tokens, "seq", mate))
+            places.append(1)
+        windows += [passed[r] for r in some]
+        places += [2 * (r + 1) + 1 for r in some]
 
     position = lax.axis_index("seq")
     chip, core = position // 2, position % 2
@@ -312,9 +321,8 @@
     normed = (unit * gain).astype(BF16)
     queries = jnp.dot(normed, w_qkv[:, :width], preferred_element_type=F32).astype(BF16)
     out_grad = dot(cotangent, w_out, 1, 1).astype(BF16)
-    attended, query_grad, own, sib, *messages = main_call(meta, windows, queries, out_grad, gain, w_qkv)
-
-    sib = lax.ppermute(sib, "seq", mate)
+    attended, query_grad, own, sib, *messages = main_call(meta, places, windows, queries, out_grad, gain, w_qkv)
+
     came, sibs = [None] * rounds, [None] * rounds
     first, last = give_order[0], give_order[-1]
     for r in give_order:
@@ -324,9 +332,11 @@
             )
             messages[r], layer_out, base = lax.optimization_barrier((messages[r], layer_out, base))
         came[r] = send(messages[r], plan[r].give)
+    came[first], sib = lax.optimization_barrier((came[first], sib))
+    sib = lax.ppermute(sib, "seq", mate)
     for r in give_order:
         sibs[r] = lax.ppermute(came[r], "seq", mate)
-    token_grad = final_call(first, parity, came, sibs, sib, base, tokens, cotangent, gain)
+    token_grad = final_call(give_order, first, parity, came, sibs, sib, base, tokens, cotangent, gain)
     return (layer_out, token_grad)
 
 

time: 84.8 us -> 75.2 us (0.89)
  starting transfers between devices: 38.5 us -> 30.6 us
  Pallas kernels: 21.1 us -> 18.3 us
    ppermute x14, starting transfers between devices: 26.2 us -> 21.8 us  [send(): lax.ppermute(x, 'seq', [(2 * s + c, 2 * r + c) for r, s in pairs for c in...]
    ppermute x7, starting transfers between devices: 6.7 us -> 3.35 us  [per_device(): sibs[r] = lax.ppermute(came[r], 'seq', mate)]
    pallas_call x2, Pallas kernels: 18 us -> 15.1 us  [the longest x1 13.3 us: main_call(): call(functools.partial(main_kernel, rounds, places), [shape((tokens, widt...]
    ppermute x1, starting transfers between devices: 1.8 us -> 0.74 us  [per_device(): windows.append(lax.ppermute(tokens, 'seq', mate))]
  transfers between devices with their start and end apart: 30 -> 30, of which waited for: 9 -> 10; matrix products, arithmetic and copies ran while one was open for 11% -> 12% of each run, Pallas kernels for 4% -> 4%
where the time goes in v3:
time: 75.2 us; the launch traced here: 74.5 us
  starting transfers between devices  30.6 us (41%)
  Pallas kernels  18.3 us (24%)
  waiting for transfers between devices  15.7 us (21%)
  other arithmetic  3.98 us (5%)
  local copies, waits for them, and re-layouts  2.73 us (4%)
  matrix products  2.31 us (3%)
  between operations  0.94 us (1%)
    ppermute x14, starting transfers between devices, send(): lax.ppermute(x, 'seq', [(2 * s + c, 2 * r + c) for r, s in pairs for c in...  21.8 us
    ppermute x14, waiting for transfers between devices, send(): lax.ppermute(x, 'seq', [(2 * s + c, 2 * r + c) for r, s in pairs for c in...  13.8 us
    pallas_call x1, Pallas kernels, main_call(): call(functools.partial(main_kernel, rounds, places), [shape((tokens, widt...  13.3 us
    ppermute x7, starting transfers between devices, per_device(): passed[r] = lax.ppermute(arrived[r], 'seq', mate)  4.18 us
    ppermute x7, starting transfers between devices, per_device(): sibs[r] = lax.ppermute(came[r], 'seq', mate)  3.35 us
    pallas_call x1, Pallas kernels, middle_call(): call(functools.partial(middle_kernel, rows_of), [jax.ShapeDtypeStruct((co...  3.17 us
    dot_general x1, matrix products, per_device(): jnp.dot(normed, w_qkv[:, :width], preferred_element_type=F32).astype(BF16)  1.77 us
    pallas_call x1, Pallas kernels, final_call(): call(functools.partial(final_kernel, order, done), jax.ShapeDtypeStruct((...  1.76 us
  transfers between devices with their start and end apart: 30, of which 10 were waited for; matrix products, arithmetic and copies ran while one was open for 12% of the time, Pallas kernels for 4%

profile of v3, /device:TPU:13, one launch (start us, length us, event | category | flops | bytes accessed | tf_op | source)
XLA Modules:
  0.0 74.5 jit_solution(4833503331839366074)
XLA Ops:
  1.6 2.3 %collective-permute-start.2 = (bf16[128,768]{1,0:T(8,128)(2,1)}, bf16[128,768]{1,0:T(8,128)(2,1)S(1)}, u32[]{:S(2)}, u32[]{:S(2)}) collective-permute-start(bf16[128,768]{1,0:T(8,128)(2,1)} %refs_16_.1), channel_id=1, source_target_pairs={{8,0},{9,1},{10,2},{11,3},{12,4},{13,5},{14,6},{15,7},{0,8},{1,9},... | collective-permute-start | bytes 589832 | tf_op jit(solution)/shard_map/ppermute | solution.py:278
  4.1 2.1 %collective-permute-start = (bf16[128,768]{1,0:T(8,128)(2,1)}, bf16[128,768]{1,0:T(8,128)(2,1)S(1)}, u32[]{:S(2)}, u32[]{:S(2)}) collective-permute-start(bf16[128,768]{1,0:T(8,128)(2,1)} %refs_16_.1), channel_id=1, source_target_pairs={{8,4},{9,5},{10,6},{11,7},{4,8},{5,9},{6,10},{7,11},{24,20},{25,21... | collective-permute-start | bytes 589832 | tf_op jit(solution)/shard_map/ppermute | solution.py:278
  6.2 1.0 %convert_reduce_fusion = f32[128]{0:T(128)S(1)} fusion(bf16[128,768]{1,0:T(8,128)(2,1)} %refs_16_.1), kind=kLoop, calls=%fused_computation.6 | loop fusion | flops 196480 | bytes 197120 | tf_op jit(solution)/shard_map/reduce_sum | solution.py:51
  7.3 1.1 %fusion.7 = f32[128]{0:T(128)S(1)} fusion(bf16[128,768]{1,0:T(8,128)(2,1)} %refs_16_.1, f32[128]{0:T(128)S(1)} %broadcast_multiply_fusion), kind=kLoop, calls=%fused_computation.9 | loop fusion | flops 393088 | bytes 197632 | tf_op jit(solution)/shard_map/reduce_sum | solution.py:52
  13.0 1.3 %collective-permute-start.9 = (bf16[128,768]{1,0:T(8,128)(2,1)S(1)}, bf16[128,768]{1,0:T(8,128)(2,1)S(1)}, u32[]{:S(2)}, u32[]{:S(2)}) collective-permute-start(bf16[128,768]{1,0:T(8,128)(2,1)S(1)} %collective-permute-done.3.refs_4_), channel_id=1, source_target_pairs={{2,0},{3,1},{0,2},{1,3},{6,4},{7,5},{4,6},{5,7},{10,8},{11,9},{8,1... | collective-permute-start | bytes 589832 | tf_op jit(solution)/shard_map/ppermute | solution.py:278
  14.3 1.5 %collective-permute-start.8 = (bf16[128,768]{1,0:T(8,128)(2,1)S(1)}, bf16[128,768]{1,0:T(8,128)(2,1)S(1)}, u32[]{:S(2)}, u32[]{:S(2)}) collective-permute-start(bf16[128,768]{1,0:T(8,128)(2,1)S(1)} %collective-permute-done.3.refs_4_), channel_id=1, source_target_pairs={{0,1},{1,0},{2,3},{3,2},{4,5},{5,4},{6,7},{7,6},{8,9},{9,8},{10,11... | collective-permute-start | bytes 589832 | tf_op jit(solution)/shard_map/ppermute | solution.py:285
  15.8 1.3 %collective-permute-start.11 = (bf16[128,768]{1,0:T(8,128)(2,1)S(1)}, bf16[128,768]{1,0:T(8,128)(2,1)S(1)}, u32[]{:S(2)}, u32[]{:S(2)}) collective-permute-start(bf16[128,768]{1,0:T(8,128)(2,1)S(1)} %collective-permute-done.2.refs_3_), channel_id=1, source_target_pairs={{0,2},{1,3},{4,6},{5,7},{10,8},{11,9},{14,12},{15,13},{16,18},{17,... | collective-permute-start | bytes 589832 | tf_op jit(solution)/shard_map/ppermute | solution.py:278
  17.4 4.0 %collective-permute-start.10 = (bf16[128,768]{1,0:T(8,128)(2,1)S(1)}, bf16[128,768]{1,0:T(8,128)(2,1)S(1)}, u32[]{:S(2)}, u32[]{:S(2)}) collective-permute-start(bf16[128,768]{1,0:T(8,128)(2,1)S(1)} %collective-permute-done.refs_1_), channel_id=1, source_target_pairs={{6,4},{7,5},{4,6},{5,7},{10,8},{11,9},{8,10},{9,11},{22,20},{23,21... | collective-permute-start | bytes 589832 | tf_op jit(solution)/shard_map/ppermute | solution.py:278
  21.4 1.8 %fusion.2.refs_16_ = bf16[128,768]{1,0:T(8,128)(2,1)S(1)} fusion(bf16[768,2304]{1,0:T(8,128)(2,1)} %refs_4_.1, bf16[128,768]{1,0:T(8,128)(2,1)} %refs_16_.1, f32[768]{0:T(1024)} %param.8, f32[128]{0:T(128)S(1)} %add_rsqrt_fusion, f32[128]{0:T(128)S(1)} %broadcast_multiply_fusion), kind=kOutput, calls=%fused_computation.3 | convolution fusion | flops 151584768 | bytes 1577984 | tf_op jit(solution)/shard_map/dot_general | solution.py:322
  24.2 1.2 %collective-permute-start.12 = (bf16[128,768]{1,0:T(8,128)(2,1)S(1)}, bf16[128,768]{1,0:T(8,128)(2,1)S(1)}, u32[]{:S(2)}, u32[]{:S(2)}) collective-permute-start(bf16[128,768]{1,0:T(8,128)(2,1)S(1)} %collective-permute-done.9.refs_10_), channel_id=1, source_target_pairs={{0,1},{1,0},{2,3},{3,2},{4,5},{5,4},{6,7},{7,6},{8,9},{9,8},{10,11... | collective-permute-start | bytes 589832 | tf_op jit(solution)/shard_map/ppermute | solution.py:285
  25.4 3.0 %collective-permute-done.10.refs_11_ = bf16[128,768]{1,0:T(8,128)(2,1)S(1)} collective-permute-done((bf16[128,768]{1,0:T(8,128)(2,1)S(1)}, bf16[128,768]{1,0:T(8,128)(2,1)S(1)}, u32[]{:S(2)}, u32[]{:S(2)}) %collective-permute-start.10) | collective-permute-done | bytes 196640 | tf_op jit(solution)/shard_map/ppermute | solution.py:278
  28.4 0.8 %collective-permute-start.13 = (bf16[128,768]{1,0:T(8,128)(2,1)S(1)}, bf16[128,768]{1,0:T(8,128)(2,1)S(1)}, u32[]{:S(2)}, u32[]{:S(2)}) collective-permute-start(bf16[128,768]{1,0:T(8,128)(2,1)S(1)} %collective-permute-done.10.refs_11_), channel_id=1, source_target_pairs={{0,1},{1,0},{2,3},{3,2},{4,5},{5,4},{6,7},{7,6},{8,9},{9,8},{10,11... | collective-permute-start | bytes 589832 | tf_op jit(solution)/shard_map/ppermute | solution.py:285
  30.2 13.3 %shard_map.86 = (bf16[128,768]{1,0:T(8,128)(2,1)S(1)}, bf16[128,768]{1,0:T(8,128)(2,1)S(1)}, f32[128,768]{1,0:T(8,128)S(1)}, bf16[64,768]{1,0:T(8,128)(2,1)S(1)}...) custom-call(s32[66]{0:T(128)S(1)} %pad_add_fusion.meta, ...), custom_call_target="tpu_custom_call" | custom-call | flops 8000000000 | bytes 5000000 | tf_op jit(solution)/shard_map/pallas_call | solution.py:177
  44.4 2.4 %collective-permute-start.17 = (bf16[128,768]{1,0:T(8,128)(2,1)S(1)}, bf16[128,768]{1,0:T(8,128)(2,1)S(1)}, u32[]{:S(2)}, u32[]{:S(2)}) collective-permute-start(bf16[128,768]{1,0:T(8,128)(2,1)S(1)} %get-tuple-element.31), channel_id=1, source_target_pairs={{2,0},{3,1},{0,2},{1,3},{6,4},{7,5},{4,6},{5,7},{10,8},{11,9},{8,1... | collective-permute-start | bytes 589832 | tf_op jit(solution)/shard_map/ppermute | solution.py:278
  46.8 2.3 %collective-permute-start.18 = (bf16[128,768]{1,0:T(8,128)(2,1)S(1)}, bf16[128,768]{1,0:T(8,128)(2,1)S(1)}, u32[]{:S(2)}, u32[]{:S(2)}) collective-permute-start(bf16[128,768]{1,0:T(8,128)(2,1)S(1)} %get-tuple-element.32), channel_id=1, source_target_pairs={{8,2},{9,3},{12,6},{13,7},{2,8},{3,9},{6,12},{7,13},{24,18},{25,19... | collective-permute-start | bytes 589832 | tf_op jit(solution)/shard_map/ppermute | solution.py:278
  49.2 3.3 %collective-permute-done.15.came.refs_0_ = bf16[128,768]{1,0:T(8,128)(2,1)S(1)} collective-permute-done((bf16[128,768]{1,0:T(8,128)(2,1)S(1)}, bf16[128,768]{1,0:T(8,128)(2,1)S(1)}, u32[]{:S(2)}, u32[]{:S(2)}) %collective-permute-start.15) | collective-permute-done | bytes 196640 | tf_op jit(solution)/shard_map/ppermute | solution.py:278
  52.5 1.9 %collective-permute-start.20 = (bf16[128,768]{1,0:T(8,128)(2,1)S(1)}, bf16[128,768]{1,0:T(8,128)(2,1)S(1)}, u32[]{:S(2)}, u32[]{:S(2)}) collective-permute-start(bf16[128,768]{1,0:T(8,128)(2,1)S(1)} %get-tuple-element.34), channel_id=1, source_target_pairs={{8,4},{9,5},{10,6},{11,7},{4,8},{5,9},{6,10},{7,11},{24,20},{25,21... | collective-permute-start | bytes 589832 | tf_op jit(solution)/shard_map/ppermute | solution.py:278
  54.4 3.2 %shard_map.87 = (bf16[128,768]{1,0:T(8,128)(2,1)}, f32[2,64,768]{2,1,0:T(8,128)S(1)}) custom-call(s32[15]{0:T(128)S(1)} %and_select_fusion.parity, bf16[128,768]{1,0:T(8,128)(2,1)S(1)} %collective-permute-done.15.came.refs_0_, bf16[128,768]{1,0:T(8,128)(2,1)S(1)} %get-tuple-element.22.refs_0_, bf16[128,768]{1,0:T(8,128)(2,1)S(1)} %get-tuple-element.23.refs_1_, ...), custom_call_target="tpu_custom_call" | custom-call | bytes 5000000 | tf_op jit(solution)/shard_map/pallas_call | solution.py:222
  57.6 1.2 %collective-permute-start.22 = (bf16[128,768]{1,0:T(8,128)(2,1)S(1)}, bf16[128,768]{1,0:T(8,128)(2,1)S(1)}, u32[]{:S(2)}, u32[]{:S(2)}) collective-permute-start(bf16[128,768]{1,0:T(8,128)(2,1)S(1)} %collective-permute-done.15.came.refs_0_), channel_id=1, source_target_pairs={{0,1},{1,0},{2,3},{3,2},{4,5},{5,4},{6,7},{7,6},{8,9},{9,8},{10,11... | collective-permute-start | bytes 589832 | tf_op jit(solution)/shard_map/ppermute | solution.py:338
  58.8 3.0 %collective-permute-start.21 = (bf16[128,768]{1,0:T(8,128)(2,1)S(1)}, bf16[128,768]{1,0:T(8,128)(2,1)S(1)}, u32[]{:S(2)}, u32[]{:S(2)}) collective-permute-start(bf16[128,768]{1,0:T(8,128)(2,1)S(1)} %get-tuple-element.35), channel_id=1, source_target_pairs={{10,4},{11,5},{8,6},{9,7},{6,8},{7,9},{4,10},{5,11},{26,20},{27,21... | collective-permute-start | bytes 589832 | tf_op jit(solution)/shard_map/ppermute | solution.py:278
  63.0 2.1 %collective-permute-done.20.refs_5_ = bf16[128,768]{1,0:T(8,128)(2,1)S(1)} collective-permute-done((bf16[128,768]{1,0:T(8,128)(2,1)S(1)}, bf16[128,768]{1,0:T(8,128)(2,1)S(1)}, u32[]{:S(2)}, u32[]{:S(2)}) %collective-permute-start.20) | collective-permute-done | bytes 196640 | tf_op jit(solution)/shard_map/ppermute | solution.py:278
  66.3 4.5 %collective-permute-done.21.refs_6_ = bf16[128,768]{1,0:T(8,128)(2,1)S(1)} collective-permute-done((bf16[128,768]{1,0:T(8,128)(2,1)S(1)}, bf16[128,768]{1,0:T(8,128)(2,1)S(1)}, u32[]{:S(2)}, u32[]{:S(2)}) %collective-permute-start.21) | collective-permute-done | bytes 196640 | tf_op jit(solution)/shard_map/ppermute | solution.py:278
  71.4 0.9 %collective-permute-done.27.refs_12_ = bf16[128,768]{1,0:T(8,128)(2,1)S(1)} collective-permute-done((bf16[128,768]{1,0:T(8,128)(2,1)S(1)}, bf16[128,768]{1,0:T(8,128)(2,1)S(1)}, u32[]{:S(2)}, u32[]{:S(2)}) %collective-permute-start.27) | collective-permute-done | bytes 196640 | tf_op jit(solution)/shard_map/ppermute | solution.py:338
  72.7 1.8 %shard_map.88 = bf16[128,768]{1,0:T(8,128)(2,1)} custom-call(s32[15]{0:T(128)S(1)} %and_select_fusion.parity, bf16[128,768]{1,0:T(8,128)(2,1)S(1)} %collective-permute-done.15.came.refs_0_, bf16[128,768]{1,0:T(8,128)(2,1)S(1)} %collective-permute-done.16.refs_1_, bf16[128,768]{1,0:T(8,128)(2,1)S(1)} %collective-permute-done.17.refs_2_, ...), custom_call_target="tpu_custom_call" | custom-call | bytes 5000000 | tf_op jit(solution)/shard_map/pallas_call | solution.py:258
  (71 shorter events, 12.3 us)
Async XLA Ops:
  0.6 13.7 %collective-permute-start.4 = (bf16[128,768]{1,0:T(8,128)(2,1)}, bf16[128,768]{1,0:T(8,128)(2,1)S(1)}, u32[]{:S(2)}, u32[]{:S(2)}) collective-permute-start(bf16[128,768]{1,0:T(8,128)(2,1)} %refs_16_.1), channel_id=1, source_target_pairs={{0,1},{1,0},{2,3},{3,2},{4,5},{5,4},{6,7},{7,6},{8,9},{9,8},{10,11... | collective-permute-start | bytes 589832 | tf_op jit(solution)/shard_map/ppermute | solution.py:293
  1.4 11.6 %collective-permute-start.3 = (bf16[128,768]{1,0:T(8,128)(2,1)}, bf16[128,768]{1,0:T(8,128)(2,1)S(1)}, u32[]{:S(2)}, u32[]{:S(2)}) collective-permute-start(bf16[128,768]{1,0:T(8,128)(2,1)} %refs_16_.1), channel_id=1, source_target_pairs={{4,0},{5,1},{6,2},{7,3},{0,4},{1,5},{2,6},{3,7},{12,8},{13,9},{14,... | collective-permute-start | bytes 589832 | tf_op jit(solution)/shard_map/ppermute | solution.py:278
  1.6 14.2 %collective-permute-start.2 = (bf16[128,768]{1,0:T(8,128)(2,1)}, bf16[128,768]{1,0:T(8,128)(2,1)S(1)}, u32[]{:S(2)}, u32[]{:S(2)}) collective-permute-start(bf16[128,768]{1,0:T(8,128)(2,1)} %refs_16_.1), channel_id=1, source_target_pairs={{8,0},{9,1},{10,2},{11,3},{12,4},{13,5},{14,6},{15,7},{0,8},{1,9},... | collective-permute-start | bytes 589832 | tf_op jit(solution)/shard_map/ppermute | solution.py:278
  3.9 13.2 %collective-permute-start.1 = (bf16[128,768]{1,0:T(8,128)(2,1)}, bf16[128,768]{1,0:T(8,128)(2,1)S(1)}, u32[]{:S(2)}, u32[]{:S(2)}) collective-permute-start(bf16[128,768]{1,0:T(8,128)(2,1)} %refs_16_.1), channel_id=1, source_target_pairs={{2,0},{3,1},{0,2},{1,3},{6,4},{7,5},{4,6},{5,7},{10,8},{11,9},{8,1... | collective-permute-start | bytes 589832 | tf_op jit(solution)/shard_map/ppermute | solution.py:278
  4.1 13.3 %collective-permute-start = (bf16[128,768]{1,0:T(8,128)(2,1)}, bf16[128,768]{1,0:T(8,128)(2,1)S(1)}, u32[]{:S(2)}, u32[]{:S(2)}) collective-permute-start(bf16[128,768]{1,0:T(8,128)(2,1)} %refs_16_.1), channel_id=1, source_target_pairs={{8,4},{9,5},{10,6},{11,7},{4,8},{5,9},{6,10},{7,11},{24,20},{25,21... | collective-permute-start | bytes 589832 | tf_op jit(solution)/shard_map/ppermute | solution.py:278
  13.0 10.2 %collective-permute-start.9 = (bf16[128,768]{1,0:T(8,128)(2,1)S(1)}, bf16[128,768]{1,0:T(8,128)(2,1)S(1)}, u32[]{:S(2)}, u32[]{:S(2)}) collective-permute-start(bf16[128,768]{1,0:T(8,128)(2,1)S(1)} %collective-permute-done.3.refs_4_), channel_id=1, source_target_pairs={{2,0},{3,1},{0,2},{1,3},{6,4},{7,5},{4,6},{5,7},{10,8},{11,9},{8,1... | collective-permute-start | bytes 589832 | tf_op jit(solution)/shard_map/ppermute | solution.py:278
  14.3 9.5 %collective-permute-start.8 = (bf16[128,768]{1,0:T(8,128)(2,1)S(1)}, bf16[128,768]{1,0:T(8,128)(2,1)S(1)}, u32[]{:S(2)}, u32[]{:S(2)}) collective-permute-start(bf16[128,768]{1,0:T(8,128)(2,1)S(1)} %collective-permute-done.3.refs_4_), channel_id=1, source_target_pairs={{0,1},{1,0},{2,3},{3,2},{4,5},{5,4},{6,7},{7,6},{8,9},{9,8},{10,11... | collective-permute-start | bytes 589832 | tf_op jit(solution)/shard_map/ppermute | solution.py:285
  15.8 8.4 %collective-permute-start.11 = (bf16[128,768]{1,0:T(8,128)(2,1)S(1)}, bf16[128,768]{1,0:T(8,128)(2,1)S(1)}, u32[]{:S(2)}, u32[]{:S(2)}) collective-permute-start(bf16[128,768]{1,0:T(8,128)(2,1)S(1)} %collective-permute-done.2.refs_3_), channel_id=1, source_target_pairs={{0,2},{1,3},{4,6},{5,7},{10,8},{11,9},{14,12},{15,13},{16,18},{17,... | collective-permute-start | bytes 589832 | tf_op jit(solution)/shard_map/ppermute | solution.py:278
  17.1 8.3 %collective-permute-start.7 = (bf16[128,768]{1,0:T(8,128)(2,1)S(1)}, bf16[128,768]{1,0:T(8,128)(2,1)S(1)}, u32[]{:S(2)}, u32[]{:S(2)}) collective-permute-start(bf16[128,768]{1,0:T(8,128)(2,1)S(1)} %collective-permute-done.2.refs_3_), channel_id=1, source_target_pairs={{0,1},{1,0},{2,3},{3,2},{4,5},{5,4},{6,7},{7,6},{8,9},{9,8},{10,11... | collective-permute-start | bytes 589832 | tf_op jit(solution)/shard_map/ppermute | solution.py:285
  17.4 10.9 %collective-permute-start.10 = (bf16[128,768]{1,0:T(8,128)(2,1)S(1)}, bf16[128,768]{1,0:T(8,128)(2,1)S(1)}, u32[]{:S(2)}, u32[]{:S(2)}) collective-permute-start(bf16[128,768]{1,0:T(8,128)(2,1)S(1)} %collective-permute-done.refs_1_), channel_id=1, source_target_pairs={{6,4},{7,5},{4,6},{5,7},{10,8},{11,9},{8,10},{9,11},{22,20},{23,21... | collective-permute-start | bytes 589832 | tf_op jit(solution)/shard_map/ppermute | solution.py:278
  23.2 6.5 %collective-permute-start.5 = (bf16[128,768]{1,0:T(8,128)(2,1)S(1)}, bf16[128,768]{1,0:T(8,128)(2,1)S(1)}, u32[]{:S(2)}, u32[]{:S(2)}) collective-permute-start(bf16[128,768]{1,0:T(8,128)(2,1)S(1)} %collective-permute-done.refs_1_), channel_id=1, source_target_pairs={{0,1},{1,0},{2,3},{3,2},{4,5},{5,4},{6,7},{7,6},{8,9},{9,8},{10,11... | collective-permute-start | bytes 589832 | tf_op jit(solution)/shard_map/ppermute | solution.py:285
  23.8 5.9 %collective-permute-start.6 = (bf16[128,768]{1,0:T(8,128)(2,1)S(1)}, bf16[128,768]{1,0:T(8,128)(2,1)S(1)}, u32[]{:S(2)}, u32[]{:S(2)}) collective-permute-start(bf16[128,768]{1,0:T(8,128)(2,1)S(1)} %collective-permute-done.1.refs_2_), channel_id=1, source_target_pairs={{0,1},{1,0},{2,3},{3,2},{4,5},{5,4},{6,7},{7,6},{8,9},{9,8},{10,11... | collective-permute-start | bytes 589832 | tf_op jit(solution)/shard_map/ppermute | solution.py:285
  24.2 5.6 %collective-permute-start.12 = (bf16[128,768]{1,0:T(8,128)(2,1)S(1)}, bf16[128,768]{1,0:T(8,128)(2,1)S(1)}, u32[]{:S(2)}, u32[]{:S(2)}) collective-permute-start(bf16[128,768]{1,0:T(8,128)(2,1)S(1)} %collective-permute-done.9.refs_10_), channel_id=1, source_target_pairs={{0,1},{1,0},{2,3},{3,2},{4,5},{5,4},{6,7},{7,6},{8,9},{9,8},{10,11... | collective-permute-start | bytes 589832 | tf_op jit(solution)/shard_map/ppermute | solution.py:285
  43.6 8.9 %collective-permute-start.15 = (bf16[128,768]{1,0:T(8,128)(2,1)S(1)}, bf16[128,768]{1,0:T(8,128)(2,1)S(1)}, u32[]{:S(2)}, u32[]{:S(2)}) collective-permute-start(bf16[128,768]{1,0:T(8,128)(2,1)S(1)} %get-tuple-element.21), channel_id=1, source_target_pairs={{8,0},{9,1},{10,2},{11,3},{12,4},{13,5},{14,6},{15,7},{0,8},{1,9},... | collective-permute-start | bytes 589832 | tf_op jit(solution)/shard_map/ppermute | solution.py:278
  43.7 13.9 %collective-permute-start.16 = (bf16[128,768]{1,0:T(8,128)(2,1)S(1)}, bf16[128,768]{1,0:T(8,128)(2,1)S(1)}, u32[]{:S(2)}, u32[]{:S(2)}) collective-permute-start(bf16[128,768]{1,0:T(8,128)(2,1)S(1)} %get-tuple-element.30), channel_id=1, source_target_pairs={{4,0},{5,1},{6,2},{7,3},{0,4},{1,5},{2,6},{3,7},{12,8},{13,9},{14,... | collective-permute-start | bytes 589832 | tf_op jit(solution)/shard_map/ppermute | solution.py:278
  44.4 14.4 %collective-permute-start.17 = (bf16[128,768]{1,0:T(8,128)(2,1)S(1)}, bf16[128,768]{1,0:T(8,128)(2,1)S(1)}, u32[]{:S(2)}, u32[]{:S(2)}) collective-permute-start(bf16[128,768]{1,0:T(8,128)(2,1)S(1)} %get-tuple-element.31), channel_id=1, source_target_pairs={{2,0},{3,1},{0,2},{1,3},{6,4},{7,5},{4,6},{5,7},{10,8},{11,9},{8,1... | collective-permute-start | bytes 589832 | tf_op jit(solution)/shard_map/ppermute | solution.py:278
  46.8 15.0 %collective-permute-start.18 = (bf16[128,768]{1,0:T(8,128)(2,1)S(1)}, bf16[128,768]{1,0:T(8,128)(2,1)S(1)}, u32[]{:S(2)}, u32[]{:S(2)}) collective-permute-start(bf16[128,768]{1,0:T(8,128)(2,1)S(1)} %get-tuple-element.32), channel_id=1, source_target_pairs={{8,2},{9,3},{12,6},{13,7},{2,8},{3,9},{6,12},{7,13},{24,18},{25,19... | collective-permute-start | bytes 589832 | tf_op jit(solution)/shard_map/ppermute | solution.py:278
  49.1 13.3 %collective-permute-start.19 = (bf16[128,768]{1,0:T(8,128)(2,1)S(1)}, bf16[128,768]{1,0:T(8,128)(2,1)S(1)}, u32[]{:S(2)}, u32[]{:S(2)}) collective-permute-start(bf16[128,768]{1,0:T(8,128)(2,1)S(1)} %get-tuple-element.33), channel_id=1, source_target_pairs={{6,0},{7,1},{4,2},{5,3},{2,4},{3,5},{0,6},{1,7},{14,8},{15,9},{12,... | collective-permute-start | bytes 589832 | tf_op jit(solution)/shard_map/ppermute | solution.py:278
  52.5 12.6 %collective-permute-start.20 = (bf16[128,768]{1,0:T(8,128)(2,1)S(1)}, bf16[128,768]{1,0:T(8,128)(2,1)S(1)}, u32[]{:S(2)}, u32[]{:S(2)}) collective-permute-start(bf16[128,768]{1,0:T(8,128)(2,1)S(1)} %get-tuple-element.34), channel_id=1, source_target_pairs={{8,4},{9,5},{10,6},{11,7},{4,8},{5,9},{6,10},{7,11},{24,20},{25,21... | collective-permute-start | bytes 589832 | tf_op jit(solution)/shard_map/ppermute | solution.py:278
  57.6 8.3 %collective-permute-start.22 = (bf16[128,768]{1,0:T(8,128)(2,1)S(1)}, bf16[128,768]{1,0:T(8,128)(2,1)S(1)}, u32[]{:S(2)}, u32[]{:S(2)}) collective-permute-start(bf16[128,768]{1,0:T(8,128)(2,1)S(1)} %collective-permute-done.15.came.refs_0_), channel_id=1, source_target_pairs={{0,1},{1,0},{2,3},{3,2},{4,5},{5,4},{6,7},{7,6},{8,9},{9,8},{10,11... | collective-permute-start | bytes 589832 | tf_op jit(solution)/shard_map/ppermute | solution.py:338
  58.8 12.1 %collective-permute-start.21 = (bf16[128,768]{1,0:T(8,128)(2,1)S(1)}, bf16[128,768]{1,0:T(8,128)(2,1)S(1)}, u32[]{:S(2)}, u32[]{:S(2)}) collective-permute-start(bf16[128,768]{1,0:T(8,128)(2,1)S(1)} %get-tuple-element.35), channel_id=1, source_target_pairs={{10,4},{11,5},{8,6},{9,7},{6,8},{7,9},{4,10},{5,11},{26,20},{27,21... | collective-permute-start | bytes 589832 | tf_op jit(solution)/shard_map/ppermute | solution.py:278
  61.8 9.5 %collective-permute-start.23 = (bf16[128,768]{1,0:T(8,128)(2,1)S(1)}, bf16[128,768]{1,0:T(8,128)(2,1)S(1)}, u32[]{:S(2)}, u32[]{:S(2)}) collective-permute-start(bf16[128,768]{1,0:T(8,128)(2,1)S(1)} %collective-permute-done.16.refs_1_), channel_id=1, source_target_pairs={{0,1},{1,0},{2,3},{3,2},{4,5},{5,4},{6,7},{7,6},{8,9},{9,8},{10,11... | collective-permute-start | bytes 589832 | tf_op jit(solution)/shard_map/ppermute | solution.py:338
  65.1 6.3 %collective-permute-start.24 = (bf16[128,768]{1,0:T(8,128)(2,1)S(1)}, bf16[128,768]{1,0:T(8,128)(2,1)S(1)}, u32[]{:S(2)}, u32[]{:S(2)}) collective-permute-start(bf16[128,768]{1,0:T(8,128)(2,1)S(1)} %collective-permute-done.17.refs_2_), channel_id=1, source_target_pairs={{0,1},{1,0},{2,3},{3,2},{4,5},{5,4},{6,7},{7,6},{8,9},{9,8},{10,11... | collective-permute-start | bytes 589832 | tf_op jit(solution)/shard_map/ppermute | solution.py:338
  65.8 5.6 %collective-permute-start.25 = (bf16[128,768]{1,0:T(8,128)(2,1)S(1)}, bf16[128,768]{1,0:T(8,128)(2,1)S(1)}, u32[]{:S(2)}, u32[]{:S(2)}) collective-permute-start(bf16[128,768]{1,0:T(8,128)(2,1)S(1)} %collective-permute-done.18.refs_3_), channel_id=1, source_target_pairs={{0,1},{1,0},{2,3},{3,2},{4,5},{5,4},{6,7},{7,6},{8,9},{9,8},{10,11... | collective-permute-start | bytes 589832 | tf_op jit(solution)/shard_map/ppermute | solution.py:338
  (9 other events, 58.0 us)

commit v4 on v3

--- a/solution.py
+++ b/solution.py
@@ -31,13 +31,13 @@
             relay = m in (3, 5, 7)
             fetch = [(k, k ^ 1) for k, _ in pairs] if relay else pairs
             rounds.append(Round(fetch, (m ^ 1) - 1 if relay else None, pairs, lambda k, m=m: k ^ m))
-        return rounds, [5, 0, 3, 1, 2, 6, 4], [3, 1, 0, 4, 2, 5, 6]
+        return rounds, [5, 0, 3, 1, 2, 6, 4], [3, 1, 0, 4, 2, 5, 6], 0
     rounds = []
     for d in range(-REACH, REACH + 1):
         if d != 0:
             pairs = [(k, k + d) for k in range(chips) if near(k, k + d)]
             rounds.append(Round(pairs, None, [(s, r) for r, s in pairs], lambda k, d=d: k - d))
-    return rounds, list(range(len(rounds))), list(range(len(rounds)))
+    return rounds, list(range(len(rounds))), list(range(len(rounds))), 0
 
 
 def round_of(chips, mine, peer):
@@ -72,13 +72,12 @@
 
 SMEM = pl.BlockSpec(memory_space=pltpu.SMEM)
 VMEM = pl.BlockSpec(memory_space=pltpu.VMEM)
-ANY = pl.BlockSpec(memory_space=pl.ANY)
-
-
-def weight_copies(source, target, sems):
+HBM = pl.BlockSpec(memory_space=pltpu.HBM)
+
+
+def weight_copies(source, target, sems, from_column):
     rows, columns = target.shape
     band = rows // sems.shape[0]
-    from_column = source.shape[1] - columns
     return [
         pltpu.make_async_copy(
             source.at[pl.ds(i * band, band), pl.ds(from_column, columns)],
@@ -89,35 +88,53 @@
     ]
 
 
-def main_kernel(rounds, places, meta, *refs):
+def main_kernel(rounds, places, chips, position, lists, counts, *refs):
     count = len(places)
     windows = refs[:count]
     q_ref, g_ref, gain_ref, w_hbm = refs[count : count + 4]
     att_ref, dq_ref, own_ref, sib_ref = refs[count + 4 : count + 8]
     msg_refs = refs[count + 8 : count + 8 + rounds]
-    normed, kv, kvt, acc, w, wsems = refs[count + 8 + rounds :]
+    xs, normed, kv, kvt, acc, w, source, target, named, wsems = refs[count + 8 + rounds :]
     width = q_ref.shape[1]
-    wcopies = weight_copies(w_hbm, w, wsems)
+    wcopies = weight_copies(w_hbm, w, wsems, w_hbm.shape[1] - 2 * width)
     for c in wcopies:
         c.start()
     slots = 2 * MAXNB
     span = MAXNB * BLK
 
+    me = position[0]
+    for i in range(2 * count):
+        named[i] = 0
+    for s in range(slots):
+        b, j = s // MAXNB, s % MAXNB
+        block = lists[(2 * me + b) * MAXNB + j]
+        owner = lax.shift_right_logical(block, 1)
+        turn = round_of(chips, lax.shift_right_logical(me, 1), lax.shift_right_logical(owner, 1))
+        place = 2 * turn + ((owner ^ me) & 1)
+        found = 2 * place + (block & 1)
+        source[s] = found
+        named[found] = 1
+        goal = jnp.where(place == 0, block & 1, 1 + place)
+        target[s] = jnp.where(j < counts[2 * me + b], goal, 3 + 2 * rounds)
+
     gain = gain_ref[...]
     for ref, place in zip(windows, places):
         for j in range(2):
 
-            @pl.when(meta[2 * slots + 2 + 2 * place + j] != 0)
+            @pl.when(named[2 * place + j] != 0)
             def _():
-                unit, _ = layer_norm(ref[j * BLK : (j + 1) * BLK, :].astype(F32))
-                normed[2 * place + j] = (unit * gain).astype(BF16)
+                xs[2 * place + j] = ref[j * BLK : (j + 1) * BLK, :]
+
+    @pl.loop(0, slots, unroll=4)
+    def _(s):
+        unit, _ = layer_norm(xs[source[s]].astype(F32))
+        normed[pl.ds(pl.multiple_of(s * BLK, BLK), BLK), :] = (unit * gain).astype(BF16)
 
     for c in wcopies:
         c.wait()
     rows = 256
     for i in range(slots * BLK // rows):
-        part = jnp.concatenate([normed[meta[4 * i + j]] for j in range(4)], axis=0)
-        kv[pl.ds(i * rows, rows), :] = dot(part, w[...], 1, 0).astype(BF16)
+        kv[pl.ds(i * rows, rows), :] = dot(normed[pl.ds(i * rows, rows), :], w[...], 1, 0).astype(BF16)
     acc[...] = jnp.zeros_like(acc)
 
     group = PACK * HD
@@ -132,7 +149,7 @@
         return out
 
     for b in range(2):
-        live = slot_row < meta[2 * slots + b] * BLK
+        live = slot_row < counts[2 * me + b] * BLK
         for p in range(width // group):
             lanes = pl.ds(p * group, group)
             vlanes = pl.ds(width + p * group, group)
@@ -146,10 +163,11 @@
             v = kv[krows, vlanes]
             scores = jnp.where(live, dot(k, qd, 1, 1), -1e30)
             weights = jnp.exp(scores - jnp.max(scores, axis=0, keepdims=True))
-            prob = weights * (1.0 / jnp.sum(weights, axis=0, keepdims=True))
+            pg = dot(v, gd, 1, 1)
+            inverse = 1.0 / jnp.sum(weights, axis=0, keepdims=True)
+            row_dot = jnp.sum(weights * pg, axis=0, keepdims=True) * inverse
+            prob = weights * inverse
             low_prob = prob.astype(BF16)
-            pg = dot(v, gd, 1, 1)
-            row_dot = jnp.sum(prob * pg, axis=0, keepdims=True)
             sg = (prob * (pg - row_dot)).astype(BF16)
             kvt[krows, lanes] = dot(sg, qd, 1, 0).astype(BF16)
             kvt[krows, vlanes] = dot(low_prob, gd, 1, 0).astype(BF16)
@@ -159,7 +177,7 @@
     for i in range(slots * BLK // rows):
         part = dot(kvt[pl.ds(i * rows, rows), :], w[...], 1, 1)
         for j in range(rows // BLK):
-            at = meta[slots + i * (rows // BLK) + j]
+            at = target[i * (rows // BLK) + j]
             acc[at] = acc[at] + part[j * BLK : (j + 1) * BLK, :]
     for r in range(rounds):
         msg_refs[r][0:BLK, :] = acc[3 + 2 * r].astype(BF16)
@@ -169,29 +187,33 @@
     sib_ref[...] = acc[2].astype(BF16)
 
 
-def main_call(meta, places, windows, queries, grads, gain, w_qkv):
+def main_call(chips, position, lists, counts, places, windows, queries, grads, gain, w_qkv):
     rounds = len(windows) // 2 - 1
     tokens, width = queries.shape
     slots = 2 * MAXNB
     shape = jax.ShapeDtypeStruct
     return call(
-        functools.partial(main_kernel, rounds, places),
+        functools.partial(main_kernel, rounds, places, chips),
         [shape((tokens, width), BF16)] * 2
         + [shape((tokens, width), F32), shape((BLK, width), BF16)]
         + [shape((2 * BLK, width), BF16)] * rounds,
-        [SMEM] + [VMEM] * (len(windows) + 3) + [ANY],
+        [SMEM] * 3 + [VMEM] * (len(windows) + 3) + [HBM],
         [VMEM] * (4 + rounds),
         [
             pltpu.VMEM((2 * len(windows), BLK, width), BF16),
+            pltpu.VMEM((slots * BLK, width), BF16),
             pltpu.VMEM((slots * BLK, 2 * width), BF16),
             pltpu.VMEM((slots * BLK, 2 * width), BF16),
             pltpu.VMEM((4 + 2 * rounds, BLK, width), F32),
             pltpu.VMEM((width, 2 * width), BF16),
+            pltpu.SMEM((slots,), jnp.int32),
+            pltpu.SMEM((slots,), jnp.int32),
+            pltpu.SMEM((2 * len(windows),), jnp.int32),
             pltpu.SemaphoreType.DMA((6,)),
         ],
         48,
         8 * 10**9,
-    )(meta, *windows, queries, grads, gain, w_qkv)
+    )(position, lists, counts, *windows, queries, grads, gain, w_qkv)
 
 
 def add_came(total, came, at, rows):
@@ -199,18 +221,17 @@
 
 
 def middle_kernel(rows_of, parity, came, *refs):
-    att_ref, dq_ref, own_ref, tok_ref, wqkv_hbm, wout_hbm, out_ref, total, wq, wout, sems = refs
-    width = tok_ref.shape[1]
-    copies = [
-        pltpu.make_async_copy(wout_hbm, wout, sems.at[0]),
-        pltpu.make_async_copy(wqkv_hbm.at[:, pl.ds(0, width)], wq, sems.at[1]),
-    ]
-    for c in copies:
+    att_ref, dq_ref, own_ref, tok_ref, wqkv_hbm, wout_hbm, out_ref, total, wq, wout, qsems, osems = refs
+    copies = weight_copies(wout_hbm, wout, osems, 0)
+    q_copies = weight_copies(wqkv_hbm, wq, qsems, 0)
+    for c in copies + q_copies:
         c.start()
     for c in copies:
         c.wait()
     out = tok_ref[...].astype(F32) + dot(att_ref[...], wout[...], 1, 0)
     out_ref[...] = out.astype(BF16)
+    for c in q_copies:
+        c.wait()
     base = own_ref[...] + dot(dq_ref[...], wq[...], 1, 1)
     for b in range(2):
         total[b] = base[b * BLK : (b + 1) * BLK, :]
@@ -222,9 +243,9 @@
     return call(
         functools.partial(middle_kernel, rows_of),
         [jax.ShapeDtypeStruct((count, width), BF16), jax.ShapeDtypeStruct((2, BLK, width), F32)],
-        [SMEM] + [VMEM] * 5 + [ANY] * 2,
+        [SMEM] + [VMEM] * 5 + [HBM] * 2,
         [VMEM] * 2,
-        [pltpu.VMEM((width, width), BF16)] * 2 + [pltpu.SemaphoreType.DMA((2,))],
+        [pltpu.VMEM((width, width), BF16)] * 2 + [pltpu.SemaphoreType.DMA((4,))] * 2,
         48,
     )(parity, came, attended, query_grad, own, tokens, w_qkv, w_out)
 
@@ -270,7 +291,7 @@
     chips = devices // 2
     count, width = tokens.shape
     blocks = count // BLK
-    plan, fetch_order, give_order = exchange_rounds(chips)
+    plan, fetch_order, give_order, early = exchange_rounds(chips)
     rounds = len(plan)
     mate = [(i, i ^ 1) for i in range(devices)]
 
@@ -281,6 +302,24 @@
     for r in fetch_order:
         source = plan[r].source
         arrived[r] = send(tokens if source is None else arrived[source], plan[r].fetch)
+    position = lax.axis_index("seq")
+    live = jnp.arange(MAXNB)[None, :] < nbr_count[:, None]
+    names_odd = jnp.any(live & (nbr_list == position * blocks + 1), axis=1)
+    givers = jnp.stack([position ^ 1] + [
+        plan[r].giver(position // 2) * 2 + ((position % 2) ^ other) for other in range(2) for r in range(rounds)
+    ])
+    row_owner = jnp.arange(nbr_list.shape[0]) // blocks
+    parity = jnp.any(names_odd[None, :] & (row_owner[None, :] == givers[:, None]), axis=1).astype(jnp.int32)
+
+    gain = gain.reshape(1, width)
+    lists = nbr_list.reshape(-1)
+    unit, _ = layer_norm(tokens.astype(F32))
+    normed = (unit * gain).astype(BF16)
+    queries = jnp.dot(normed, w_qkv[:, :width], preferred_element_type=F32).astype(BF16)
+    out_grad = dot(cotangent, w_out, 1, 1).astype(BF16)
+    arrived[early], parity, lists, gain = lax.optimization_barrier(
+        (arrived[early], parity, lists, gain)
+    )
     for r in fetch_order:
         passed[r] = lax.ppermute(arrived[r], "seq", mate)
     direct = [r for r in fetch_order if plan[r].source is None]
@@ -295,33 +334,9 @@
         windows += [passed[r] for r in some]
         places += [2 * (r + 1) + 1 for r in some]
 
-    position = lax.axis_index("seq")
-    chip, core = position // 2, position % 2
-    my_lists = lax.dynamic_slice_in_dim(nbr_list, position * blocks, blocks, 0)
-    my_counts = lax.dynamic_slice_in_dim(nbr_count, position * blocks, blocks, 0)
-    owner = my_lists // blocks
-    block = my_lists % blocks
-    turn = round_of(chips, chip, owner // 2)
-    other = (owner % 2) ^ core
-    source = (turn * 2 + other) * 2 + block
-    target = jnp.where(owner == position, block, 1 + 2 * turn + other)
-    live = jnp.arange(MAXNB)[None, :] < my_counts[:, None]
-    target = jnp.where(live, target, 3 + 2 * rounds)
-    named = jnp.any(source.reshape(-1, 1) == jnp.arange(4 * (rounds + 1))[None, :], axis=0)
-    meta = jnp.concatenate([source.reshape(-1), target.reshape(-1), my_counts, named]).astype(jnp.int32)
-
-    all_live = jnp.arange(MAXNB)[None, :] < nbr_count[:, None]
-    names_odd = jnp.any((all_live & (nbr_list == position * blocks + 1)).reshape(devices, -1), axis=1)
-    givers = jnp.stack([position ^ 1] + [plan[r].giver(chip) * 2 + core for r in range(rounds)]
-                       + [plan[r].giver(chip) * 2 + (1 - core) for r in range(rounds)])
-    parity = jnp.take(names_odd.astype(jnp.int32), jnp.clip(givers, 0, devices - 1))
-
-    gain = gain.reshape(1, width)
-    unit, _ = layer_norm(tokens.astype(F32))
-    normed = (unit * gain).astype(BF16)
-    queries = jnp.dot(normed, w_qkv[:, :width], preferred_element_type=F32).astype(BF16)
-    out_grad = dot(cotangent, w_out, 1, 1).astype(BF16)
-    attended, query_grad, own, sib, *messages = main_call(meta, places, windows, queries, out_grad, gain, w_qkv)
+    attended, query_grad, own, sib, *messages = main_call(
+        chips, position.reshape(1), lists, nbr_count, places, windows, queries, out_grad, gain, w_qkv
+    )
 
     came, sibs = [None] * rounds, [None] * rounds
     first, last = give_order[0], give_order[-1]

time: 75.2 us -> 73.1 us (0.972)
  starting transfers between devices: 30.6 us -> 31.9 us
  Pallas kernels: 18.3 us -> 17.1 us
  local copies, waits for them, and re-layouts: 2.73 us -> 1.67 us
  other arithmetic: 3.98 us -> 3.21 us
    ppermute x7, starting transfers between devices: 3.35 us -> 4.99 us  [per_device(): sibs[r] = lax.ppermute(came[r], 'seq', mate)]
    pallas_call x1, Pallas kernels: 13.3 us -> 12.1 us  [main_call(): call(functools.partial(main_kernel, rounds, places, chips), [shape((token...]
    select_n x3 -> x1, other arithmetic: 0.8 us -> 0.01 us  [per_device(): row_owner = jnp.arange(nbr_list.shape[0]) // blocks]
    unnamed x6 -> x9, local copies, waits for them, and re-layouts: 0.02 us -> 0.8 us
    ppermute x14, starting transfers between devices: 21.8 us -> 21 us  [send(): lax.ppermute(x, 'seq', [(2 * s + c, 2 * r + c) for r, s in pairs for c in...]
  transfers between devices with their start and end apart: 30 -> 30, of which waited for: 10 -> 8; matrix products, arithmetic and copies ran while one was open for 12% -> 10% of each run, Pallas kernels for 4% -> 4%
where the time goes in v4:
time: 73.1 us; the launch traced here: 72.7 us
  starting transfers between devices  31.9 us (44%)
  Pallas kernels  17.1 us (23%)
  waiting for transfers between devices  15.6 us (21%)
  other arithmetic  3.21 us (4%)
  matrix products  2.3 us (3%)
  local copies, waits for them, and re-layouts  1.67 us (2%)
  between operations  0.89 us (1%)
    ppermute x14, starting transfers between devices, send(): lax.ppermute(x, 'seq', [(2 * s + c, 2 * r + c) for r, s in pairs for c in...  21 us
    ppermute x14, waiting for transfers between devices, send(): lax.ppermute(x, 'seq', [(2 * s + c, 2 * r + c) for r, s in pairs for c in...  13.6 us
    pallas_call x1, Pallas kernels, main_call(): call(functools.partial(main_kernel, rounds, places, chips), [shape((token...  12.1 us
    ppermute x7, starting transfers between devices, per_device(): sibs[r] = lax.ppermute(came[r], 'seq', mate)  4.99 us
    ppermute x7, starting transfers between devices, per_device(): passed[r] = lax.ppermute(arrived[r], 'seq', mate)  4.49 us
    pallas_call x1, Pallas kernels, middle_call(): call(functools.partial(middle_kernel, rows_of), [jax.ShapeDtypeStruct((co...  3.18 us
    dot_general x1, matrix products, per_device(): jnp.dot(normed, w_qkv[:, :width], preferred_element_type=F32).astype(BF16)  1.77 us
    pallas_call x1, Pallas kernels, final_call(): call(functools.partial(final_kernel, order, done), jax.ShapeDtypeStruct((...  1.76 us
  transfers between devices with their start and end apart: 30, of which 8 were waited for; matrix products, arithmetic and copies ran while one was open for 10% of the time, Pallas kernels for 4%

profile of v4, /device:TPU:13, one launch (start us, length us, event | category | flops | bytes accessed | tf_op | source)
XLA Modules:
  0.0 72.7 jit_solution(7958280510714595562)
XLA Ops:
  1.6 2.3 %collective-permute-start.2 = (bf16[128,768]{1,0:T(8,128)(2,1)}, bf16[128,768]{1,0:T(8,128)(2,1)S(1)}, u32[]{:S(2)}, u32[]{:S(2)}) collective-permute-start(bf16[128,768]{1,0:T(8,128)(2,1)} %refs_16_.1), channel_id=1, source_target_pairs={{8,0},{9,1},{10,2},{11,3},{12,4},{13,5},{14,6},{15,7},{0,8},{1,9},... | collective-permute-start | bytes 589832 | tf_op jit(solution)/shard_map/ppermute | solution.py:299
  3.9 2.1 %collective-permute-start.1 = (bf16[128,768]{1,0:T(8,128)(2,1)}, bf16[128,768]{1,0:T(8,128)(2,1)S(1)}, u32[]{:S(2)}, u32[]{:S(2)}) collective-permute-start(bf16[128,768]{1,0:T(8,128)(2,1)} %refs_16_.1), channel_id=1, source_target_pairs={{8,4},{9,5},{10,6},{11,7},{4,8},{5,9},{6,10},{7,11},{24,20},{25,21... | collective-permute-start | bytes 589832 | tf_op jit(solution)/shard_map/ppermute | solution.py:299
  6.2 1.1 %convert_reduce_fusion = f32[128]{0:T(128)S(1)} fusion(bf16[128,768]{1,0:T(8,128)(2,1)} %refs_16_.1), kind=kLoop, calls=%fused_computation.5 | loop fusion | flops 196480 | bytes 197120 | tf_op jit(solution)/shard_map/reduce_sum | solution.py:51
  7.4 1.2 %fusion.7 = f32[128]{0:T(128)S(1)} fusion(bf16[128,768]{1,0:T(8,128)(2,1)} %refs_16_.1, f32[128]{0:T(128)S(1)} %broadcast_multiply_fusion), kind=kLoop, calls=%fused_computation.8 | loop fusion | flops 393088 | bytes 197632 | tf_op jit(solution)/shard_map/reduce_sum | solution.py:52
  11.2 1.3 %collective-permute-start.9 = (bf16[128,768]{1,0:T(8,128)(2,1)S(1)}, bf16[128,768]{1,0:T(8,128)(2,1)S(1)}, u32[]{:S(2)}, u32[]{:S(2)}) collective-permute-start(bf16[128,768]{1,0:T(8,128)(2,1)S(1)} %collective-permute-done.3.refs_4_), channel_id=1, source_target_pairs={{2,0},{3,1},{0,2},{1,3},{6,4},{7,5},{4,6},{5,7},{10,8},{11,9},{8,1... | collective-permute-start | bytes 589832 | tf_op jit(solution)/shard_map/ppermute | solution.py:299
  12.5 1.5 %collective-permute-start.8 = (bf16[128,768]{1,0:T(8,128)(2,1)S(1)}, bf16[128,768]{1,0:T(8,128)(2,1)S(1)}, u32[]{:S(2)}, u32[]{:S(2)}) collective-permute-start(bf16[128,768]{1,0:T(8,128)(2,1)S(1)} %collective-permute-done.3.refs_4_), channel_id=1, source_target_pairs={{0,1},{1,0},{2,3},{3,2},{4,5},{5,4},{6,7},{7,6},{8,9},{9,8},{10,11... | collective-permute-start | bytes 589832 | tf_op jit(solution)/shard_map/ppermute | solution.py:324
  13.9 1.3 %collective-permute-start.11 = (bf16[128,768]{1,0:T(8,128)(2,1)S(1)}, bf16[128,768]{1,0:T(8,128)(2,1)S(1)}, u32[]{:S(2)}, u32[]{:S(2)}) collective-permute-start(bf16[128,768]{1,0:T(8,128)(2,1)S(1)} %collective-permute-done.2.refs_3_), channel_id=1, source_target_pairs={{0,2},{1,3},{4,6},{5,7},{10,8},{11,9},{14,12},{15,13},{16,18},{17,... | collective-permute-start | bytes 589832 | tf_op jit(solution)/shard_map/ppermute | solution.py:299
  15.2 2.2 %collective-permute-done.1.refs_1_ = bf16[128,768]{1,0:T(8,128)(2,1)S(1)} collective-permute-done((bf16[128,768]{1,0:T(8,128)(2,1)}, bf16[128,768]{1,0:T(8,128)(2,1)S(1)}, u32[]{:S(2)}, u32[]{:S(2)}) %collective-permute-start.1) | collective-permute-done | bytes 196640 | tf_op jit(solution)/shard_map/ppermute | solution.py:299
  17.4 1.2 %collective-permute-start.7 = (bf16[128,768]{1,0:T(8,128)(2,1)S(1)}, bf16[128,768]{1,0:T(8,128)(2,1)S(1)}, u32[]{:S(2)}, u32[]{:S(2)}) collective-permute-start(bf16[128,768]{1,0:T(8,128)(2,1)S(1)} %collective-permute-done.2.refs_3_), channel_id=1, source_target_pairs={{0,1},{1,0},{2,3},{3,2},{4,5},{5,4},{6,7},{7,6},{8,9},{9,8},{10,11... | collective-permute-start | bytes 589832 | tf_op jit(solution)/shard_map/ppermute | solution.py:324
  18.6 2.1 %collective-permute-start.10 = (bf16[128,768]{1,0:T(8,128)(2,1)S(1)}, bf16[128,768]{1,0:T(8,128)(2,1)S(1)}, u32[]{:S(2)}, u32[]{:S(2)}) collective-permute-start(bf16[128,768]{1,0:T(8,128)(2,1)S(1)} %collective-permute-done.1.refs_1_), channel_id=1, source_target_pairs={{6,4},{7,5},{4,6},{5,7},{10,8},{11,9},{8,10},{9,11},{22,20},{23,21... | collective-permute-start | bytes 589832 | tf_op jit(solution)/shard_map/ppermute | solution.py:299
  20.7 1.8 %fusion.2.refs_16_ = bf16[128,768]{1,0:T(8,128)(2,1)S(1)} fusion(bf16[768,2304]{1,0:T(8,128)(2,1)} %refs_4_.1, bf16[128,768]{1,0:T(8,128)(2,1)} %refs_16_.1, f32[768]{0:T(1024)} %param.8, f32[128]{0:T(128)S(1)} %add_rsqrt_fusion, f32[128]{0:T(128)S(1)} %broadcast_multiply_fusion), kind=kOutput, calls=%fused_computation.2 | convolution fusion | flops 151584768 | bytes 1577984 | tf_op jit(solution)/shard_map/dot_general | solution.py:318
  23.6 3.4 %collective-permute-done.10.refs_11_ = bf16[128,768]{1,0:T(8,128)(2,1)S(1)} collective-permute-done((bf16[128,768]{1,0:T(8,128)(2,1)S(1)}, bf16[128,768]{1,0:T(8,128)(2,1)S(1)}, u32[]{:S(2)}, u32[]{:S(2)}) %collective-permute-start.10) | collective-permute-done | bytes 196640 | tf_op jit(solution)/shard_map/ppermute | solution.py:299
  28.9 12.1 %shard_map.86 = (bf16[128,768]{1,0:T(8,128)(2,1)S(1)}, bf16[128,768]{1,0:T(8,128)(2,1)S(1)}, f32[128,768]{1,0:T(8,128)S(1)}, bf16[64,768]{1,0:T(8,128)(2,1)S(1)}...) custom-call(s32[1]{0:T(128)} %bitcast.position, ...), custom_call_target="tpu_custom_call" | custom-call | flops 8000000000 | bytes 5000000 | tf_op jit(solution)/shard_map/pallas_call | solution.py:195
  41.1 2.4 %collective-permute-start.16 = (bf16[128,768]{1,0:T(8,128)(2,1)S(1)}, bf16[128,768]{1,0:T(8,128)(2,1)S(1)}, u32[]{:S(2)}, u32[]{:S(2)}) collective-permute-start(bf16[128,768]{1,0:T(8,128)(2,1)S(1)} %get-tuple-element.38), channel_id=1, source_target_pairs={{4,0},{5,1},{6,2},{7,3},{0,4},{1,5},{2,6},{3,7},{12,8},{13,9},{14,... | collective-permute-start | bytes 589832 | tf_op jit(solution)/shard_map/ppermute | solution.py:299
  44.0 2.7 %collective-permute-start.18 = (bf16[128,768]{1,0:T(8,128)(2,1)S(1)}, bf16[128,768]{1,0:T(8,128)(2,1)S(1)}, u32[]{:S(2)}, u32[]{:S(2)}) collective-permute-start(bf16[128,768]{1,0:T(8,128)(2,1)S(1)} %get-tuple-element.40), channel_id=1, source_target_pairs={{8,2},{9,3},{12,6},{13,7},{2,8},{3,9},{6,12},{7,13},{24,18},{25,19... | collective-permute-start | bytes 589832 | tf_op jit(solution)/shard_map/ppermute | solution.py:299
  46.8 2.6 %collective-permute-done.15.came.refs_0_ = bf16[128,768]{1,0:T(8,128)(2,1)S(1)} collective-permute-done((bf16[128,768]{1,0:T(8,128)(2,1)S(1)}, bf16[128,768]{1,0:T(8,128)(2,1)S(1)}, u32[]{:S(2)}, u32[]{:S(2)}) %collective-permute-start.15) | collective-permute-done | bytes 196640 | tf_op jit(solution)/shard_map/ppermute | solution.py:299
  49.4 3.4 %collective-permute-start.20 = (bf16[128,768]{1,0:T(8,128)(2,1)S(1)}, bf16[128,768]{1,0:T(8,128)(2,1)S(1)}, u32[]{:S(2)}, u32[]{:S(2)}) collective-permute-start(bf16[128,768]{1,0:T(8,128)(2,1)S(1)} %get-tuple-element.42), channel_id=1, source_target_pairs={{8,4},{9,5},{10,6},{11,7},{4,8},{5,9},{6,10},{7,11},{24,20},{25,21... | collective-permute-start | bytes 589832 | tf_op jit(solution)/shard_map/ppermute | solution.py:299
  52.8 3.2 %shard_map.87 = (bf16[128,768]{1,0:T(8,128)(2,1)}, f32[2,64,768]{2,1,0:T(8,128)S(1)}) custom-call(s32[15]{0:T(128)S(1)} %convert_element_type.15.parity, bf16[128,768]{1,0:T(8,128)(2,1)S(1)} %collective-permute-done.15.came.refs_0_, bf16[128,768]{1,0:T(8,128)(2,1)S(1)} %get-tuple-element.30.refs_0_, bf16[128,768]{1,0:T(8,128)(2,1)S(1)} %get-tuple-element.31.refs_1_, ...), custom_call_target="tpu_custom_call" | custom-call | bytes 5000000 | tf_op jit(solution)/shard_map/pallas_call | solution.py:243
  56.0 1.2 %collective-permute-start.22 = (bf16[128,768]{1,0:T(8,128)(2,1)S(1)}, bf16[128,768]{1,0:T(8,128)(2,1)S(1)}, u32[]{:S(2)}, u32[]{:S(2)}) collective-permute-start(bf16[128,768]{1,0:T(8,128)(2,1)S(1)} %collective-permute-done.15.came.refs_0_), channel_id=1, source_target_pairs={{0,1},{1,0},{2,3},{3,2},{4,5},{5,4},{6,7},{7,6},{8,9},{9,8},{10,11... | collective-permute-start | bytes 589832 | tf_op jit(solution)/shard_map/ppermute | solution.py:353
  57.2 2.3 %collective-permute-start.21 = (bf16[128,768]{1,0:T(8,128)(2,1)S(1)}, bf16[128,768]{1,0:T(8,128)(2,1)S(1)}, u32[]{:S(2)}, u32[]{:S(2)}) collective-permute-start(bf16[128,768]{1,0:T(8,128)(2,1)S(1)} %get-tuple-element.43), channel_id=1, source_target_pairs={{10,4},{11,5},{8,6},{9,7},{6,8},{7,9},{4,10},{5,11},{26,20},{27,21... | collective-permute-start | bytes 589832 | tf_op jit(solution)/shard_map/ppermute | solution.py:299
  62.2 1.3 %collective-permute-start.24 = (bf16[128,768]{1,0:T(8,128)(2,1)S(1)}, bf16[128,768]{1,0:T(8,128)(2,1)S(1)}, u32[]{:S(2)}, u32[]{:S(2)}) collective-permute-start(bf16[128,768]{1,0:T(8,128)(2,1)S(1)} %collective-permute-done.17.refs_2_), channel_id=1, source_target_pairs={{0,1},{1,0},{2,3},{3,2},{4,5},{5,4},{6,7},{7,6},{8,9},{9,8},{10,11... | collective-permute-start | bytes 589832 | tf_op jit(solution)/shard_map/ppermute | solution.py:353
  64.1 4.5 %collective-permute-done.21.refs_6_ = bf16[128,768]{1,0:T(8,128)(2,1)S(1)} collective-permute-done((bf16[128,768]{1,0:T(8,128)(2,1)S(1)}, bf16[128,768]{1,0:T(8,128)(2,1)S(1)}, u32[]{:S(2)}, u32[]{:S(2)}) %collective-permute-start.21) | collective-permute-done | bytes 196640 | tf_op jit(solution)/shard_map/ppermute | solution.py:299
  69.5 1.0 %collective-permute-done.27.refs_12_ = bf16[128,768]{1,0:T(8,128)(2,1)S(1)} collective-permute-done((bf16[128,768]{1,0:T(8,128)(2,1)S(1)}, bf16[128,768]{1,0:T(8,128)(2,1)S(1)}, u32[]{:S(2)}, u32[]{:S(2)}) %collective-permute-start.27) | collective-permute-done | bytes 196640 | tf_op jit(solution)/shard_map/ppermute | solution.py:353
  70.9 1.8 %shard_map.88 = bf16[128,768]{1,0:T(8,128)(2,1)} custom-call(s32[15]{0:T(128)S(1)} %convert_element_type.15.parity, bf16[128,768]{1,0:T(8,128)(2,1)S(1)} %collective-permute-done.15.came.refs_0_, bf16[128,768]{1,0:T(8,128)(2,1)S(1)} %collective-permute-done.16.refs_1_, bf16[128,768]{1,0:T(8,128)(2,1)S(1)} %collective-permute-done.17.refs_2_, ...), custom_call_target="tpu_custom_call" | custom-call | bytes 5000000 | tf_op jit(solution)/shard_map/pallas_call | solution.py:279
  (61 shorter events, 11.8 us)
Async XLA Ops:
  0.6 11.8 %collective-permute-start.4 = (bf16[128,768]{1,0:T(8,128)(2,1)}, bf16[128,768]{1,0:T(8,128)(2,1)S(1)}, u32[]{:S(2)}, u32[]{:S(2)}) collective-permute-start(bf16[128,768]{1,0:T(8,128)(2,1)} %refs_16_.1), channel_id=1, source_target_pairs={{0,1},{1,0},{2,3},{3,2},{4,5},{5,4},{6,7},{7,6},{8,9},{9,8},{10,11... | collective-permute-start | bytes 589832 | tf_op jit(solution)/shard_map/ppermute | solution.py:332
  1.4 9.8 %collective-permute-start.3 = (bf16[128,768]{1,0:T(8,128)(2,1)}, bf16[128,768]{1,0:T(8,128)(2,1)S(1)}, u32[]{:S(2)}, u32[]{:S(2)}) collective-permute-start(bf16[128,768]{1,0:T(8,128)(2,1)} %refs_16_.1), channel_id=1, source_target_pairs={{4,0},{5,1},{6,2},{7,3},{0,4},{1,5},{2,6},{3,7},{12,8},{13,9},{14,... | collective-permute-start | bytes 589832 | tf_op jit(solution)/shard_map/ppermute | solution.py:299
  1.6 12.4 %collective-permute-start.2 = (bf16[128,768]{1,0:T(8,128)(2,1)}, bf16[128,768]{1,0:T(8,128)(2,1)S(1)}, u32[]{:S(2)}, u32[]{:S(2)}) collective-permute-start(bf16[128,768]{1,0:T(8,128)(2,1)} %refs_16_.1), channel_id=1, source_target_pairs={{8,0},{9,1},{10,2},{11,3},{12,4},{13,5},{14,6},{15,7},{0,8},{1,9},... | collective-permute-start | bytes 589832 | tf_op jit(solution)/shard_map/ppermute | solution.py:299
  3.9 13.6 %collective-permute-start.1 = (bf16[128,768]{1,0:T(8,128)(2,1)}, bf16[128,768]{1,0:T(8,128)(2,1)S(1)}, u32[]{:S(2)}, u32[]{:S(2)}) collective-permute-start(bf16[128,768]{1,0:T(8,128)(2,1)} %refs_16_.1), channel_id=1, source_target_pairs={{8,4},{9,5},{10,6},{11,7},{4,8},{5,9},{6,10},{7,11},{24,20},{25,21... | collective-permute-start | bytes 589832 | tf_op jit(solution)/shard_map/ppermute | solution.py:299
  5.9 12.6 %collective-permute-start = (bf16[128,768]{1,0:T(8,128)(2,1)}, bf16[128,768]{1,0:T(8,128)(2,1)S(1)}, u32[]{:S(2)}, u32[]{:S(2)}) collective-permute-start(bf16[128,768]{1,0:T(8,128)(2,1)} %refs_16_.1), channel_id=1, source_target_pairs={{2,0},{3,1},{0,2},{1,3},{6,4},{7,5},{4,6},{5,7},{10,8},{11,9},{8,1... | collective-permute-start | bytes 589832 | tf_op jit(solution)/shard_map/ppermute | solution.py:299
  11.2 11.4 %collective-permute-start.9 = (bf16[128,768]{1,0:T(8,128)(2,1)S(1)}, bf16[128,768]{1,0:T(8,128)(2,1)S(1)}, u32[]{:S(2)}, u32[]{:S(2)}) collective-permute-start(bf16[128,768]{1,0:T(8,128)(2,1)S(1)} %collective-permute-done.3.refs_4_), channel_id=1, source_target_pairs={{2,0},{3,1},{0,2},{1,3},{6,4},{7,5},{4,6},{5,7},{10,8},{11,9},{8,1... | collective-permute-start | bytes 589832 | tf_op jit(solution)/shard_map/ppermute | solution.py:299
  12.5 10.4 %collective-permute-start.8 = (bf16[128,768]{1,0:T(8,128)(2,1)S(1)}, bf16[128,768]{1,0:T(8,128)(2,1)S(1)}, u32[]{:S(2)}, u32[]{:S(2)}) collective-permute-start(bf16[128,768]{1,0:T(8,128)(2,1)S(1)} %collective-permute-done.3.refs_4_), channel_id=1, source_target_pairs={{0,1},{1,0},{2,3},{3,2},{4,5},{5,4},{6,7},{7,6},{8,9},{9,8},{10,11... | collective-permute-start | bytes 589832 | tf_op jit(solution)/shard_map/ppermute | solution.py:324
  13.9 9.2 %collective-permute-start.11 = (bf16[128,768]{1,0:T(8,128)(2,1)S(1)}, bf16[128,768]{1,0:T(8,128)(2,1)S(1)}, u32[]{:S(2)}, u32[]{:S(2)}) collective-permute-start(bf16[128,768]{1,0:T(8,128)(2,1)S(1)} %collective-permute-done.2.refs_3_), channel_id=1, source_target_pairs={{0,2},{1,3},{4,6},{5,7},{10,8},{11,9},{14,12},{15,13},{16,18},{17,... | collective-permute-start | bytes 589832 | tf_op jit(solution)/shard_map/ppermute | solution.py:299
  17.4 6.0 %collective-permute-start.7 = (bf16[128,768]{1,0:T(8,128)(2,1)S(1)}, bf16[128,768]{1,0:T(8,128)(2,1)S(1)}, u32[]{:S(2)}, u32[]{:S(2)}) collective-permute-start(bf16[128,768]{1,0:T(8,128)(2,1)S(1)} %collective-permute-done.2.refs_3_), channel_id=1, source_target_pairs={{0,1},{1,0},{2,3},{3,2},{4,5},{5,4},{6,7},{7,6},{8,9},{9,8},{10,11... | collective-permute-start | bytes 589832 | tf_op jit(solution)/shard_map/ppermute | solution.py:324
  18.6 8.4 %collective-permute-start.10 = (bf16[128,768]{1,0:T(8,128)(2,1)S(1)}, bf16[128,768]{1,0:T(8,128)(2,1)S(1)}, u32[]{:S(2)}, u32[]{:S(2)}) collective-permute-start(bf16[128,768]{1,0:T(8,128)(2,1)S(1)} %collective-permute-done.1.refs_1_), channel_id=1, source_target_pairs={{6,4},{7,5},{4,6},{5,7},{10,8},{11,9},{8,10},{9,11},{22,20},{23,21... | collective-permute-start | bytes 589832 | tf_op jit(solution)/shard_map/ppermute | solution.py:299
  22.5 5.8 %collective-permute-start.6 = (bf16[128,768]{1,0:T(8,128)(2,1)S(1)}, bf16[128,768]{1,0:T(8,128)(2,1)S(1)}, u32[]{:S(2)}, u32[]{:S(2)}) collective-permute-start(bf16[128,768]{1,0:T(8,128)(2,1)S(1)} %collective-permute-done.refs_2_), channel_id=1, source_target_pairs={{0,1},{1,0},{2,3},{3,2},{4,5},{5,4},{6,7},{7,6},{8,9},{9,8},{10,11... | collective-permute-start | bytes 589832 | tf_op jit(solution)/shard_map/ppermute | solution.py:324
  22.9 5.5 %collective-permute-start.5 = (bf16[128,768]{1,0:T(8,128)(2,1)S(1)}, bf16[128,768]{1,0:T(8,128)(2,1)S(1)}, u32[]{:S(2)}, u32[]{:S(2)}) collective-permute-start(bf16[128,768]{1,0:T(8,128)(2,1)S(1)} %collective-permute-done.1.refs_1_), channel_id=1, source_target_pairs={{0,1},{1,0},{2,3},{3,2},{4,5},{5,4},{6,7},{7,6},{8,9},{9,8},{10,11... | collective-permute-start | bytes 589832 | tf_op jit(solution)/shard_map/ppermute | solution.py:324
  41.0 8.4 %collective-permute-start.15 = (bf16[128,768]{1,0:T(8,128)(2,1)S(1)}, bf16[128,768]{1,0:T(8,128)(2,1)S(1)}, u32[]{:S(2)}, u32[]{:S(2)}) collective-permute-start(bf16[128,768]{1,0:T(8,128)(2,1)S(1)} %get-tuple-element.29), channel_id=1, source_target_pairs={{8,0},{9,1},{10,2},{11,3},{12,4},{13,5},{14,6},{15,7},{0,8},{1,9},... | collective-permute-start | bytes 589832 | tf_op jit(solution)/shard_map/ppermute | solution.py:299
  41.1 14.9 %collective-permute-start.16 = (bf16[128,768]{1,0:T(8,128)(2,1)S(1)}, bf16[128,768]{1,0:T(8,128)(2,1)S(1)}, u32[]{:S(2)}, u32[]{:S(2)}) collective-permute-start(bf16[128,768]{1,0:T(8,128)(2,1)S(1)} %get-tuple-element.38), channel_id=1, source_target_pairs={{4,0},{5,1},{6,2},{7,3},{0,4},{1,5},{2,6},{3,7},{12,8},{13,9},{14,... | collective-permute-start | bytes 589832 | tf_op jit(solution)/shard_map/ppermute | solution.py:299
  43.5 13.7 %collective-permute-start.17 = (bf16[128,768]{1,0:T(8,128)(2,1)S(1)}, bf16[128,768]{1,0:T(8,128)(2,1)S(1)}, u32[]{:S(2)}, u32[]{:S(2)}) collective-permute-start(bf16[128,768]{1,0:T(8,128)(2,1)S(1)} %get-tuple-element.39), channel_id=1, source_target_pairs={{2,0},{3,1},{0,2},{1,3},{6,4},{7,5},{4,6},{5,7},{10,8},{11,9},{8,1... | collective-permute-start | bytes 589832 | tf_op jit(solution)/shard_map/ppermute | solution.py:299
  44.0 15.6 %collective-permute-start.18 = (bf16[128,768]{1,0:T(8,128)(2,1)S(1)}, bf16[128,768]{1,0:T(8,128)(2,1)S(1)}, u32[]{:S(2)}, u32[]{:S(2)}) collective-permute-start(bf16[128,768]{1,0:T(8,128)(2,1)S(1)} %get-tuple-element.40), channel_id=1, source_target_pairs={{8,2},{9,3},{12,6},{13,7},{2,8},{3,9},{6,12},{7,13},{24,18},{25,19... | collective-permute-start | bytes 589832 | tf_op jit(solution)/shard_map/ppermute | solution.py:299
  46.7 13.9 %collective-permute-start.19 = (bf16[128,768]{1,0:T(8,128)(2,1)S(1)}, bf16[128,768]{1,0:T(8,128)(2,1)S(1)}, u32[]{:S(2)}, u32[]{:S(2)}) collective-permute-start(bf16[128,768]{1,0:T(8,128)(2,1)S(1)} %get-tuple-element.41), channel_id=1, source_target_pairs={{6,0},{7,1},{4,2},{5,3},{2,4},{3,5},{0,6},{1,7},{14,8},{15,9},{12,... | collective-permute-start | bytes 589832 | tf_op jit(solution)/shard_map/ppermute | solution.py:299
  49.4 12.8 %collective-permute-start.20 = (bf16[128,768]{1,0:T(8,128)(2,1)S(1)}, bf16[128,768]{1,0:T(8,128)(2,1)S(1)}, u32[]{:S(2)}, u32[]{:S(2)}) collective-permute-start(bf16[128,768]{1,0:T(8,128)(2,1)S(1)} %get-tuple-element.42), channel_id=1, source_target_pairs={{8,4},{9,5},{10,6},{11,7},{4,8},{5,9},{6,10},{7,11},{24,20},{25,21... | collective-permute-start | bytes 589832 | tf_op jit(solution)/shard_map/ppermute | solution.py:299
  56.0 7.6 %collective-permute-start.22 = (bf16[128,768]{1,0:T(8,128)(2,1)S(1)}, bf16[128,768]{1,0:T(8,128)(2,1)S(1)}, u32[]{:S(2)}, u32[]{:S(2)}) collective-permute-start(bf16[128,768]{1,0:T(8,128)(2,1)S(1)} %collective-permute-done.15.came.refs_0_), channel_id=1, source_target_pairs={{0,1},{1,0},{2,3},{3,2},{4,5},{5,4},{6,7},{7,6},{8,9},{9,8},{10,11... | collective-permute-start | bytes 589832 | tf_op jit(solution)/shard_map/ppermute | solution.py:353
  57.2 11.4 %collective-permute-start.21 = (bf16[128,768]{1,0:T(8,128)(2,1)S(1)}, bf16[128,768]{1,0:T(8,128)(2,1)S(1)}, u32[]{:S(2)}, u32[]{:S(2)}) collective-permute-start(bf16[128,768]{1,0:T(8,128)(2,1)S(1)} %get-tuple-element.43), channel_id=1, source_target_pairs={{10,4},{11,5},{8,6},{9,7},{6,8},{7,9},{4,10},{5,11},{26,20},{27,21... | collective-permute-start | bytes 589832 | tf_op jit(solution)/shard_map/ppermute | solution.py:299
  59.6 9.9 %collective-permute-start.23 = (bf16[128,768]{1,0:T(8,128)(2,1)S(1)}, bf16[128,768]{1,0:T(8,128)(2,1)S(1)}, u32[]{:S(2)}, u32[]{:S(2)}) collective-permute-start(bf16[128,768]{1,0:T(8,128)(2,1)S(1)} %collective-permute-done.16.refs_1_), channel_id=1, source_target_pairs={{0,1},{1,0},{2,3},{3,2},{4,5},{5,4},{6,7},{7,6},{8,9},{9,8},{10,11... | collective-permute-start | bytes 589832 | tf_op jit(solution)/shard_map/ppermute | solution.py:353
  62.2 7.2 %collective-permute-start.24 = (bf16[128,768]{1,0:T(8,128)(2,1)S(1)}, bf16[128,768]{1,0:T(8,128)(2,1)S(1)}, u32[]{:S(2)}, u32[]{:S(2)}) collective-permute-start(bf16[128,768]{1,0:T(8,128)(2,1)S(1)} %collective-permute-done.17.refs_2_), channel_id=1, source_target_pairs={{0,1},{1,0},{2,3},{3,2},{4,5},{5,4},{6,7},{7,6},{8,9},{9,8},{10,11... | collective-permute-start | bytes 589832 | tf_op jit(solution)/shard_map/ppermute | solution.py:353
  63.6 5.9 %collective-permute-start.25 = (bf16[128,768]{1,0:T(8,128)(2,1)S(1)}, bf16[128,768]{1,0:T(8,128)(2,1)S(1)}, u32[]{:S(2)}, u32[]{:S(2)}) collective-permute-start(bf16[128,768]{1,0:T(8,128)(2,1)S(1)} %collective-permute-done.18.refs_3_), channel_id=1, source_target_pairs={{0,1},{1,0},{2,3},{3,2},{4,5},{5,4},{6,7},{7,6},{8,9},{9,8},{10,11... | collective-permute-start | bytes 589832 | tf_op jit(solution)/shard_map/ppermute | solution.py:353
  63.6 5.9 %collective-permute-start.26 = (bf16[128,768]{1,0:T(8,128)(2,1)S(1)}, bf16[128,768]{1,0:T(8,128)(2,1)S(1)}, u32[]{:S(2)}, u32[]{:S(2)}) collective-permute-start(bf16[128,768]{1,0:T(8,128)(2,1)S(1)} %collective-permute-done.19.refs_4_), channel_id=1, source_target_pairs={{0,1},{1,0},{2,3},{3,2},{4,5},{5,4},{6,7},{7,6},{8,9},{9,8},{10,11... | collective-permute-start | bytes 589832 | tf_op jit(solution)/shard_map/ppermute | solution.py:353
  (10 other events, 72.1 us)

commit v5 on v4

--- a/solution.py
+++ b/solution.py
@@ -28,10 +28,10 @@
         rounds = []
         for m in range(1, 8):
             pairs = [(k, k ^ m) for k in range(chips) if near(k, k ^ m)]
-            relay = m in (3, 5, 7)
+            relay = m in (5, 7)
             fetch = [(k, k ^ 1) for k, _ in pairs] if relay else pairs
             rounds.append(Round(fetch, (m ^ 1) - 1 if relay else None, pairs, lambda k, m=m: k ^ m))
-        return rounds, [5, 0, 3, 1, 2, 6, 4], [3, 1, 0, 4, 2, 5, 6], 0
+        return rounds, [1, 5, 2, 0, 3, 4, 6], [3, 1, 0, 4, 2, 5, 6], 0
     rounds = []
     for d in range(-REACH, REACH + 1):
         if d != 0:

time: 73.1 us -> 72.6 us (level)
  waiting for transfers between devices: 15.6 us -> 14 us
  starting transfers between devices: 31.9 us -> 33 us
    ppermute x14, starting transfers between devices: 21 us -> 23 us  [send(): lax.ppermute(x, 'seq', [(2 * s + c, 2 * r + c) for r, s in pairs for c in...]
    ppermute x14, waiting for transfers between devices: 13.6 us -> 12 us  [send(): lax.ppermute(x, 'seq', [(2 * s + c, 2 * r + c) for r, s in pairs for c in...]
    ppermute x7, starting transfers between devices: 4.99 us -> 3.99 us  [per_device(): sibs[r] = lax.ppermute(came[r], 'seq', mate)]
  transfers between devices with their start and end apart: 30 -> 30, of which waited for: 8 -> 9; matrix products, arithmetic and copies ran while one was open for 10% -> 10% of each run, Pallas kernels for 4% -> 4%
where the time goes in v5:
time: 72.6 us; the launch traced here: 72.2 us
  starting transfers between devices  33 us (45%)
  Pallas kernels  17.1 us (24%)
  waiting for transfers between devices  14 us (19%)
  other arithmetic  3.21 us (4%)
  matrix products  2.3 us (3%)
  local copies, waits for them, and re-layouts  1.67 us (2%)
  between operations  0.91 us (1%)
    ppermute x14, starting transfers between devices, send(): lax.ppermute(x, 'seq', [(2 * s + c, 2 * r + c) for r, s in pairs for c in...  23 us
    pallas_call x1, Pallas kernels, main_call(): call(functools.partial(main_kernel, rounds, places, chips), [shape((token...  12.1 us
    ppermute x14, waiting for transfers between devices, send(): lax.ppermute(x, 'seq', [(2 * s + c, 2 * r + c) for r, s in pairs for c in...  12 us
    ppermute x7, starting transfers between devices, per_device(): passed[r] = lax.ppermute(arrived[r], 'seq', mate)  4.33 us
    ppermute x7, starting transfers between devices, per_device(): sibs[r] = lax.ppermute(came[r], 'seq', mate)  3.99 us
    pallas_call x1, Pallas kernels, middle_call(): call(functools.partial(middle_kernel, rows_of), [jax.ShapeDtypeStruct((co...  3.18 us
    dot_general x1, matrix products, per_device(): jnp.dot(normed, w_qkv[:, :width], preferred_element_type=F32).astype(BF16)  1.77 us
    pallas_call x1, Pallas kernels, final_call(): call(functools.partial(final_kernel, order, done), jax.ShapeDtypeStruct((...  1.76 us
  transfers between devices with their start and end apart: 30, of which 9 were waited for; matrix products, arithmetic and copies ran while one was open for 10% of the time, Pallas kernels for 4%

profile of v5, /device:TPU:13, one launch (start us, length us, event | category | flops | bytes accessed | tf_op | source)
XLA Modules:
  0.0 72.2 jit_solution(8441029277136829944)
XLA Ops:
  1.4 2.3 %collective-permute-start.4 = (bf16[128,768]{1,0:T(8,128)(2,1)}, bf16[128,768]{1,0:T(8,128)(2,1)S(1)}, u32[]{:S(2)}, u32[]{:S(2)}) collective-permute-start(bf16[128,768]{1,0:T(8,128)(2,1)} %refs_16_.1), channel_id=1, source_target_pairs={{8,0},{9,1},{10,2},{11,3},{12,4},{13,5},{14,6},{15,7},{0,8},{1,9},... | collective-permute-start | bytes 589832 | tf_op jit(solution)/shard_map/ppermute | solution.py:299
  3.8 2.1 %collective-permute-start.2 = (bf16[128,768]{1,0:T(8,128)(2,1)}, bf16[128,768]{1,0:T(8,128)(2,1)S(1)}, u32[]{:S(2)}, u32[]{:S(2)}) collective-permute-start(bf16[128,768]{1,0:T(8,128)(2,1)} %refs_16_.1), channel_id=1, source_target_pairs={{8,4},{9,5},{10,6},{11,7},{4,8},{5,9},{6,10},{7,11},{24,20},{25,21... | collective-permute-start | bytes 589832 | tf_op jit(solution)/shard_map/ppermute | solution.py:299
  5.9 1.3 %collective-permute-start = (bf16[128,768]{1,0:T(8,128)(2,1)}, bf16[128,768]{1,0:T(8,128)(2,1)S(1)}, u32[]{:S(2)}, u32[]{:S(2)}) collective-permute-start(bf16[128,768]{1,0:T(8,128)(2,1)} %refs_16_.1), channel_id=1, source_target_pairs={{2,0},{3,1},{0,2},{1,3},{6,4},{7,5},{4,6},{5,7},{10,8},{11,9},{8,1... | collective-permute-start | bytes 589832 | tf_op jit(solution)/shard_map/ppermute | solution.py:299
  7.2 1.1 %convert_reduce_fusion = f32[128]{0:T(128)S(1)} fusion(bf16[128,768]{1,0:T(8,128)(2,1)} %refs_16_.1), kind=kLoop, calls=%fused_computation.5 | loop fusion | flops 196480 | bytes 197120 | tf_op jit(solution)/shard_map/reduce_sum | solution.py:51
  8.3 1.2 %fusion.7 = f32[128]{0:T(128)S(1)} fusion(bf16[128,768]{1,0:T(8,128)(2,1)} %refs_16_.1, f32[128]{0:T(128)S(1)} %broadcast_multiply_fusion), kind=kLoop, calls=%fused_computation.8 | loop fusion | flops 393088 | bytes 197632 | tf_op jit(solution)/shard_map/reduce_sum | solution.py:52
  12.8 1.3 %collective-permute-start.11 = (bf16[128,768]{1,0:T(8,128)(2,1)S(1)}, bf16[128,768]{1,0:T(8,128)(2,1)S(1)}, u32[]{:S(2)}, u32[]{:S(2)}) collective-permute-start(bf16[128,768]{1,0:T(8,128)(2,1)S(1)} %collective-permute-done.4.refs_5_), channel_id=1, source_target_pairs={{0,2},{1,3},{4,6},{5,7},{10,8},{11,9},{14,12},{15,13},{16,18},{17,... | collective-permute-start | bytes 589832 | tf_op jit(solution)/shard_map/ppermute | solution.py:299
  14.8 2.2 %collective-permute-done.2.refs_2_ = bf16[128,768]{1,0:T(8,128)(2,1)S(1)} collective-permute-done((bf16[128,768]{1,0:T(8,128)(2,1)}, bf16[128,768]{1,0:T(8,128)(2,1)S(1)}, u32[]{:S(2)}, u32[]{:S(2)}) %collective-permute-start.2) | collective-permute-done | bytes 196640 | tf_op jit(solution)/shard_map/ppermute | solution.py:299
  17.4 2.2 %collective-permute-start.12 = (bf16[128,768]{1,0:T(8,128)(2,1)S(1)}, bf16[128,768]{1,0:T(8,128)(2,1)S(1)}, u32[]{:S(2)}, u32[]{:S(2)}) collective-permute-start(bf16[128,768]{1,0:T(8,128)(2,1)S(1)} %collective-permute-done.2.refs_2_), channel_id=1, source_target_pairs={{6,4},{7,5},{4,6},{5,7},{10,8},{11,9},{8,10},{9,11},{22,20},{23,21... | collective-permute-start | bytes 589832 | tf_op jit(solution)/shard_map/ppermute | solution.py:299
  19.6 1.8 %fusion.2.refs_16_ = bf16[128,768]{1,0:T(8,128)(2,1)S(1)} fusion(bf16[768,2304]{1,0:T(8,128)(2,1)} %refs_4_.1, bf16[128,768]{1,0:T(8,128)(2,1)} %refs_16_.1, f32[768]{0:T(1024)} %param.8, f32[128]{0:T(128)S(1)} %add_rsqrt_fusion, f32[128]{0:T(128)S(1)} %broadcast_multiply_fusion), kind=kOutput, calls=%fused_computation.2 | convolution fusion | flops 151584768 | bytes 1577984 | tf_op jit(solution)/shard_map/dot_general | solution.py:318
  21.4 1.5 %collective-permute-start.9 = (bf16[128,768]{1,0:T(8,128)(2,1)S(1)}, bf16[128,768]{1,0:T(8,128)(2,1)S(1)}, u32[]{:S(2)}, u32[]{:S(2)}) collective-permute-start(bf16[128,768]{1,0:T(8,128)(2,1)S(1)} %collective-permute-done.refs_4_), channel_id=1, source_target_pairs={{0,1},{1,0},{2,3},{3,2},{4,5},{5,4},{6,7},{7,6},{8,9},{9,8},{10,11... | collective-permute-start | bytes 589832 | tf_op jit(solution)/shard_map/ppermute | solution.py:324
  23.6 2.0 %collective-permute-done.12.refs_13_ = bf16[128,768]{1,0:T(8,128)(2,1)S(1)} collective-permute-done((bf16[128,768]{1,0:T(8,128)(2,1)S(1)}, bf16[128,768]{1,0:T(8,128)(2,1)S(1)}, u32[]{:S(2)}, u32[]{:S(2)}) %collective-permute-start.12) | collective-permute-done | bytes 196640 | tf_op jit(solution)/shard_map/ppermute | solution.py:299
  25.6 1.1 %collective-permute-start.14 = (bf16[128,768]{1,0:T(8,128)(2,1)S(1)}, bf16[128,768]{1,0:T(8,128)(2,1)S(1)}, u32[]{:S(2)}, u32[]{:S(2)}) collective-permute-start(bf16[128,768]{1,0:T(8,128)(2,1)S(1)} %collective-permute-done.12.refs_13_), channel_id=1, source_target_pairs={{0,1},{1,0},{2,3},{3,2},{4,5},{5,4},{6,7},{7,6},{8,9},{9,8},{10,11... | collective-permute-start | bytes 589832 | tf_op jit(solution)/shard_map/ppermute | solution.py:324
  27.7 12.1 %shard_map.86 = (bf16[128,768]{1,0:T(8,128)(2,1)S(1)}, bf16[128,768]{1,0:T(8,128)(2,1)S(1)}, f32[128,768]{1,0:T(8,128)S(1)}, bf16[64,768]{1,0:T(8,128)(2,1)S(1)}...) custom-call(s32[1]{0:T(128)} %bitcast.position, ...), custom_call_target="tpu_custom_call" | custom-call | flops 8000000000 | bytes 5000000 | tf_op jit(solution)/shard_map/pallas_call | solution.py:195
  39.9 3.3 %collective-permute-start.16 = (bf16[128,768]{1,0:T(8,128)(2,1)S(1)}, bf16[128,768]{1,0:T(8,128)(2,1)S(1)}, u32[]{:S(2)}, u32[]{:S(2)}) collective-permute-start(bf16[128,768]{1,0:T(8,128)(2,1)S(1)} %get-tuple-element.38), channel_id=1, source_target_pairs={{4,0},{5,1},{6,2},{7,3},{0,4},{1,5},{2,6},{3,7},{12,8},{13,9},{14,... | collective-permute-start | bytes 589832 | tf_op jit(solution)/shard_map/ppermute | solution.py:299
  43.5 2.9 %collective-permute-start.18 = (bf16[128,768]{1,0:T(8,128)(2,1)S(1)}, bf16[128,768]{1,0:T(8,128)(2,1)S(1)}, u32[]{:S(2)}, u32[]{:S(2)}) collective-permute-start(bf16[128,768]{1,0:T(8,128)(2,1)S(1)} %get-tuple-element.40), channel_id=1, source_target_pairs={{8,2},{9,3},{12,6},{13,7},{2,8},{3,9},{6,12},{7,13},{24,18},{25,19... | collective-permute-start | bytes 589832 | tf_op jit(solution)/shard_map/ppermute | solution.py:299
  46.4 1.3 %collective-permute-done.15.came.refs_0_ = bf16[128,768]{1,0:T(8,128)(2,1)S(1)} collective-permute-done((bf16[128,768]{1,0:T(8,128)(2,1)S(1)}, bf16[128,768]{1,0:T(8,128)(2,1)S(1)}, u32[]{:S(2)}, u32[]{:S(2)}) %collective-permute-start.15) | collective-permute-done | bytes 196640 | tf_op jit(solution)/shard_map/ppermute | solution.py:299
  47.8 4.8 %collective-permute-start.20 = (bf16[128,768]{1,0:T(8,128)(2,1)S(1)}, bf16[128,768]{1,0:T(8,128)(2,1)S(1)}, u32[]{:S(2)}, u32[]{:S(2)}) collective-permute-start(bf16[128,768]{1,0:T(8,128)(2,1)S(1)} %get-tuple-element.42), channel_id=1, source_target_pairs={{8,4},{9,5},{10,6},{11,7},{4,8},{5,9},{6,10},{7,11},{24,20},{25,21... | collective-permute-start | bytes 589832 | tf_op jit(solution)/shard_map/ppermute | solution.py:299
  52.6 3.2 %shard_map.87 = (bf16[128,768]{1,0:T(8,128)(2,1)}, f32[2,64,768]{2,1,0:T(8,128)S(1)}) custom-call(s32[15]{0:T(128)S(1)} %convert_element_type.15.parity, bf16[128,768]{1,0:T(8,128)(2,1)S(1)} %collective-permute-done.15.came.refs_0_, bf16[128,768]{1,0:T(8,128)(2,1)S(1)} %get-tuple-element.30.refs_0_, bf16[128,768]{1,0:T(8,128)(2,1)S(1)} %get-tuple-element.31.refs_1_, ...), custom_call_target="tpu_custom_call" | custom-call | bytes 5000000 | tf_op jit(solution)/shard_map/pallas_call | solution.py:243
  55.8 1.0 %collective-permute-start.22 = (bf16[128,768]{1,0:T(8,128)(2,1)S(1)}, bf16[128,768]{1,0:T(8,128)(2,1)S(1)}, u32[]{:S(2)}, u32[]{:S(2)}) collective-permute-start(bf16[128,768]{1,0:T(8,128)(2,1)S(1)} %collective-permute-done.15.came.refs_0_), channel_id=1, source_target_pairs={{0,1},{1,0},{2,3},{3,2},{4,5},{5,4},{6,7},{7,6},{8,9},{9,8},{10,11... | collective-permute-start | bytes 589832 | tf_op jit(solution)/shard_map/ppermute | solution.py:353
  56.9 2.3 %collective-permute-start.21 = (bf16[128,768]{1,0:T(8,128)(2,1)S(1)}, bf16[128,768]{1,0:T(8,128)(2,1)S(1)}, u32[]{:S(2)}, u32[]{:S(2)}) collective-permute-start(bf16[128,768]{1,0:T(8,128)(2,1)S(1)} %get-tuple-element.43), channel_id=1, source_target_pairs={{10,4},{11,5},{8,6},{9,7},{6,8},{7,9},{4,10},{5,11},{26,20},{27,21... | collective-permute-start | bytes 589832 | tf_op jit(solution)/shard_map/ppermute | solution.py:299
  61.1 1.4 %collective-permute-start.24 = (bf16[128,768]{1,0:T(8,128)(2,1)S(1)}, bf16[128,768]{1,0:T(8,128)(2,1)S(1)}, u32[]{:S(2)}, u32[]{:S(2)}) collective-permute-start(bf16[128,768]{1,0:T(8,128)(2,1)S(1)} %collective-permute-done.17.refs_2_), channel_id=1, source_target_pairs={{0,1},{1,0},{2,3},{3,2},{4,5},{5,4},{6,7},{7,6},{8,9},{9,8},{10,11... | collective-permute-start | bytes 589832 | tf_op jit(solution)/shard_map/ppermute | solution.py:353
  62.9 5.3 %collective-permute-done.21.refs_6_ = bf16[128,768]{1,0:T(8,128)(2,1)S(1)} collective-permute-done((bf16[128,768]{1,0:T(8,128)(2,1)S(1)}, bf16[128,768]{1,0:T(8,128)(2,1)S(1)}, u32[]{:S(2)}, u32[]{:S(2)}) %collective-permute-start.21) | collective-permute-done | bytes 196640 | tf_op jit(solution)/shard_map/ppermute | solution.py:299
  69.0 1.0 %collective-permute-done.27.refs_12_ = bf16[128,768]{1,0:T(8,128)(2,1)S(1)} collective-permute-done((bf16[128,768]{1,0:T(8,128)(2,1)S(1)}, bf16[128,768]{1,0:T(8,128)(2,1)S(1)}, u32[]{:S(2)}, u32[]{:S(2)}) %collective-permute-start.27) | collective-permute-done | bytes 196640 | tf_op jit(solution)/shard_map/ppermute | solution.py:353
  70.4 1.8 %shard_map.88 = bf16[128,768]{1,0:T(8,128)(2,1)} custom-call(s32[15]{0:T(128)S(1)} %convert_element_type.15.parity, bf16[128,768]{1,0:T(8,128)(2,1)S(1)} %collective-permute-done.15.came.refs_0_, bf16[128,768]{1,0:T(8,128)(2,1)S(1)} %collective-permute-done.16.refs_1_, bf16[128,768]{1,0:T(8,128)(2,1)S(1)} %collective-permute-done.17.refs_2_, ...), custom_call_target="tpu_custom_call" | custom-call | bytes 5000000 | tf_op jit(solution)/shard_map/pallas_call | solution.py:279
  (61 shorter events, 10.8 us)
Async XLA Ops:
  0.6 11.5 %collective-permute-start.5 = (bf16[128,768]{1,0:T(8,128)(2,1)}, bf16[128,768]{1,0:T(8,128)(2,1)S(1)}, u32[]{:S(2)}, u32[]{:S(2)}) collective-permute-start(bf16[128,768]{1,0:T(8,128)(2,1)} %refs_16_.1), channel_id=1, source_target_pairs={{0,1},{1,0},{2,3},{3,2},{4,5},{5,4},{6,7},{7,6},{8,9},{9,8},{10,11... | collective-permute-start | bytes 589832 | tf_op jit(solution)/shard_map/ppermute | solution.py:332
  1.4 11.4 %collective-permute-start.4 = (bf16[128,768]{1,0:T(8,128)(2,1)}, bf16[128,768]{1,0:T(8,128)(2,1)S(1)}, u32[]{:S(2)}, u32[]{:S(2)}) collective-permute-start(bf16[128,768]{1,0:T(8,128)(2,1)} %refs_16_.1), channel_id=1, source_target_pairs={{8,0},{9,1},{10,2},{11,3},{12,4},{13,5},{14,6},{15,7},{0,8},{1,9},... | collective-permute-start | bytes 589832 | tf_op jit(solution)/shard_map/ppermute | solution.py:299
  3.7 10.4 %collective-permute-start.3 = (bf16[128,768]{1,0:T(8,128)(2,1)}, bf16[128,768]{1,0:T(8,128)(2,1)S(1)}, u32[]{:S(2)}, u32[]{:S(2)}) collective-permute-start(bf16[128,768]{1,0:T(8,128)(2,1)} %refs_16_.1), channel_id=1, source_target_pairs={{6,0},{7,1},{4,2},{5,3},{2,4},{3,5},{0,6},{1,7},{14,8},{15,9},{12,... | collective-permute-start | bytes 589832 | tf_op jit(solution)/shard_map/ppermute | solution.py:299
  3.8 13.2 %collective-permute-start.2 = (bf16[128,768]{1,0:T(8,128)(2,1)}, bf16[128,768]{1,0:T(8,128)(2,1)S(1)}, u32[]{:S(2)}, u32[]{:S(2)}) collective-permute-start(bf16[128,768]{1,0:T(8,128)(2,1)} %refs_16_.1), channel_id=1, source_target_pairs={{8,4},{9,5},{10,6},{11,7},{4,8},{5,9},{6,10},{7,11},{24,20},{25,21... | collective-permute-start | bytes 589832 | tf_op jit(solution)/shard_map/ppermute | solution.py:299
  5.9 11.6 %collective-permute-start = (bf16[128,768]{1,0:T(8,128)(2,1)}, bf16[128,768]{1,0:T(8,128)(2,1)S(1)}, u32[]{:S(2)}, u32[]{:S(2)}) collective-permute-start(bf16[128,768]{1,0:T(8,128)(2,1)} %refs_16_.1), channel_id=1, source_target_pairs={{2,0},{3,1},{0,2},{1,3},{6,4},{7,5},{4,6},{5,7},{10,8},{11,9},{8,1... | collective-permute-start | bytes 589832 | tf_op jit(solution)/shard_map/ppermute | solution.py:299
  12.1 9.3 %collective-permute-start.1 = (bf16[128,768]{1,0:T(8,128)(2,1)}, bf16[128,768]{1,0:T(8,128)(2,1)S(1)}, u32[]{:S(2)}, u32[]{:S(2)}) collective-permute-start(bf16[128,768]{1,0:T(8,128)(2,1)} %refs_16_.1), channel_id=1, source_target_pairs={{4,0},{5,1},{6,2},{7,3},{0,4},{1,5},{2,6},{3,7},{12,8},{13,9},{14,... | collective-permute-start | bytes 589832 | tf_op jit(solution)/shard_map/ppermute | solution.py:299
  12.8 10.2 %collective-permute-start.11 = (bf16[128,768]{1,0:T(8,128)(2,1)S(1)}, bf16[128,768]{1,0:T(8,128)(2,1)S(1)}, u32[]{:S(2)}, u32[]{:S(2)}) collective-permute-start(bf16[128,768]{1,0:T(8,128)(2,1)S(1)} %collective-permute-done.4.refs_5_), channel_id=1, source_target_pairs={{0,2},{1,3},{4,6},{5,7},{10,8},{11,9},{14,12},{15,13},{16,18},{17,... | collective-permute-start | bytes 589832 | tf_op jit(solution)/shard_map/ppermute | solution.py:299
  14.1 9.0 %collective-permute-start.10 = (bf16[128,768]{1,0:T(8,128)(2,1)S(1)}, bf16[128,768]{1,0:T(8,128)(2,1)S(1)}, u32[]{:S(2)}, u32[]{:S(2)}) collective-permute-start(bf16[128,768]{1,0:T(8,128)(2,1)S(1)} %collective-permute-done.4.refs_5_), channel_id=1, source_target_pairs={{0,1},{1,0},{2,3},{3,2},{4,5},{5,4},{6,7},{7,6},{8,9},{9,8},{10,11... | collective-permute-start | bytes 589832 | tf_op jit(solution)/shard_map/ppermute | solution.py:324
  17.0 6.5 %collective-permute-start.8 = (bf16[128,768]{1,0:T(8,128)(2,1)S(1)}, bf16[128,768]{1,0:T(8,128)(2,1)S(1)}, u32[]{:S(2)}, u32[]{:S(2)}) collective-permute-start(bf16[128,768]{1,0:T(8,128)(2,1)S(1)} %collective-permute-done.3.refs_3_), channel_id=1, source_target_pairs={{0,1},{1,0},{2,3},{3,2},{4,5},{5,4},{6,7},{7,6},{8,9},{9,8},{10,11... | collective-permute-start | bytes 589832 | tf_op jit(solution)/shard_map/ppermute | solution.py:324
  17.4 8.1 %collective-permute-start.12 = (bf16[128,768]{1,0:T(8,128)(2,1)S(1)}, bf16[128,768]{1,0:T(8,128)(2,1)S(1)}, u32[]{:S(2)}, u32[]{:S(2)}) collective-permute-start(bf16[128,768]{1,0:T(8,128)(2,1)S(1)} %collective-permute-done.2.refs_2_), channel_id=1, source_target_pairs={{6,4},{7,5},{4,6},{5,7},{10,8},{11,9},{8,10},{9,11},{22,20},{23,21... | collective-permute-start | bytes 589832 | tf_op jit(solution)/shard_map/ppermute | solution.py:299
  21.4 5.8 %collective-permute-start.9 = (bf16[128,768]{1,0:T(8,128)(2,1)S(1)}, bf16[128,768]{1,0:T(8,128)(2,1)S(1)}, u32[]{:S(2)}, u32[]{:S(2)}) collective-permute-start(bf16[128,768]{1,0:T(8,128)(2,1)S(1)} %collective-permute-done.refs_4_), channel_id=1, source_target_pairs={{0,1},{1,0},{2,3},{3,2},{4,5},{5,4},{6,7},{7,6},{8,9},{9,8},{10,11... | collective-permute-start | bytes 589832 | tf_op jit(solution)/shard_map/ppermute | solution.py:324
  23.0 4.2 %collective-permute-start.7 = (bf16[128,768]{1,0:T(8,128)(2,1)S(1)}, bf16[128,768]{1,0:T(8,128)(2,1)S(1)}, u32[]{:S(2)}, u32[]{:S(2)}) collective-permute-start(bf16[128,768]{1,0:T(8,128)(2,1)S(1)} %collective-permute-done.2.refs_2_), channel_id=1, source_target_pairs={{0,1},{1,0},{2,3},{3,2},{4,5},{5,4},{6,7},{7,6},{8,9},{9,8},{10,11... | collective-permute-start | bytes 589832 | tf_op jit(solution)/shard_map/ppermute | solution.py:324
  39.9 7.9 %collective-permute-start.15 = (bf16[128,768]{1,0:T(8,128)(2,1)S(1)}, bf16[128,768]{1,0:T(8,128)(2,1)S(1)}, u32[]{:S(2)}, u32[]{:S(2)}) collective-permute-start(bf16[128,768]{1,0:T(8,128)(2,1)S(1)} %get-tuple-element.29), channel_id=1, source_target_pairs={{8,0},{9,1},{10,2},{11,3},{12,4},{13,5},{14,6},{15,7},{0,8},{1,9},... | collective-permute-start | bytes 589832 | tf_op jit(solution)/shard_map/ppermute | solution.py:299
  39.9 15.9 %collective-permute-start.16 = (bf16[128,768]{1,0:T(8,128)(2,1)S(1)}, bf16[128,768]{1,0:T(8,128)(2,1)S(1)}, u32[]{:S(2)}, u32[]{:S(2)}) collective-permute-start(bf16[128,768]{1,0:T(8,128)(2,1)S(1)} %get-tuple-element.38), channel_id=1, source_target_pairs={{4,0},{5,1},{6,2},{7,3},{0,4},{1,5},{2,6},{3,7},{12,8},{13,9},{14,... | collective-permute-start | bytes 589832 | tf_op jit(solution)/shard_map/ppermute | solution.py:299
  43.2 13.7 %collective-permute-start.17 = (bf16[128,768]{1,0:T(8,128)(2,1)S(1)}, bf16[128,768]{1,0:T(8,128)(2,1)S(1)}, u32[]{:S(2)}, u32[]{:S(2)}) collective-permute-start(bf16[128,768]{1,0:T(8,128)(2,1)S(1)} %get-tuple-element.39), channel_id=1, source_target_pairs={{2,0},{3,1},{0,2},{1,3},{6,4},{7,5},{4,6},{5,7},{10,8},{11,9},{8,1... | collective-permute-start | bytes 589832 | tf_op jit(solution)/shard_map/ppermute | solution.py:299
  43.5 15.7 %collective-permute-start.18 = (bf16[128,768]{1,0:T(8,128)(2,1)S(1)}, bf16[128,768]{1,0:T(8,128)(2,1)S(1)}, u32[]{:S(2)}, u32[]{:S(2)}) collective-permute-start(bf16[128,768]{1,0:T(8,128)(2,1)S(1)} %get-tuple-element.40), channel_id=1, source_target_pairs={{8,2},{9,3},{12,6},{13,7},{2,8},{3,9},{6,12},{7,13},{24,18},{25,19... | collective-permute-start | bytes 589832 | tf_op jit(solution)/shard_map/ppermute | solution.py:299
  46.4 13.2 %collective-permute-start.19 = (bf16[128,768]{1,0:T(8,128)(2,1)S(1)}, bf16[128,768]{1,0:T(8,128)(2,1)S(1)}, u32[]{:S(2)}, u32[]{:S(2)}) collective-permute-start(bf16[128,768]{1,0:T(8,128)(2,1)S(1)} %get-tuple-element.41), channel_id=1, source_target_pairs={{6,0},{7,1},{4,2},{5,3},{2,4},{3,5},{0,6},{1,7},{14,8},{15,9},{12,... | collective-permute-start | bytes 589832 | tf_op jit(solution)/shard_map/ppermute | solution.py:299
  47.8 13.3 %collective-permute-start.20 = (bf16[128,768]{1,0:T(8,128)(2,1)S(1)}, bf16[128,768]{1,0:T(8,128)(2,1)S(1)}, u32[]{:S(2)}, u32[]{:S(2)}) collective-permute-start(bf16[128,768]{1,0:T(8,128)(2,1)S(1)} %get-tuple-element.42), channel_id=1, source_target_pairs={{8,4},{9,5},{10,6},{11,7},{4,8},{5,9},{6,10},{7,11},{24,20},{25,21... | collective-permute-start | bytes 589832 | tf_op jit(solution)/shard_map/ppermute | solution.py:299
  55.8 6.6 %collective-permute-start.22 = (bf16[128,768]{1,0:T(8,128)(2,1)S(1)}, bf16[128,768]{1,0:T(8,128)(2,1)S(1)}, u32[]{:S(2)}, u32[]{:S(2)}) collective-permute-start(bf16[128,768]{1,0:T(8,128)(2,1)S(1)} %collective-permute-done.15.came.refs_0_), channel_id=1, source_target_pairs={{0,1},{1,0},{2,3},{3,2},{4,5},{5,4},{6,7},{7,6},{8,9},{9,8},{10,11... | collective-permute-start | bytes 589832 | tf_op jit(solution)/shard_map/ppermute | solution.py:353
  56.9 11.4 %collective-permute-start.21 = (bf16[128,768]{1,0:T(8,128)(2,1)S(1)}, bf16[128,768]{1,0:T(8,128)(2,1)S(1)}, u32[]{:S(2)}, u32[]{:S(2)}) collective-permute-start(bf16[128,768]{1,0:T(8,128)(2,1)S(1)} %get-tuple-element.43), channel_id=1, source_target_pairs={{10,4},{11,5},{8,6},{9,7},{6,8},{7,9},{4,10},{5,11},{26,20},{27,21... | collective-permute-start | bytes 589832 | tf_op jit(solution)/shard_map/ppermute | solution.py:299
  59.1 9.8 %collective-permute-start.23 = (bf16[128,768]{1,0:T(8,128)(2,1)S(1)}, bf16[128,768]{1,0:T(8,128)(2,1)S(1)}, u32[]{:S(2)}, u32[]{:S(2)}) collective-permute-start(bf16[128,768]{1,0:T(8,128)(2,1)S(1)} %collective-permute-done.16.refs_1_), channel_id=1, source_target_pairs={{0,1},{1,0},{2,3},{3,2},{4,5},{5,4},{6,7},{7,6},{8,9},{9,8},{10,11... | collective-permute-start | bytes 589832 | tf_op jit(solution)/shard_map/ppermute | solution.py:353
  61.1 7.9 %collective-permute-start.24 = (bf16[128,768]{1,0:T(8,128)(2,1)S(1)}, bf16[128,768]{1,0:T(8,128)(2,1)S(1)}, u32[]{:S(2)}, u32[]{:S(2)}) collective-permute-start(bf16[128,768]{1,0:T(8,128)(2,1)S(1)} %collective-permute-done.17.refs_2_), channel_id=1, source_target_pairs={{0,1},{1,0},{2,3},{3,2},{4,5},{5,4},{6,7},{7,6},{8,9},{9,8},{10,11... | collective-permute-start | bytes 589832 | tf_op jit(solution)/shard_map/ppermute | solution.py:353
  62.4 6.6 %collective-permute-start.25 = (bf16[128,768]{1,0:T(8,128)(2,1)S(1)}, bf16[128,768]{1,0:T(8,128)(2,1)S(1)}, u32[]{:S(2)}, u32[]{:S(2)}) collective-permute-start(bf16[128,768]{1,0:T(8,128)(2,1)S(1)} %collective-permute-done.18.refs_3_), channel_id=1, source_target_pairs={{0,1},{1,0},{2,3},{3,2},{4,5},{5,4},{6,7},{7,6},{8,9},{9,8},{10,11... | collective-permute-start | bytes 589832 | tf_op jit(solution)/shard_map/ppermute | solution.py:353
  62.4 6.6 %collective-permute-start.26 = (bf16[128,768]{1,0:T(8,128)(2,1)S(1)}, bf16[128,768]{1,0:T(8,128)(2,1)S(1)}, u32[]{:S(2)}, u32[]{:S(2)}) collective-permute-start(bf16[128,768]{1,0:T(8,128)(2,1)S(1)} %collective-permute-done.19.refs_4_), channel_id=1, source_target_pairs={{0,1},{1,0},{2,3},{3,2},{4,5},{5,4},{6,7},{7,6},{8,9},{9,8},{10,11... | collective-permute-start | bytes 589832 | tf_op jit(solution)/shard_map/ppermute | solution.py:353
  (10 other events, 65.4 us)

commit v6 on v5

--- a/solution.py
+++ b/solution.py
@@ -99,6 +99,7 @@
     wcopies = weight_copies(w_hbm, w, wsems, w_hbm.shape[1] - 2 * width)
     for c in wcopies:
         c.start()
+    acc[...] = jnp.zeros_like(acc)
     slots = 2 * MAXNB
     span = MAXNB * BLK
 
@@ -135,7 +136,6 @@
     rows = 256
     for i in range(slots * BLK // rows):
         kv[pl.ds(i * rows, rows), :] = dot(normed[pl.ds(i * rows, rows), :], w[...], 1, 0).astype(BF16)
-    acc[...] = jnp.zeros_like(acc)
 
     group = PACK * HD
     lane = lax.broadcasted_iota(jnp.int32, (1, group), 1)

time: 72.6 us -> 72.6 us (level)
  no operation moved by 1% of the time
where the time goes in v6:
time: 72.6 us; the launch traced here: 72.1 us
  starting transfers between devices  33 us (45%)
  Pallas kernels  17.1 us (24%)
  waiting for transfers between devices  14 us (19%)
  other arithmetic  3.21 us (4%)
  matrix products  2.3 us (3%)
  local copies, waits for them, and re-layouts  1.67 us (2%)
  between operations  0.91 us (1%)
    ppermute x14, starting transfers between devices, send(): lax.ppermute(x, 'seq', [(2 * s + c, 2 * r + c) for r, s in pairs for c in...  22.9 us
    pallas_call x1, Pallas kernels, main_call(): call(functools.partial(main_kernel, rounds, places, chips), [shape((token...  12.1 us
    ppermute x14, waiting for transfers between devices, send(): lax.ppermute(x, 'seq', [(2 * s + c, 2 * r + c) for r, s in pairs for c in...  12.1 us
    ppermute x7, starting transfers between devices, per_device(): passed[r] = lax.ppermute(arrived[r], 'seq', mate)  4.33 us
    ppermute x7, starting transfers between devices, per_device(): sibs[r] = lax.ppermute(came[r], 'seq', mate)  4.03 us
    pallas_call x1, Pallas kernels, middle_call(): call(functools.partial(middle_kernel, rows_of), [jax.ShapeDtypeStruct((co...  3.19 us
    dot_general x1, matrix products, per_device(): jnp.dot(normed, w_qkv[:, :width], preferred_element_type=F32).astype(BF16)  1.77 us
    pallas_call x1, Pallas kernels, final_call(): call(functools.partial(final_kernel, order, done), jax.ShapeDtypeStruct((...  1.76 us
  transfers between devices with their start and end apart: 30, of which 9 were waited for; matrix products, arithmetic and copies ran while one was open for 10% of the time, Pallas kernels for 4%

profile of v6, /device:TPU:13, one launch (start us, length us, event | category | flops | bytes accessed | tf_op | source)
XLA Modules:
  0.0 72.1 jit_solution(16896951973739628992)
XLA Ops:
  1.4 2.3 %collective-permute-start.4 = (bf16[128,768]{1,0:T(8,128)(2,1)}, bf16[128,768]{1,0:T(8,128)(2,1)S(1)}, u32[]{:S(2)}, u32[]{:S(2)}) collective-permute-start(bf16[128,768]{1,0:T(8,128)(2,1)} %refs_16_.1), channel_id=1, source_target_pairs={{8,0},{9,1},{10,2},{11,3},{12,4},{13,5},{14,6},{15,7},{0,8},{1,9},... | collective-permute-start | bytes 589832 | tf_op jit(solution)/shard_map/ppermute | solution.py:299
  3.8 2.1 %collective-permute-start.2 = (bf16[128,768]{1,0:T(8,128)(2,1)}, bf16[128,768]{1,0:T(8,128)(2,1)S(1)}, u32[]{:S(2)}, u32[]{:S(2)}) collective-permute-start(bf16[128,768]{1,0:T(8,128)(2,1)} %refs_16_.1), channel_id=1, source_target_pairs={{8,4},{9,5},{10,6},{11,7},{4,8},{5,9},{6,10},{7,11},{24,20},{25,21... | collective-permute-start | bytes 589832 | tf_op jit(solution)/shard_map/ppermute | solution.py:299
  5.9 1.3 %collective-permute-start = (bf16[128,768]{1,0:T(8,128)(2,1)}, bf16[128,768]{1,0:T(8,128)(2,1)S(1)}, u32[]{:S(2)}, u32[]{:S(2)}) collective-permute-start(bf16[128,768]{1,0:T(8,128)(2,1)} %refs_16_.1), channel_id=1, source_target_pairs={{2,0},{3,1},{0,2},{1,3},{6,4},{7,5},{4,6},{5,7},{10,8},{11,9},{8,1... | collective-permute-start | bytes 589832 | tf_op jit(solution)/shard_map/ppermute | solution.py:299
  7.2 1.1 %convert_reduce_fusion = f32[128]{0:T(128)S(1)} fusion(bf16[128,768]{1,0:T(8,128)(2,1)} %refs_16_.1), kind=kLoop, calls=%fused_computation.5 | loop fusion | flops 196480 | bytes 197120 | tf_op jit(solution)/shard_map/reduce_sum | solution.py:51
  8.3 1.2 %fusion.7 = f32[128]{0:T(128)S(1)} fusion(bf16[128,768]{1,0:T(8,128)(2,1)} %refs_16_.1, f32[128]{0:T(128)S(1)} %broadcast_multiply_fusion), kind=kLoop, calls=%fused_computation.8 | loop fusion | flops 393088 | bytes 197632 | tf_op jit(solution)/shard_map/reduce_sum | solution.py:52
  12.8 1.3 %collective-permute-start.11 = (bf16[128,768]{1,0:T(8,128)(2,1)S(1)}, bf16[128,768]{1,0:T(8,128)(2,1)S(1)}, u32[]{:S(2)}, u32[]{:S(2)}) collective-permute-start(bf16[128,768]{1,0:T(8,128)(2,1)S(1)} %collective-permute-done.4.refs_5_), channel_id=1, source_target_pairs={{0,2},{1,3},{4,6},{5,7},{10,8},{11,9},{14,12},{15,13},{16,18},{17,... | collective-permute-start | bytes 589832 | tf_op jit(solution)/shard_map/ppermute | solution.py:299
  14.8 2.2 %collective-permute-done.2.refs_2_ = bf16[128,768]{1,0:T(8,128)(2,1)S(1)} collective-permute-done((bf16[128,768]{1,0:T(8,128)(2,1)}, bf16[128,768]{1,0:T(8,128)(2,1)S(1)}, u32[]{:S(2)}, u32[]{:S(2)}) %collective-permute-start.2) | collective-permute-done | bytes 196640 | tf_op jit(solution)/shard_map/ppermute | solution.py:299
  17.4 2.2 %collective-permute-start.12 = (bf16[128,768]{1,0:T(8,128)(2,1)S(1)}, bf16[128,768]{1,0:T(8,128)(2,1)S(1)}, u32[]{:S(2)}, u32[]{:S(2)}) collective-permute-start(bf16[128,768]{1,0:T(8,128)(2,1)S(1)} %collective-permute-done.2.refs_2_), channel_id=1, source_target_pairs={{6,4},{7,5},{4,6},{5,7},{10,8},{11,9},{8,10},{9,11},{22,20},{23,21... | collective-permute-start | bytes 589832 | tf_op jit(solution)/shard_map/ppermute | solution.py:299
  19.6 1.8 %fusion.2.refs_16_ = bf16[128,768]{1,0:T(8,128)(2,1)S(1)} fusion(bf16[768,2304]{1,0:T(8,128)(2,1)} %refs_4_.1, bf16[128,768]{1,0:T(8,128)(2,1)} %refs_16_.1, f32[768]{0:T(1024)} %param.8, f32[128]{0:T(128)S(1)} %add_rsqrt_fusion, f32[128]{0:T(128)S(1)} %broadcast_multiply_fusion), kind=kOutput, calls=%fused_computation.2 | convolution fusion | flops 151584768 | bytes 1577984 | tf_op jit(solution)/shard_map/dot_general | solution.py:318
  21.4 1.5 %collective-permute-start.9 = (bf16[128,768]{1,0:T(8,128)(2,1)S(1)}, bf16[128,768]{1,0:T(8,128)(2,1)S(1)}, u32[]{:S(2)}, u32[]{:S(2)}) collective-permute-start(bf16[128,768]{1,0:T(8,128)(2,1)S(1)} %collective-permute-done.refs_4_), channel_id=1, source_target_pairs={{0,1},{1,0},{2,3},{3,2},{4,5},{5,4},{6,7},{7,6},{8,9},{9,8},{10,11... | collective-permute-start | bytes 589832 | tf_op jit(solution)/shard_map/ppermute | solution.py:324
  23.6 2.0 %collective-permute-done.12.refs_13_ = bf16[128,768]{1,0:T(8,128)(2,1)S(1)} collective-permute-done((bf16[128,768]{1,0:T(8,128)(2,1)S(1)}, bf16[128,768]{1,0:T(8,128)(2,1)S(1)}, u32[]{:S(2)}, u32[]{:S(2)}) %collective-permute-start.12) | collective-permute-done | bytes 196640 | tf_op jit(solution)/shard_map/ppermute | solution.py:299
  25.6 1.1 %collective-permute-start.14 = (bf16[128,768]{1,0:T(8,128)(2,1)S(1)}, bf16[128,768]{1,0:T(8,128)(2,1)S(1)}, u32[]{:S(2)}, u32[]{:S(2)}) collective-permute-start(bf16[128,768]{1,0:T(8,128)(2,1)S(1)} %collective-permute-done.12.refs_13_), channel_id=1, source_target_pairs={{0,1},{1,0},{2,3},{3,2},{4,5},{5,4},{6,7},{7,6},{8,9},{9,8},{10,11... | collective-permute-start | bytes 589832 | tf_op jit(solution)/shard_map/ppermute | solution.py:324
  27.7 12.1 %shard_map.86 = (bf16[128,768]{1,0:T(8,128)(2,1)S(1)}, bf16[128,768]{1,0:T(8,128)(2,1)S(1)}, f32[128,768]{1,0:T(8,128)S(1)}, bf16[64,768]{1,0:T(8,128)(2,1)S(1)}...) custom-call(s32[1]{0:T(128)} %bitcast.position, ...), custom_call_target="tpu_custom_call" | custom-call | flops 8000000000 | bytes 5000000 | tf_op jit(solution)/shard_map/pallas_call | solution.py:195
  40.0 3.2 %collective-permute-start.16 = (bf16[128,768]{1,0:T(8,128)(2,1)S(1)}, bf16[128,768]{1,0:T(8,128)(2,1)S(1)}, u32[]{:S(2)}, u32[]{:S(2)}) collective-permute-start(bf16[128,768]{1,0:T(8,128)(2,1)S(1)} %get-tuple-element.38), channel_id=1, source_target_pairs={{4,0},{5,1},{6,2},{7,3},{0,4},{1,5},{2,6},{3,7},{12,8},{13,9},{14,... | collective-permute-start | bytes 589832 | tf_op jit(solution)/shard_map/ppermute | solution.py:299
  43.4 2.9 %collective-permute-start.18 = (bf16[128,768]{1,0:T(8,128)(2,1)S(1)}, bf16[128,768]{1,0:T(8,128)(2,1)S(1)}, u32[]{:S(2)}, u32[]{:S(2)}) collective-permute-start(bf16[128,768]{1,0:T(8,128)(2,1)S(1)} %get-tuple-element.40), channel_id=1, source_target_pairs={{8,2},{9,3},{12,6},{13,7},{2,8},{3,9},{6,12},{7,13},{24,18},{25,19... | collective-permute-start | bytes 589832 | tf_op jit(solution)/shard_map/ppermute | solution.py:299
  46.4 1.4 %collective-permute-done.15.came.refs_0_ = bf16[128,768]{1,0:T(8,128)(2,1)S(1)} collective-permute-done((bf16[128,768]{1,0:T(8,128)(2,1)S(1)}, bf16[128,768]{1,0:T(8,128)(2,1)S(1)}, u32[]{:S(2)}, u32[]{:S(2)}) %collective-permute-start.15) | collective-permute-done | bytes 196640 | tf_op jit(solution)/shard_map/ppermute | solution.py:299
  47.8 4.8 %collective-permute-start.20 = (bf16[128,768]{1,0:T(8,128)(2,1)S(1)}, bf16[128,768]{1,0:T(8,128)(2,1)S(1)}, u32[]{:S(2)}, u32[]{:S(2)}) collective-permute-start(bf16[128,768]{1,0:T(8,128)(2,1)S(1)} %get-tuple-element.42), channel_id=1, source_target_pairs={{8,4},{9,5},{10,6},{11,7},{4,8},{5,9},{6,10},{7,11},{24,20},{25,21... | collective-permute-start | bytes 589832 | tf_op jit(solution)/shard_map/ppermute | solution.py:299
  52.6 3.2 %shard_map.87 = (bf16[128,768]{1,0:T(8,128)(2,1)}, f32[2,64,768]{2,1,0:T(8,128)S(1)}) custom-call(s32[15]{0:T(128)S(1)} %convert_element_type.15.parity, bf16[128,768]{1,0:T(8,128)(2,1)S(1)} %collective-permute-done.15.came.refs_0_, bf16[128,768]{1,0:T(8,128)(2,1)S(1)} %get-tuple-element.30.refs_0_, bf16[128,768]{1,0:T(8,128)(2,1)S(1)} %get-tuple-element.31.refs_1_, ...), custom_call_target="tpu_custom_call" | custom-call | bytes 5000000 | tf_op jit(solution)/shard_map/pallas_call | solution.py:243
  55.8 1.1 %collective-permute-start.22 = (bf16[128,768]{1,0:T(8,128)(2,1)S(1)}, bf16[128,768]{1,0:T(8,128)(2,1)S(1)}, u32[]{:S(2)}, u32[]{:S(2)}) collective-permute-start(bf16[128,768]{1,0:T(8,128)(2,1)S(1)} %collective-permute-done.15.came.refs_0_), channel_id=1, source_target_pairs={{0,1},{1,0},{2,3},{3,2},{4,5},{5,4},{6,7},{7,6},{8,9},{9,8},{10,11... | collective-permute-start | bytes 589832 | tf_op jit(solution)/shard_map/ppermute | solution.py:353
  56.9 2.3 %collective-permute-start.21 = (bf16[128,768]{1,0:T(8,128)(2,1)S(1)}, bf16[128,768]{1,0:T(8,128)(2,1)S(1)}, u32[]{:S(2)}, u32[]{:S(2)}) collective-permute-start(bf16[128,768]{1,0:T(8,128)(2,1)S(1)} %get-tuple-element.43), channel_id=1, source_target_pairs={{10,4},{11,5},{8,6},{9,7},{6,8},{7,9},{4,10},{5,11},{26,20},{27,21... | collective-permute-start | bytes 589832 | tf_op jit(solution)/shard_map/ppermute | solution.py:299
  61.1 1.3 %collective-permute-start.24 = (bf16[128,768]{1,0:T(8,128)(2,1)S(1)}, bf16[128,768]{1,0:T(8,128)(2,1)S(1)}, u32[]{:S(2)}, u32[]{:S(2)}) collective-permute-start(bf16[128,768]{1,0:T(8,128)(2,1)S(1)} %collective-permute-done.17.refs_2_), channel_id=1, source_target_pairs={{0,1},{1,0},{2,3},{3,2},{4,5},{5,4},{6,7},{7,6},{8,9},{9,8},{10,11... | collective-permute-start | bytes 589832 | tf_op jit(solution)/shard_map/ppermute | solution.py:353
  63.0 5.2 %collective-permute-done.21.refs_6_ = bf16[128,768]{1,0:T(8,128)(2,1)S(1)} collective-permute-done((bf16[128,768]{1,0:T(8,128)(2,1)S(1)}, bf16[128,768]{1,0:T(8,128)(2,1)S(1)}, u32[]{:S(2)}, u32[]{:S(2)}) %collective-permute-start.21) | collective-permute-done | bytes 196640 | tf_op jit(solution)/shard_map/ppermute | solution.py:299
  69.0 1.0 %collective-permute-done.27.refs_12_ = bf16[128,768]{1,0:T(8,128)(2,1)S(1)} collective-permute-done((bf16[128,768]{1,0:T(8,128)(2,1)S(1)}, bf16[128,768]{1,0:T(8,128)(2,1)S(1)}, u32[]{:S(2)}, u32[]{:S(2)}) %collective-permute-start.27) | collective-permute-done | bytes 196640 | tf_op jit(solution)/shard_map/ppermute | solution.py:353
  70.4 1.8 %shard_map.88 = bf16[128,768]{1,0:T(8,128)(2,1)} custom-call(s32[15]{0:T(128)S(1)} %convert_element_type.15.parity, bf16[128,768]{1,0:T(8,128)(2,1)S(1)} %collective-permute-done.15.came.refs_0_, bf16[128,768]{1,0:T(8,128)(2,1)S(1)} %collective-permute-done.16.refs_1_, bf16[128,768]{1,0:T(8,128)(2,1)S(1)} %collective-permute-done.17.refs_2_, ...), custom_call_target="tpu_custom_call" | custom-call | bytes 5000000 | tf_op jit(solution)/shard_map/pallas_call | solution.py:279
  (61 shorter events, 10.9 us)
Async XLA Ops:
  0.6 11.5 %collective-permute-start.5 = (bf16[128,768]{1,0:T(8,128)(2,1)}, bf16[128,768]{1,0:T(8,128)(2,1)S(1)}, u32[]{:S(2)}, u32[]{:S(2)}) collective-permute-start(bf16[128,768]{1,0:T(8,128)(2,1)} %refs_16_.1), channel_id=1, source_target_pairs={{0,1},{1,0},{2,3},{3,2},{4,5},{5,4},{6,7},{7,6},{8,9},{9,8},{10,11... | collective-permute-start | bytes 589832 | tf_op jit(solution)/shard_map/ppermute | solution.py:332
  1.4 11.4 %collective-permute-start.4 = (bf16[128,768]{1,0:T(8,128)(2,1)}, bf16[128,768]{1,0:T(8,128)(2,1)S(1)}, u32[]{:S(2)}, u32[]{:S(2)}) collective-permute-start(bf16[128,768]{1,0:T(8,128)(2,1)} %refs_16_.1), channel_id=1, source_target_pairs={{8,0},{9,1},{10,2},{11,3},{12,4},{13,5},{14,6},{15,7},{0,8},{1,9},... | collective-permute-start | bytes 589832 | tf_op jit(solution)/shard_map/ppermute | solution.py:299
  3.7 10.4 %collective-permute-start.3 = (bf16[128,768]{1,0:T(8,128)(2,1)}, bf16[128,768]{1,0:T(8,128)(2,1)S(1)}, u32[]{:S(2)}, u32[]{:S(2)}) collective-permute-start(bf16[128,768]{1,0:T(8,128)(2,1)} %refs_16_.1), channel_id=1, source_target_pairs={{6,0},{7,1},{4,2},{5,3},{2,4},{3,5},{0,6},{1,7},{14,8},{15,9},{12,... | collective-permute-start | bytes 589832 | tf_op jit(solution)/shard_map/ppermute | solution.py:299
  3.8 13.2 %collective-permute-start.2 = (bf16[128,768]{1,0:T(8,128)(2,1)}, bf16[128,768]{1,0:T(8,128)(2,1)S(1)}, u32[]{:S(2)}, u32[]{:S(2)}) collective-permute-start(bf16[128,768]{1,0:T(8,128)(2,1)} %refs_16_.1), channel_id=1, source_target_pairs={{8,4},{9,5},{10,6},{11,7},{4,8},{5,9},{6,10},{7,11},{24,20},{25,21... | collective-permute-start | bytes 589832 | tf_op jit(solution)/shard_map/ppermute | solution.py:299
  5.9 11.6 %collective-permute-start = (bf16[128,768]{1,0:T(8,128)(2,1)}, bf16[128,768]{1,0:T(8,128)(2,1)S(1)}, u32[]{:S(2)}, u32[]{:S(2)}) collective-permute-start(bf16[128,768]{1,0:T(8,128)(2,1)} %refs_16_.1), channel_id=1, source_target_pairs={{2,0},{3,1},{0,2},{1,3},{6,4},{7,5},{4,6},{5,7},{10,8},{11,9},{8,1... | collective-permute-start | bytes 589832 | tf_op jit(solution)/shard_map/ppermute | solution.py:299
  12.1 9.3 %collective-permute-start.1 = (bf16[128,768]{1,0:T(8,128)(2,1)}, bf16[128,768]{1,0:T(8,128)(2,1)S(1)}, u32[]{:S(2)}, u32[]{:S(2)}) collective-permute-start(bf16[128,768]{1,0:T(8,128)(2,1)} %refs_16_.1), channel_id=1, source_target_pairs={{4,0},{5,1},{6,2},{7,3},{0,4},{1,5},{2,6},{3,7},{12,8},{13,9},{14,... | collective-permute-start | bytes 589832 | tf_op jit(solution)/shard_map/ppermute | solution.py:299
  12.8 10.2 %collective-permute-start.11 = (bf16[128,768]{1,0:T(8,128)(2,1)S(1)}, bf16[128,768]{1,0:T(8,128)(2,1)S(1)}, u32[]{:S(2)}, u32[]{:S(2)}) collective-permute-start(bf16[128,768]{1,0:T(8,128)(2,1)S(1)} %collective-permute-done.4.refs_5_), channel_id=1, source_target_pairs={{0,2},{1,3},{4,6},{5,7},{10,8},{11,9},{14,12},{15,13},{16,18},{17,... | collective-permute-start | bytes 589832 | tf_op jit(solution)/shard_map/ppermute | solution.py:299
  14.1 9.0 %collective-permute-start.10 = (bf16[128,768]{1,0:T(8,128)(2,1)S(1)}, bf16[128,768]{1,0:T(8,128)(2,1)S(1)}, u32[]{:S(2)}, u32[]{:S(2)}) collective-permute-start(bf16[128,768]{1,0:T(8,128)(2,1)S(1)} %collective-permute-done.4.refs_5_), channel_id=1, source_target_pairs={{0,1},{1,0},{2,3},{3,2},{4,5},{5,4},{6,7},{7,6},{8,9},{9,8},{10,11... | collective-permute-start | bytes 589832 | tf_op jit(solution)/shard_map/ppermute | solution.py:324
  17.0 6.5 %collective-permute-start.8 = (bf16[128,768]{1,0:T(8,128)(2,1)S(1)}, bf16[128,768]{1,0:T(8,128)(2,1)S(1)}, u32[]{:S(2)}, u32[]{:S(2)}) collective-permute-start(bf16[128,768]{1,0:T(8,128)(2,1)S(1)} %collective-permute-done.3.refs_3_), channel_id=1, source_target_pairs={{0,1},{1,0},{2,3},{3,2},{4,5},{5,4},{6,7},{7,6},{8,9},{9,8},{10,11... | collective-permute-start | bytes 589832 | tf_op jit(solution)/shard_map/ppermute | solution.py:324
  17.4 8.1 %collective-permute-start.12 = (bf16[128,768]{1,0:T(8,128)(2,1)S(1)}, bf16[128,768]{1,0:T(8,128)(2,1)S(1)}, u32[]{:S(2)}, u32[]{:S(2)}) collective-permute-start(bf16[128,768]{1,0:T(8,128)(2,1)S(1)} %collective-permute-done.2.refs_2_), channel_id=1, source_target_pairs={{6,4},{7,5},{4,6},{5,7},{10,8},{11,9},{8,10},{9,11},{22,20},{23,21... | collective-permute-start | bytes 589832 | tf_op jit(solution)/shard_map/ppermute | solution.py:299
  21.4 5.8 %collective-permute-start.9 = (bf16[128,768]{1,0:T(8,128)(2,1)S(1)}, bf16[128,768]{1,0:T(8,128)(2,1)S(1)}, u32[]{:S(2)}, u32[]{:S(2)}) collective-permute-start(bf16[128,768]{1,0:T(8,128)(2,1)S(1)} %collective-permute-done.refs_4_), channel_id=1, source_target_pairs={{0,1},{1,0},{2,3},{3,2},{4,5},{5,4},{6,7},{7,6},{8,9},{9,8},{10,11... | collective-permute-start | bytes 589832 | tf_op jit(solution)/shard_map/ppermute | solution.py:324
  23.0 4.2 %collective-permute-start.7 = (bf16[128,768]{1,0:T(8,128)(2,1)S(1)}, bf16[128,768]{1,0:T(8,128)(2,1)S(1)}, u32[]{:S(2)}, u32[]{:S(2)}) collective-permute-start(bf16[128,768]{1,0:T(8,128)(2,1)S(1)} %collective-permute-done.2.refs_2_), channel_id=1, source_target_pairs={{0,1},{1,0},{2,3},{3,2},{4,5},{5,4},{6,7},{7,6},{8,9},{9,8},{10,11... | collective-permute-start | bytes 589832 | tf_op jit(solution)/shard_map/ppermute | solution.py:324
  39.9 8.0 %collective-permute-start.15 = (bf16[128,768]{1,0:T(8,128)(2,1)S(1)}, bf16[128,768]{1,0:T(8,128)(2,1)S(1)}, u32[]{:S(2)}, u32[]{:S(2)}) collective-permute-start(bf16[128,768]{1,0:T(8,128)(2,1)S(1)} %get-tuple-element.29), channel_id=1, source_target_pairs={{8,0},{9,1},{10,2},{11,3},{12,4},{13,5},{14,6},{15,7},{0,8},{1,9},... | collective-permute-start | bytes 589832 | tf_op jit(solution)/shard_map/ppermute | solution.py:299
  40.0 15.8 %collective-permute-start.16 = (bf16[128,768]{1,0:T(8,128)(2,1)S(1)}, bf16[128,768]{1,0:T(8,128)(2,1)S(1)}, u32[]{:S(2)}, u32[]{:S(2)}) collective-permute-start(bf16[128,768]{1,0:T(8,128)(2,1)S(1)} %get-tuple-element.38), channel_id=1, source_target_pairs={{4,0},{5,1},{6,2},{7,3},{0,4},{1,5},{2,6},{3,7},{12,8},{13,9},{14,... | collective-permute-start | bytes 589832 | tf_op jit(solution)/shard_map/ppermute | solution.py:299
  43.2 13.7 %collective-permute-start.17 = (bf16[128,768]{1,0:T(8,128)(2,1)S(1)}, bf16[128,768]{1,0:T(8,128)(2,1)S(1)}, u32[]{:S(2)}, u32[]{:S(2)}) collective-permute-start(bf16[128,768]{1,0:T(8,128)(2,1)S(1)} %get-tuple-element.39), channel_id=1, source_target_pairs={{2,0},{3,1},{0,2},{1,3},{6,4},{7,5},{4,6},{5,7},{10,8},{11,9},{8,1... | collective-permute-start | bytes 589832 | tf_op jit(solution)/shard_map/ppermute | solution.py:299
  43.4 15.7 %collective-permute-start.18 = (bf16[128,768]{1,0:T(8,128)(2,1)S(1)}, bf16[128,768]{1,0:T(8,128)(2,1)S(1)}, u32[]{:S(2)}, u32[]{:S(2)}) collective-permute-start(bf16[128,768]{1,0:T(8,128)(2,1)S(1)} %get-tuple-element.40), channel_id=1, source_target_pairs={{8,2},{9,3},{12,6},{13,7},{2,8},{3,9},{6,12},{7,13},{24,18},{25,19... | collective-permute-start | bytes 589832 | tf_op jit(solution)/shard_map/ppermute | solution.py:299
  46.4 13.2 %collective-permute-start.19 = (bf16[128,768]{1,0:T(8,128)(2,1)S(1)}, bf16[128,768]{1,0:T(8,128)(2,1)S(1)}, u32[]{:S(2)}, u32[]{:S(2)}) collective-permute-start(bf16[128,768]{1,0:T(8,128)(2,1)S(1)} %get-tuple-element.41), channel_id=1, source_target_pairs={{6,0},{7,1},{4,2},{5,3},{2,4},{3,5},{0,6},{1,7},{14,8},{15,9},{12,... | collective-permute-start | bytes 589832 | tf_op jit(solution)/shard_map/ppermute | solution.py:299
  47.8 13.3 %collective-permute-start.20 = (bf16[128,768]{1,0:T(8,128)(2,1)S(1)}, bf16[128,768]{1,0:T(8,128)(2,1)S(1)}, u32[]{:S(2)}, u32[]{:S(2)}) collective-permute-start(bf16[128,768]{1,0:T(8,128)(2,1)S(1)} %get-tuple-element.42), channel_id=1, source_target_pairs={{8,4},{9,5},{10,6},{11,7},{4,8},{5,9},{6,10},{7,11},{24,20},{25,21... | collective-permute-start | bytes 589832 | tf_op jit(solution)/shard_map/ppermute | solution.py:299
  55.8 6.6 %collective-permute-start.22 = (bf16[128,768]{1,0:T(8,128)(2,1)S(1)}, bf16[128,768]{1,0:T(8,128)(2,1)S(1)}, u32[]{:S(2)}, u32[]{:S(2)}) collective-permute-start(bf16[128,768]{1,0:T(8,128)(2,1)S(1)} %collective-permute-done.15.came.refs_0_), channel_id=1, source_target_pairs={{0,1},{1,0},{2,3},{3,2},{4,5},{5,4},{6,7},{7,6},{8,9},{9,8},{10,11... | collective-permute-start | bytes 589832 | tf_op jit(solution)/shard_map/ppermute | solution.py:353
  56.9 11.3 %collective-permute-start.21 = (bf16[128,768]{1,0:T(8,128)(2,1)S(1)}, bf16[128,768]{1,0:T(8,128)(2,1)S(1)}, u32[]{:S(2)}, u32[]{:S(2)}) collective-permute-start(bf16[128,768]{1,0:T(8,128)(2,1)S(1)} %get-tuple-element.43), channel_id=1, source_target_pairs={{10,4},{11,5},{8,6},{9,7},{6,8},{7,9},{4,10},{5,11},{26,20},{27,21... | collective-permute-start | bytes 589832 | tf_op jit(solution)/shard_map/ppermute | solution.py:299
  59.1 9.8 %collective-permute-start.23 = (bf16[128,768]{1,0:T(8,128)(2,1)S(1)}, bf16[128,768]{1,0:T(8,128)(2,1)S(1)}, u32[]{:S(2)}, u32[]{:S(2)}) collective-permute-start(bf16[128,768]{1,0:T(8,128)(2,1)S(1)} %collective-permute-done.16.refs_1_), channel_id=1, source_target_pairs={{0,1},{1,0},{2,3},{3,2},{4,5},{5,4},{6,7},{7,6},{8,9},{9,8},{10,11... | collective-permute-start | bytes 589832 | tf_op jit(solution)/shard_map/ppermute | solution.py:353
  61.1 7.9 %collective-permute-start.24 = (bf16[128,768]{1,0:T(8,128)(2,1)S(1)}, bf16[128,768]{1,0:T(8,128)(2,1)S(1)}, u32[]{:S(2)}, u32[]{:S(2)}) collective-permute-start(bf16[128,768]{1,0:T(8,128)(2,1)S(1)} %collective-permute-done.17.refs_2_), channel_id=1, source_target_pairs={{0,1},{1,0},{2,3},{3,2},{4,5},{5,4},{6,7},{7,6},{8,9},{9,8},{10,11... | collective-permute-start | bytes 589832 | tf_op jit(solution)/shard_map/ppermute | solution.py:353
  62.4 6.5 %collective-permute-start.25 = (bf16[128,768]{1,0:T(8,128)(2,1)S(1)}, bf16[128,768]{1,0:T(8,128)(2,1)S(1)}, u32[]{:S(2)}, u32[]{:S(2)}) collective-permute-start(bf16[128,768]{1,0:T(8,128)(2,1)S(1)} %collective-permute-done.18.refs_3_), channel_id=1, source_target_pairs={{0,1},{1,0},{2,3},{3,2},{4,5},{5,4},{6,7},{7,6},{8,9},{9,8},{10,11... | collective-permute-start | bytes 589832 | tf_op jit(solution)/shard_map/ppermute | solution.py:353
  62.4 6.5 %collective-permute-start.26 = (bf16[128,768]{1,0:T(8,128)(2,1)S(1)}, bf16[128,768]{1,0:T(8,128)(2,1)S(1)}, u32[]{:S(2)}, u32[]{:S(2)}) collective-permute-start(bf16[128,768]{1,0:T(8,128)(2,1)S(1)} %collective-permute-done.19.refs_4_), channel_id=1, source_target_pairs={{0,1},{1,0},{2,3},{3,2},{4,5},{5,4},{6,7},{7,6},{8,9},{9,8},{10,11... | collective-permute-start | bytes 589832 | tf_op jit(solution)/shard_map/ppermute | solution.py:353
  (10 other events, 65.4 us)
